TPU v7x, 32 devices: a whole 2x2x4 slice. The times are simulated.
32 devices in a mesh: outer: 2 (over y), inner: 16 (over z, x, core).
Axes of the slice: x: 2, y: 2, z: 4, core: 2. Of those that a mesh axis runs over, the one named last changes fastest.
Arguments:
- hidden: bfloat16 [32, 1024, 768], P(('outer', 'inner')), may hold values from -6 to 6
- cotangent: bfloat16 [32, 1024, 768], P(('outer', 'inner')), may hold values from -6 to 6
- capacity_class: int32 [32], P(('outer', 'inner')), may hold values from 0 to 2, as said below
- token_index: int32 [32, 512], P(('outer', 'inner')), may hold values from 0 to 1023, as said below
- gain_attn_a: bfloat16 [768], P(('outer', 'inner')), may hold values from 0.5 to 1.5
- qkv_weight_a: bfloat16 [768, 2304], P('inner', 'outer'), may hold values from -0.21875 to 0.21875
- out_weight_a: bfloat16 [768, 768], P('inner', 'outer'), may hold values from -0.625 to 0.625
- gain_mlp_a: bfloat16 [768], P(('outer', 'inner')), may hold values from 0.5 to 1.5
- up_weight_a: bfloat16 [768, 3072], P('inner', 'outer'), may hold values from -0.21875 to 0.21875
- down_weight_a: bfloat16 [3072, 768], P('inner', 'outer'), may hold values from -0.109375 to 0.109375
- router_weight: bfloat16 [768], P(('outer', 'inner')), may hold values from -0.21875 to 0.21875
- gain_attn_b: bfloat16 [768], P(('outer', 'inner')), may hold values from 0.5 to 1.5
- qkv_weight_b: bfloat16 [768, 2304], P('inner', 'outer'), may hold values from -0.21875 to 0.21875
- out_weight_b: bfloat16 [768, 768], P('inner', 'outer'), may hold values from -0.625 to 0.625
- gain_mlp_b: bfloat16 [768], P(('outer', 'inner')), may hold values from 0.5 to 1.5
- up_weight_b: bfloat16 [768, 3072], P('inner', 'outer'), may hold values from -0.21875 to 0.21875
- down_weight_b: bfloat16 [3072, 768], P('inner', 'outer'), may hold values from -0.109375 to 0.109375
Outputs:
- output: bfloat16 [32, 1024, 768], P(('outer', 'inner'))
- input_grad: float32 [32, 1024, 768], P(('outer', 'inner'))
- grad_gain_attn_a: float32 [768], P(('outer', 'inner'))
- grad_qkv_a: float32 [768, 2304], P('inner', 'outer')
- grad_out_a: float32 [768, 768], P('inner', 'outer')
- grad_gain_mlp_a: float32 [768], P(('outer', 'inner'))
- grad_up_a: float32 [768, 3072], P('inner', 'outer')
- grad_down_a: float32 [3072, 768], P('inner', 'outer')
- grad_router: float32 [768], P(('outer', 'inner'))
- grad_gain_attn_b: float32 [768], P(('outer', 'inner'))
- grad_qkv_b: float32 [768, 2304], P('inner', 'outer')
- grad_out_b: float32 [768, 768], P('inner', 'outer')
- grad_gain_mlp_b: float32 [768], P(('outer', 'inner'))
- grad_up_b: float32 [768, 3072], P('inner', 'outer')
- grad_down_b: float32 [3072, 768], P('inner', 'outer')
Inputs may be any that keep to these rules, and one draw needn't show every extreme that they name: `capacity_class`: a sequence of class c has a buffer of 1024 / 8 * 2^c tokens; classes 0 and 2 both occur in every draw. `token_index`: row s holds, in its first 1024 / 8 * 2^capacity_class[s] entries, distinct positions of the sequence in increasing order; the remaining entries are 0 and are not used.
All inputs are finite; a program needn't handle non-finite values.
Results may differ from a plain program's by a relative error of at most 0.024.
Values may be sent and summed in bfloat16 or wider, within the bound.
A program may use at most 256 MiB of HBM per device.

v0:
```python
import jax
import jax.numpy as jnp
from jax import lax
from jax.sharding import PartitionSpec as P

HEADS = 12
HEAD = 64


def lowered(values):
    return values.astype(jnp.bfloat16)


def product(left, right):
    return jnp.dot(left, right, preferred_element_type=jnp.float32)


def rms_norm(values, norm_gain):
    return values * lax.rsqrt(jnp.mean(values * values, axis=-1, keepdims=True) + 1e-06) * norm_gain


def gelu_tanh(values):
    return jax.nn.gelu(values, approximate=True)


def causal_probs(query_head, key_head):
    scores = product(query_head, key_head.T) * 0.125
    length = scores.shape[0]
    causal = lax.broadcasted_iota(jnp.int32, (length, length), 0) >= lax.broadcasted_iota(
        jnp.int32, (length, length), 1
    )
    scores = jnp.where(causal, scores, -1000000000.0)
    return jax.nn.softmax(scores, axis=-1)


def attend_forward(pieces):
    query_head, key_head, value_head = pieces
    probs = causal_probs(query_head, key_head)
    return lowered(product(lowered(probs), value_head))


def attend_backward(pieces):
    query_head, key_head, value_head, grad_out = pieces
    probs = causal_probs(query_head, key_head)
    probs_low = lowered(probs)
    grad_probs = product(grad_out, value_head.T)
    grad_scores = probs * (grad_probs - jnp.sum(grad_probs * probs, axis=-1, keepdims=True))
    grad_raw = lowered(0.125 * grad_scores)
    grad_query = product(grad_raw, key_head)
    grad_key = product(grad_raw.T, query_head)
    grad_value = product(probs_low.T, grad_out)
    return (grad_query, grad_key, grad_value)


def split_heads(values):
    length = values.shape[0]
    return values.reshape(length, 3, HEADS, HEAD).transpose(1, 2, 0, 3)


def block_pass(hidden, params):
    gain_attn, qkv_weight, out_weight, gain_mlp, up_weight, down_weight = params
    length = hidden.shape[0]
    normed = lowered(rms_norm(hidden, gain_attn))
    projected = lowered(product(normed, qkv_weight))
    heads_split = split_heads(projected)
    attended = lax.map(attend_forward, (heads_split[0], heads_split[1], heads_split[2]))
    merged = attended.transpose(1, 0, 2).reshape(length, HEADS * HEAD)
    branch = product(merged, out_weight)
    middle = hidden + branch
    normed_mlp = lowered(rms_norm(middle, gain_mlp))
    inner_pre = product(normed_mlp, up_weight)
    active = lowered(gelu_tanh(inner_pre))
    result = branch + product(active, down_weight)
    return (result, (normed, projected, merged, middle, normed_mlp, inner_pre, active))


def block_backward(hidden, params, grad_result):
    gain_attn, qkv_weight, out_weight, gain_mlp, up_weight, down_weight = params
    length = hidden.shape[0]
    result, saved = block_pass(hidden, params)
    normed, projected, merged, middle, normed_mlp, inner_pre, active = saved
    grad_down_out = lowered(grad_result)
    grad_active = product(grad_down_out, down_weight.T)
    grad_down = product(active.T, grad_down_out)
    grad_inner = jax.vjp(gelu_tanh, inner_pre)[1](grad_active)[0]
    grad_inner_low = lowered(grad_inner)
    grad_normed_mlp = product(grad_inner_low, up_weight.T)
    grad_up = product(normed_mlp.T, grad_inner_low)
    grad_middle, grad_gain_mlp = jax.vjp(rms_norm, middle, gain_mlp)[1](grad_normed_mlp)
    grad_branch = lowered(grad_result + grad_middle)
    grad_merged = product(grad_branch, out_weight.T)
    grad_out = product(merged.T, grad_branch)
    grad_heads = lowered(grad_merged).reshape(length, HEADS, HEAD).transpose(1, 0, 2)
    heads_split = split_heads(projected)
    grad_query, grad_key, grad_value = lax.map(
        attend_backward, (heads_split[0], heads_split[1], heads_split[2], grad_heads)
    )
    grad_projected = (
        jnp.stack([grad_query, grad_key, grad_value])
        .transpose(2, 0, 1, 3)
        .reshape(length, 3 * HEADS * HEAD)
    )
    grad_projected = lowered(grad_projected)
    grad_normed = product(grad_projected, qkv_weight.T)
    grad_qkv = product(normed.T, grad_projected)
    grad_hidden, grad_gain_attn = jax.vjp(rms_norm, hidden, gain_attn)[1](grad_normed)
    grad_hidden = grad_hidden + grad_middle
    return (
        result,
        grad_hidden,
        (grad_gain_attn, grad_qkv, grad_out, grad_gain_mlp, grad_up, grad_down),
    )


def routed_forward(sequence, router, params, seq_class, seq_index):
    length = sequence.shape[0]

    def builder(buffer_size):

        def runner(sequence):
            picked_index = seq_index[:buffer_size]
            picked = sequence[picked_index]
            logits = jnp.sum(picked * router, axis=-1)
            change = block_pass(picked, params)[0]
            return sequence.at[picked_index].add(jax.nn.sigmoid(logits)[:, None] * change)

        return runner

    return lax.switch(
        seq_class, [builder(length // 8), builder(length // 4), builder(length // 2)], sequence
    )


def routed_backward(sequence, router, params, seq_class, seq_index, grad_middle):
    length = sequence.shape[0]

    def builder(buffer_size):

        def runner(sequence, grad_middle):
            picked_index = seq_index[:buffer_size]
            picked = sequence[picked_index]
            logits = jnp.sum(picked * router, axis=-1)
            gate = jax.nn.sigmoid(logits)
            grad_rows = grad_middle[picked_index]
            change, grad_picked, grads = block_backward(picked, params, gate[:, None] * grad_rows)
            grad_gate = jnp.sum(grad_rows * change, axis=-1)
            grad_logits = grad_gate * gate * (1.0 - gate)
            grad_picked = grad_picked + grad_logits[:, None] * router
            grad_router = jnp.sum(grad_logits[:, None] * picked, axis=0)
            grad_sequence = grad_middle.at[picked_index].add(grad_picked)
            return (grad_sequence, grads, grad_router)

        return runner

    return lax.switch(
        seq_class,
        [builder(length // 8), builder(length // 4), builder(length // 2)],
        sequence,
        grad_middle,
    )


def prepare(gathered):
    return (
        gathered[0].astype(jnp.float32),
        gathered[1],
        gathered[2],
        gathered[3].astype(jnp.float32),
        gathered[4],
        gathered[5],
    )


def zero_grads(params):
    return tuple((jnp.zeros(weight_arr.shape, jnp.float32) for weight_arr in params))


def per_device(
    hidden,
    cotangent,
    capacity_class,
    token_index,
    gain_attn_a,
    qkv_weight_a,
    out_weight_a,
    gain_mlp_a,
    up_weight_a,
    down_weight_a,
    router_weight,
    gain_attn_b,
    qkv_weight_b,
    out_weight_b,
    gain_mlp_b,
    up_weight_b,
    down_weight_b,
):
    rows_a = (
        lax.all_gather(gain_attn_a, "inner", axis=0, tiled=True),
        lax.all_gather(qkv_weight_a, "inner", axis=0, tiled=True),
        lax.all_gather(out_weight_a, "inner", axis=0, tiled=True),
        lax.all_gather(gain_mlp_a, "inner", axis=0, tiled=True),
        lax.all_gather(up_weight_a, "inner", axis=0, tiled=True),
        lax.all_gather(down_weight_a, "inner", axis=0, tiled=True),
        lax.all_gather(router_weight, "inner", axis=0, tiled=True),
    )
    gathered_a = (
        lax.all_gather(rows_a[0], "outer", axis=0, tiled=True),
        lax.all_gather(rows_a[1], "outer", axis=1, tiled=True),
        lax.all_gather(rows_a[2], "outer", axis=1, tiled=True),
        lax.all_gather(rows_a[3], "outer", axis=0, tiled=True),
        lax.all_gather(rows_a[4], "outer", axis=1, tiled=True),
        lax.all_gather(rows_a[5], "outer", axis=1, tiled=True),
        lax.all_gather(rows_a[6], "outer", axis=0, tiled=True),
    )
    params_a = prepare(gathered_a)
    router = gathered_a[6].astype(jnp.float32)
    layer_input = hidden.astype(jnp.float32)

    def routed_step(sliced):
        sequence, seq_class, seq_index = sliced
        return routed_forward(sequence, router, params_a, seq_class, seq_index)

    middle = lax.map(routed_step, (layer_input, capacity_class, token_index))
    rows_b = (
        lax.all_gather(gain_attn_b, "inner", axis=0, tiled=True),
        lax.all_gather(qkv_weight_b, "inner", axis=0, tiled=True),
        lax.all_gather(out_weight_b, "inner", axis=0, tiled=True),
        lax.all_gather(gain_mlp_b, "inner", axis=0, tiled=True),
        lax.all_gather(up_weight_b, "inner", axis=0, tiled=True),
        lax.all_gather(down_weight_b, "inner", axis=0, tiled=True),
    )
    gathered_b = (
        lax.all_gather(rows_b[0], "outer", axis=0, tiled=True),
        lax.all_gather(rows_b[1], "outer", axis=1, tiled=True),
        lax.all_gather(rows_b[2], "outer", axis=1, tiled=True),
        lax.all_gather(rows_b[3], "outer", axis=0, tiled=True),
        lax.all_gather(rows_b[4], "outer", axis=1, tiled=True),
        lax.all_gather(rows_b[5], "outer", axis=1, tiled=True),
    )
    params_b = prepare(gathered_b)

    def dense_step(sequence):
        return (sequence + block_pass(sequence, params_b)[0]).astype(jnp.bfloat16)

    layer_output = lax.map(dense_step, middle)
    again_rows_b = (
        lax.all_gather(gain_attn_b, "inner", axis=0, tiled=True),
        lax.all_gather(qkv_weight_b, "inner", axis=0, tiled=True),
        lax.all_gather(out_weight_b, "inner", axis=0, tiled=True),
        lax.all_gather(gain_mlp_b, "inner", axis=0, tiled=True),
        lax.all_gather(up_weight_b, "inner", axis=0, tiled=True),
        lax.all_gather(down_weight_b, "inner", axis=0, tiled=True),
    )
    params_b = prepare(
        (
            lax.all_gather(again_rows_b[0], "outer", axis=0, tiled=True),
            lax.all_gather(again_rows_b[1], "outer", axis=1, tiled=True),
            lax.all_gather(again_rows_b[2], "outer", axis=1, tiled=True),
            lax.all_gather(again_rows_b[3], "outer", axis=0, tiled=True),
            lax.all_gather(again_rows_b[4], "outer", axis=1, tiled=True),
            lax.all_gather(again_rows_b[5], "outer", axis=1, tiled=True),
        )
    )

    def dense_back(totals, sliced):
        sequence, grad_rows = sliced
        upstream = grad_rows.astype(jnp.float32)
        unused, grad_hidden, grads = block_backward(sequence, params_b, upstream)
        totals = tuple((total + grad for total, grad in zip(totals, grads)))
        return (totals, upstream + grad_hidden)

    grads_b, middle_grad = lax.scan(dense_back, zero_grads(params_b), (middle, cotangent))
    columns_b = (
        lax.psum_scatter(
            grads_b[0].astype(jnp.bfloat16), "outer", scatter_dimension=0, tiled=True
        ).astype(jnp.float32),
        lax.psum_scatter(
            grads_b[1].astype(jnp.bfloat16), "outer", scatter_dimension=1, tiled=True
        ).astype(jnp.float32),
        lax.psum_scatter(
            grads_b[2].astype(jnp.bfloat16), "outer", scatter_dimension=1, tiled=True
        ).astype(jnp.float32),
        lax.psum_scatter(
            grads_b[3].astype(jnp.bfloat16), "outer", scatter_dimension=0, tiled=True
        ).astype(jnp.float32),
        lax.psum_scatter(
            grads_b[4].astype(jnp.bfloat16), "outer", scatter_dimension=1, tiled=True
        ).astype(jnp.float32),
        lax.psum_scatter(
            grads_b[5].astype(jnp.bfloat16), "outer", scatter_dimension=1, tiled=True
        ).astype(jnp.float32),
    )
    shard_b = (
        lax.psum_scatter(
            columns_b[0].astype(jnp.bfloat16), "inner", scatter_dimension=0, tiled=True
        ).astype(jnp.float32),
        lax.psum_scatter(
            columns_b[1].astype(jnp.bfloat16), "inner", scatter_dimension=0, tiled=True
        ).astype(jnp.float32),
        lax.psum_scatter(
            columns_b[2].astype(jnp.bfloat16), "inner", scatter_dimension=0, tiled=True
        ).astype(jnp.float32),
        lax.psum_scatter(
            columns_b[3].astype(jnp.bfloat16), "inner", scatter_dimension=0, tiled=True
        ).astype(jnp.float32),
        lax.psum_scatter(
            columns_b[4].astype(jnp.bfloat16), "inner", scatter_dimension=0, tiled=True
        ).astype(jnp.float32),
        lax.psum_scatter(
            columns_b[5].astype(jnp.bfloat16), "inner", scatter_dimension=0, tiled=True
        ).astype(jnp.float32),
    )
    again_rows_a = (
        lax.all_gather(gain_attn_a, "inner", axis=0, tiled=True),
        lax.all_gather(qkv_weight_a, "inner", axis=0, tiled=True),
        lax.all_gather(out_weight_a, "inner", axis=0, tiled=True),
        lax.all_gather(gain_mlp_a, "inner", axis=0, tiled=True),
        lax.all_gather(up_weight_a, "inner", axis=0, tiled=True),
        lax.all_gather(down_weight_a, "inner", axis=0, tiled=True),
        lax.all_gather(router_weight, "inner", axis=0, tiled=True),
    )
    again_a = (
        lax.all_gather(again_rows_a[0], "outer", axis=0, tiled=True),
        lax.all_gather(again_rows_a[1], "outer", axis=1, tiled=True),
        lax.all_gather(again_rows_a[2], "outer", axis=1, tiled=True),
        lax.all_gather(again_rows_a[3], "outer", axis=0, tiled=True),
        lax.all_gather(again_rows_a[4], "outer", axis=1, tiled=True),
        lax.all_gather(again_rows_a[5], "outer", axis=1, tiled=True),
        lax.all_gather(again_rows_a[6], "outer", axis=0, tiled=True),
    )
    params_a = prepare(again_a)
    router = again_a[6].astype(jnp.float32)

    def routed_back(totals, sliced):
        sequence, grad_rows, seq_class, seq_index = sliced
        grad_sequence, grads, grad_router = routed_backward(
            sequence, router, params_a, seq_class, seq_index, grad_rows
        )
        block_totals, router_total = totals
        block_totals = tuple((total + grad for total, grad in zip(block_totals, grads)))
        return ((block_totals, router_total + grad_router), grad_sequence)

    initial = (zero_grads(params_a), jnp.zeros(router.shape, jnp.float32))
    totals_a, input_grad = lax.scan(
        routed_back, initial, (layer_input, middle_grad, capacity_class, token_index)
    )
    grads_a = totals_a[0] + (totals_a[1],)
    columns_a = (
        lax.psum_scatter(
            grads_a[0].astype(jnp.bfloat16), "outer", scatter_dimension=0, tiled=True
        ).astype(jnp.float32),
        lax.psum_scatter(
            grads_a[1].astype(jnp.bfloat16), "outer", scatter_dimension=1, tiled=True
        ).astype(jnp.float32),
        lax.psum_scatter(
            grads_a[2].astype(jnp.bfloat16), "outer", scatter_dimension=1, tiled=True
        ).astype(jnp.float32),
        lax.psum_scatter(
            grads_a[3].astype(jnp.bfloat16), "outer", scatter_dimension=0, tiled=True
        ).astype(jnp.float32),
        lax.psum_scatter(
            grads_a[4].astype(jnp.bfloat16), "outer", scatter_dimension=1, tiled=True
        ).astype(jnp.float32),
        lax.psum_scatter(
            grads_a[5].astype(jnp.bfloat16), "outer", scatter_dimension=1, tiled=True
        ).astype(jnp.float32),
        lax.psum_scatter(
            grads_a[6].astype(jnp.bfloat16), "outer", scatter_dimension=0, tiled=True
        ).astype(jnp.float32),
    )
    shard_a = (
        lax.psum_scatter(
            columns_a[0].astype(jnp.bfloat16), "inner", scatter_dimension=0, tiled=True
        ).astype(jnp.float32),
        lax.psum_scatter(
            columns_a[1].astype(jnp.bfloat16), "inner", scatter_dimension=0, tiled=True
        ).astype(jnp.float32),
        lax.psum_scatter(
            columns_a[2].astype(jnp.bfloat16), "inner", scatter_dimension=0, tiled=True
        ).astype(jnp.float32),
        lax.psum_scatter(
            columns_a[3].astype(jnp.bfloat16), "inner", scatter_dimension=0, tiled=True
        ).astype(jnp.float32),
        lax.psum_scatter(
            columns_a[4].astype(jnp.bfloat16), "inner", scatter_dimension=0, tiled=True
        ).astype(jnp.float32),
        lax.psum_scatter(
            columns_a[5].astype(jnp.bfloat16), "inner", scatter_dimension=0, tiled=True
        ).astype(jnp.float32),
        lax.psum_scatter(
            columns_a[6].astype(jnp.bfloat16), "inner", scatter_dimension=0, tiled=True
        ).astype(jnp.float32),
    )
    return (
        layer_output,
        input_grad,
        shard_a[0],
        shard_a[1],
        shard_a[2],
        shard_a[3],
        shard_a[4],
        shard_a[5],
        shard_a[6],
        shard_b[0],
        shard_b[1],
        shard_b[2],
        shard_b[3],
        shard_b[4],
        shard_b[5],
    )


def solution(mesh):
    return jax.shard_map(
        per_device,
        mesh=mesh,
        in_specs=(
            P(("outer", "inner"), None, None),
            P(("outer", "inner"), None, None),
            P(("outer", "inner")),
            P(("outer", "inner"), None),
            P(("outer", "inner")),
            P("inner", "outer"),
            P("inner", "outer"),
            P(("outer", "inner")),
            P("inner", "outer"),
            P("inner", "outer"),
            P(("outer", "inner")),
            P(("outer", "inner")),
            P("inner", "outer"),
            P("inner", "outer"),
            P(("outer", "inner")),
            P("inner", "outer"),
            P("inner", "outer"),
        ),
        out_specs=(
            P(("outer", "inner"), None, None),
            P(("outer", "inner"), None, None),
            P(("outer", "inner")),
            P("inner", "outer"),
            P("inner", "outer"),
            P(("outer", "inner")),
            P("inner", "outer"),
            P("inner", "outer"),
            P(("outer", "inner")),
            P(("outer", "inner")),
            P("inner", "outer"),
            P("inner", "outer"),
            P(("outer", "inner")),
            P("inner", "outer"),
            P("inner", "outer"),
        ),
        check_vma=False,
    )
```

profile of v0, /device:TPU:0, one launch (start us, length us, event | category | flops | bytes accessed | tf_op | source)
XLA Modules:
  0.0 2003.4 jit_solution(16910447046243304602)
XLA Ops:
  54.3 43.2 %all-gather.26.cloned.1.call-done = bf16[768,1536]{1,0:T(8,128)(2,1)} async-done(((bf16[48,1536]{1,0:T(8,128)(2,1)}), bf16[768,1536]{1,0:T(8,128)(2,1)}) %all-gather.26.cloned.1.call-update) | async-done | bytes 2359312 | tf_op jit(solution)/shard_map/all_gather | solution.py:202
  97.6 43.4 %all-gather.30.cloned.1.call-done = bf16[3072,384]{1,0:T(8,128)(2,1)} async-done(((bf16[192,384]{1,0:T(8,128)(2,1)}), bf16[3072,384]{1,0:T(8,128)(2,1)}) %all-gather.30.cloned.1.call-update) | async-done | bytes 2359312 | tf_op jit(solution)/shard_map/all_gather | solution.py:203
  292.3 50.9 %all-gather.22.cloned.1.call-done = bf16[768,2304]{1,0:T(8,128)(2,1)} async-done(((bf16[768,1152]{1,0:T(8,128)(2,1)}), bf16[768,2304]{1,0:T(8,128)(2,1)}) %all-gather.22.cloned.1.call-update) | async-done | bytes 3538960 | tf_op jit(solution)/shard_map/all_gather | solution.py:208
  343.3 64.2 %all-gather.28.cloned.1.call-done = bf16[768,3072]{1,0:T(8,128)(2,1)} async-done(((bf16[768,1536]{1,0:T(8,128)(2,1)}), bf16[768,3072]{1,0:T(8,128)(2,1)}) %all-gather.28.cloned.1.call-update) | async-done | bytes 4718608 | tf_op jit(solution)/shard_map/all_gather | solution.py:211
  407.5 64.1 %all-gather.32.cloned.1.call-done = bf16[3072,768]{1,0:T(8,128)(2,1)} async-done(((bf16[3072,384]{1,0:T(8,128)(2,1)}), bf16[3072,768]{1,0:T(8,128)(2,1)}) %all-gather.32.cloned.1.call-update) | async-done | bytes 4718608 | tf_op jit(solution)/shard_map/all_gather | solution.py:212
  553.2 54.6 %while.194 = (s32[]{:T(128)}, bf16[12,1024,64]{1,2,0:T(8,128)(2,1)}, bf16[12,1024,64]{2,1,0:T(8,128)(2,1)}, bf16[12,1024,64]{2,1,0:T(8,128)(2,1)S(1)}, bf16[12,1024,64]{2,1,0:T(8,128)(2,1)}, /*index=5*/s32[]{:T(128)}) while((s32[]{:T(128)}, bf16[12,1024,64]{1,2,0:T(8,128)(2,1)}, bf16[12,1024,64]{2,1,0:T(8,128)(2,1)}, ...), condition=%wide.region_31.32_spmd, body=%wide.region_28.31_spmd.sunk | while | flops 284227584 | bytes 13523021 | solution.py:66
  630.8 44.4 %all-gather.46.cloned.1.call-done = bf16[3072,768]{1,0:T(8,128)(2,1)} async-done(((bf16[3072,384]{1,0:T(8,128)(2,1)}), bf16[3072,768]{1,0:T(8,128)(2,1)}) %all-gather.46.cloned.1.call-update) | async-done | bytes 4718608 | tf_op jit(solution)/shard_map/all_gather | solution.py:238
  712.6 133.5 %while.195 = (s32[]{:T(128)}, bf16[12,1024,64]{1,2,0:T(8,128)(2,1)}, bf16[12,1024,64]{1,2,0:T(8,128)(2,1)}, bf16[12,1024,64]{1,2,0:T(8,128)(2,1)}, bf16[12,1024,...) while((s32[]{:T(128)}, bf16[12,1024,64]{1,2,0:T(8,128)(2,1)}, ...), condition=%wide.region_38.39_spmd, body=%wide.region_34.38_spmd.sunk | while | flops 703591424 | bytes 38323300 | solution.py:95
  862.4 137.6 %conditional.3 = (bf16[768]{0:T(1024)(128)(2,1)}, bf16[768,2304]{1,0:T(8,128)(2,1)}, bf16[768,768]{1,0:T(8,128)(2,1)}, bf16[768]{0:T(1024)(128)(2,1)}, bf16[768,...) conditional(s32[]{:T(128)} %bitcast.134, (s32[512]{0:T(512)S(1)}, ...), branch_computations={%region_40.60_spmd, %region_60.0_spmd, %region_80.100_spmd} | conditional | flops 22077542400 | bytes 332482272 | solution.py:155
  911.3 48.7 %while.186 = (s32[]{:T(128)}, bf16[12,128,64]{1,2,0:T(8,128)(2,1)S(1)}, bf16[12,128,64]{1,2,0:T(8,128)(2,1)S(1)}, bf16[12,128,64]{1,2,0:T(8,128)(2,1)S(1)}, bf16...) while((s32[]{:T(128)}, ...), condition=%wide.region_53.53_spmd, body=%wide.region_49.52_spmd.sunk | while | flops 10796674 | bytes 862821 | solution.py:95
  1060.6 79.3 %reduce-scatter.51.cloned.1.call-done = bf16[384,768]{1,0:T(8,128)(2,1)} async-done(((bf16[768,768]{1,0:T(8,128)(2,1)}), bf16[384,768]{1,0:T(8,128)(2,1)}) %reduce-scatter.51.cloned.1.call-update) | async-done | bytes 589840
  1142.1 47.6 %reduce-scatter.55.cloned.1.call-done = bf16[1152,768]{1,0:T(8,128)(2,1)} async-done(((bf16[2304,768]{1,0:T(8,128)(2,1)}), bf16[1152,768]{1,0:T(8,128)(2,1)}) %reduce-scatter.55.cloned.1.call-update) | async-done | bytes 1769488
  1193.6 46.0 %reduce-scatter.49.cloned.1.call-done = bf16[1152,768]{1,0:T(8,128)(2,1)} async-done(((bf16[2304,768]{1,0:T(8,128)(2,1)}), bf16[1152,768]{1,0:T(8,128)(2,1)}) %reduce-scatter.49.cloned.1.call-update) | async-done | bytes 1769488
  1243.6 58.4 %reduce-scatter.43.cloned.1.call-done = bf16[768,1536]{1,0:T(8,128)(2,1)} async-done(((bf16[768,3072]{1,0:T(8,128)(2,1)}), bf16[768,1536]{1,0:T(8,128)(2,1)}) %reduce-scatter.43.cloned.1.call-update) | async-done | bytes 2359312 | tf_op jit(solution)/shard_map/reduce_scatter | solution.py:286
  1302.0 62.2 %reduce-scatter.59.cloned.1.call-done = bf16[384,3072]{1,0:T(8,128)(2,1)} async-done(((bf16[768,3072]{1,0:T(8,128)(2,1)}), bf16[384,3072]{1,0:T(8,128)(2,1)}) %reduce-scatter.59.cloned.1.call-update) | async-done | bytes 2359312
  1368.6 58.0 %reduce-scatter.33.cloned.1.call-done = bf16[768,1536]{1,0:T(8,128)(2,1)} async-done(((bf16[768,3072]{1,0:T(8,128)(2,1)}), bf16[768,1536]{1,0:T(8,128)(2,1)}) %reduce-scatter.33.cloned.1.call-update) | async-done | bytes 2359312 | tf_op jit(solution)/shard_map/reduce_scatter | solution.py:361
  1426.6 62.4 %reduce-scatter.53.cloned.1.call-done = bf16[384,3072]{1,0:T(8,128)(2,1)} async-done(((bf16[768,3072]{1,0:T(8,128)(2,1)}), bf16[384,3072]{1,0:T(8,128)(2,1)}) %reduce-scatter.53.cloned.1.call-update) | async-done | bytes 2359312
  1553.0 52.3 %reduce-scatter.31.cloned.1.call-done = bf16[48,384]{1,0:T(8,128)(2,1)} async-done(((bf16[768,384]{1,0:T(8,128)(2,1)}), bf16[48,384]{1,0:T(8,128)(2,1)}) %reduce-scatter.31.cloned.1.call-update) | async-done | bytes 36880 | tf_op jit(solution)/shard_map/reduce_scatter | solution.py:378
  1606.7 61.7 %reduce-scatter.39.cloned.1.call-done = bf16[48,1152]{1,0:T(8,128)(2,1)} async-done(((bf16[768,1152]{1,0:T(8,128)(2,1)}), bf16[48,1152]{1,0:T(8,128)(2,1)}) %reduce-scatter.39.cloned.1.call-update) | async-done | bytes 110608 | tf_op jit(solution)/shard_map/reduce_scatter | solution.py:297
  1669.9 61.1 %reduce-scatter.29.cloned.1.call-done = bf16[48,1152]{1,0:T(8,128)(2,1)} async-done(((bf16[768,1152]{1,0:T(8,128)(2,1)}), bf16[48,1152]{1,0:T(8,128)(2,1)}) %reduce-scatter.29.cloned.1.call-update) | async-done | bytes 110608 | tf_op jit(solution)/shard_map/reduce_scatter | solution.py:375
  1732.6 64.0 %reduce-scatter.45.cloned.1.call-done = bf16[48,1536]{1,0:T(8,128)(2,1)} async-done(((bf16[768,1536]{1,0:T(8,128)(2,1)}), bf16[48,1536]{1,0:T(8,128)(2,1)}) %reduce-scatter.45.cloned.1.call-update) | async-done | bytes 147472 | tf_op jit(solution)/shard_map/reduce_scatter | solution.py:306
  1798.3 64.6 %reduce-scatter.47.cloned.1.call-done = bf16[192,384]{1,0:T(8,128)(2,1)} async-done(((bf16[3072,384]{1,0:T(8,128)(2,1)}), bf16[192,384]{1,0:T(8,128)(2,1)}) %reduce-scatter.47.cloned.1.call-update) | async-done | bytes 147472 | tf_op jit(solution)/shard_map/reduce_scatter | solution.py:309
  1864.5 64.2 %reduce-scatter.35.cloned.1.call-done = bf16[48,1536]{1,0:T(8,128)(2,1)} async-done(((bf16[768,1536]{1,0:T(8,128)(2,1)}), bf16[48,1536]{1,0:T(8,128)(2,1)}) %reduce-scatter.35.cloned.1.call-update) | async-done | bytes 147472 | tf_op jit(solution)/shard_map/reduce_scatter | solution.py:384
  1930.3 64.4 %reduce-scatter.37.cloned.1.call-done = bf16[192,384]{1,0:T(8,128)(2,1)} async-done(((bf16[3072,384]{1,0:T(8,128)(2,1)}), bf16[192,384]{1,0:T(8,128)(2,1)}) %reduce-scatter.37.cloned.1.call-update) | async-done | bytes 147472 | tf_op jit(solution)/shard_map/reduce_scatter | solution.py:387
  (668 shorter events, 844.2 us)
Async XLA Ops:
  10.6 279.2 %all-gather.44.cloned.1.call-start = ((), (), s32[]{:S(2)}) async-start(), calls=%async_computation.28 | async-start | bytes 2506752 | tf_op jit(solution)/shard_map/all_gather | solution.py:230
  11.1 281.2 %all-gather.24.cloned.1.call-start = ((), (), s32[]{:S(2)}) async-start(), calls=%async_computation.18 | async-start | bytes 1769472 | tf_op jit(solution)/shard_map/all_gather | solution.py:209
  38.5 304.7 %all-gather.22.cloned.1.call-start = ((), (), s32[]{:S(2)}) async-start(), calls=%async_computation.17 | async-start | bytes 5308416 | tf_op jit(solution)/shard_map/all_gather | solution.py:208
  54.3 353.2 %all-gather.28.cloned.1.call-start = ((), (), s32[]{:S(2)}) async-start(), calls=%async_computation.20 | async-start | bytes 7077888 | tf_op jit(solution)/shard_map/all_gather | solution.py:211
  97.6 374.0 %all-gather.32.cloned.1.call-start = ((), (), s32[]{:S(2)}) async-start(), calls=%async_computation.22 | async-start | bytes 7077888 | tf_op jit(solution)/shard_map/all_gather | solution.py:212
  141.1 381.5 %all-gather.36.cloned.1.call-start = ((), (), s32[]{:S(2)}) async-start(), calls=%async_computation.24 | async-start | bytes 5308416 | tf_op jit(solution)/shard_map/all_gather | solution.py:234
  182.2 430.4 %all-gather.38.cloned.1.call-start = ((), (), s32[]{:S(2)}) async-start(), calls=%async_computation.25 | async-start | bytes 1769472 | tf_op jit(solution)/shard_map/all_gather | solution.py:235
  204.9 413.7 %all-gather.42.cloned.1.call-start = ((), (), s32[]{:S(2)}) async-start(), calls=%async_computation.27 | async-start | bytes 7077888 | tf_op jit(solution)/shard_map/all_gather | solution.py:237
  225.8 449.4 %all-gather.46.cloned.1.call-start = ((), (), s32[]{:S(2)}) async-start(), calls=%async_computation.29 | async-start | bytes 7077888 | tf_op jit(solution)/shard_map/all_gather | solution.py:238
  289.8 768.6 %reduce-scatter.57.cloned.1.call-start = ((), (), s32[]{:S(2)}) async-start(), calls=%async_computation.44 | async-start | bytes 1769472
  704.7 435.2 %reduce-scatter.51.cloned.1.call-start = ((), (), s32[]{:S(2)}) async-start(), calls=%async_computation.41 | async-start | bytes 1769472
  1013.6 226.0 %reduce-scatter.49.cloned.1.call-start = ((), (), s32[]{:S(2)}) async-start(), calls=%async_computation.40 | async-start | bytes 5308416
  1019.4 282.5 %reduce-scatter.43.cloned.1.call-start = ((), (), s32[]{:S(2)}) async-start(), calls=%async_computation.37 | async-start | bytes 7077888 | tf_op jit(solution)/shard_map/reduce_scatter | solution.py:286
  1031.0 333.3 %reduce-scatter.59.cloned.1.call-start = ((), (), s32[]{:S(2)}) async-start(), calls=%async_computation.45 | async-start | bytes 7077888
  1050.6 375.9 %reduce-scatter.33.cloned.1.call-start = ((), (), s32[]{:S(2)}) async-start(), calls=%async_computation.32 | async-start | bytes 7077888 | tf_op jit(solution)/shard_map/reduce_scatter | solution.py:361
  1051.4 437.6 %reduce-scatter.53.cloned.1.call-start = ((), (), s32[]{:S(2)}) async-start(), calls=%async_computation.42 | async-start | bytes 7077888
  1058.1 493.5 %reduce-scatter.41.cloned.1.call-start = ((), (), s32[]{:S(2)}) async-start(), calls=%async_computation.36 | async-start | bytes 626688 | tf_op jit(solution)/shard_map/reduce_scatter | solution.py:300
  1060.5 544.7 %reduce-scatter.31.cloned.1.call-start = ((), (), s32[]{:S(2)}) async-start(), calls=%async_computation.31 | async-start | bytes 626688 | tf_op jit(solution)/shard_map/reduce_scatter | solution.py:378
  1142.1 526.2 %reduce-scatter.39.cloned.1.call-start = ((), (), s32[]{:S(2)}) async-start(), calls=%async_computation.35 | async-start | bytes 1880064 | tf_op jit(solution)/shard_map/reduce_scatter | solution.py:297
  1193.6 537.4 %reduce-scatter.29.cloned.1.call-start = ((), (), s32[]{:S(2)}) async-start(), calls=%async_computation.30 | async-start | bytes 1880064 | tf_op jit(solution)/shard_map/reduce_scatter | solution.py:375
  1243.5 553.1 %reduce-scatter.45.cloned.1.call-start = ((), (), s32[]{:S(2)}) async-start(), calls=%async_computation.38 | async-start | bytes 2506752 | tf_op jit(solution)/shard_map/reduce_scatter | solution.py:306
  1302.0 560.9 %reduce-scatter.47.cloned.1.call-start = ((), (), s32[]{:S(2)}) async-start(), calls=%async_computation.39 | async-start | bytes 2506752 | tf_op jit(solution)/shard_map/reduce_scatter | solution.py:309
  1368.5 560.1 %reduce-scatter.35.cloned.1.call-start = ((), (), s32[]{:S(2)}) async-start(), calls=%async_computation.33 | async-start | bytes 2506752 | tf_op jit(solution)/shard_map/reduce_scatter | solution.py:384
  1426.6 568.1 %reduce-scatter.37.cloned.1.call-start = ((), (), s32[]{:S(2)}) async-start(), calls=%async_computation.34 | async-start | bytes 2506752 | tf_op jit(solution)/shard_map/reduce_scatter | solution.py:387
  (89 other events, 3553.4 us)
Sparse Core Ops, SparseCore 0:
  10.2 44.0 all-gather.19
  99.8 41.0 all-gather.29
  184.3 41.4 all-gather.39
  293.9 49.3 all-gather.21
  344.8 62.6 all-gather.27
  408.9 62.6 all-gather.31
  473.1 49.3 all-gather.35
  548.4 62.6 all-gather.41
  612.5 62.6 all-gather.45
  1002.5 137.3 reduce-scatter.50
  1142.0 47.6 reduce-scatter.54
  1191.9 47.6 reduce-scatter.48
  1241.9 59.9 reduce-scatter.42
  1304.2 59.9 reduce-scatter.58
  1366.5 59.9 reduce-scatter.32
  1429.0 59.9 reduce-scatter.52
  1492.6 54.8 reduce-scatter.40
  1551.3 53.8 reduce-scatter.30
  1609.0 59.2 reduce-scatter.38
  1671.9 59.0 reduce-scatter.28
  1734.6 61.9 reduce-scatter.44
  1800.9 61.9 reduce-scatter.46
  1866.6 61.9 reduce-scatter.34
  1932.8 61.9 reduce-scatter.36
  (6 shorter events, 187.5 us)
where the time goes:
time: 2020 us; the launch traced here: 2000 us
  waiting for transfers between devices  1260 us (62%)
  matrix products  367 us (18%)
  blocking collectives  144 us (7%)
  local copies, waits for them, and re-layouts  110 us (5%)
  other arithmetic  77.2 us (4%)
  loops' own time  26.4 us (1%)
    dot_general x219, matrix products, product(): return jnp.dot(left, right, preferred_element_type=jnp.float32)  367 us
    unnamed x36, waiting for transfers between devices  302 us
    unnamed x3, blocking collectives  71.9 us
    reduce_scatter x1, waiting for transfers between devices, per_device(): lax.psum_scatter(columns_b[5].astype(jnp.bfloat16), 'inner', scatter_dime...  64.6 us
    reduce_scatter x1, waiting for transfers between devices, per_device(): lax.psum_scatter(columns_a[5].astype(jnp.bfloat16), 'inner', scatter_dime...  64.4 us
    all_gather x1, waiting for transfers between devices, per_device(): lax.all_gather(rows_a[4], 'outer', axis=1, tiled=True)  64.2 us
    reduce_scatter x1, waiting for transfers between devices, per_device(): lax.psum_scatter(columns_a[4].astype(jnp.bfloat16), 'inner', scatter_dime...  64.2 us
    all_gather x1, waiting for transfers between devices, per_device(): lax.all_gather(rows_a[5], 'outer', axis=1, tiled=True)  64.1 us
  transfers between devices with their start and end apart: 30, of which 25 were waited for; matrix products, arithmetic and copies ran while one was open for 26% of the time, Pallas kernels for 0%

commit v1 on v0

v1 whole, which is shorter than its diff:
```python
import functools

import jax
import jax.numpy as jnp
from jax import lax
from jax.experimental import pallas as pl
from jax.experimental.pallas import tpu as pltpu
from jax.sharding import PartitionSpec as P

HEADS = 12
HEAD = 64
MESH = pl.DeviceIdType.MESH


def place():
    o, i = lax.axis_index("outer"), lax.axis_index("inner")
    return o, i // 4, (i // 2) % 2, i % 2


def device(o, z, x, c):
    return (o, z * 4 + x * 2 + c)


def greet(o, z, x, c):
    barrier = pltpu.get_barrier_semaphore()
    signal = functools.partial(pl.semaphore_signal, barrier, inc=1, device_id_type=MESH)
    signal(device_id=device(1 - o, z, x, c))
    signal(device_id=device(o, z, 1 - x, c))
    signal(device_id=device(o, z, x, 1 - c))

    @pl.when(z > 0)
    def _():
        signal(device_id=device(o, z - 1, x, c))

    @pl.when(z < 3)
    def _():
        signal(device_id=device(o, z + 1, x, c))

    pl.semaphore_wait(barrier, 3 + jnp.where(z > 0, 1, 0) + jnp.where(z < 3, 1, 0))


def scatter_kernel(n, *refs):
    grads, outs = refs[:n], refs[n:2 * n]
    rest = refs[2 * n:]
    own, got_c, got_b, got_a, got_z = (rest[j * n:(j + 1) * n] for j in range(5))
    local_sem, send_sem, recv_sem = rest[5 * n:]
    o, z, x, c = place()
    greet(o, z, x, c)

    def block(p, s, cc):
        r, w = outs[p].shape
        bs, as_, k = s // 8, (s // 4) % 2, s % 4
        if p % 2 == 0:
            co, cx = jnp.where(bs == 1, o, 1 - o), jnp.where(as_ == 1, x, 1 - x)
        else:
            cx, co = jnp.where(bs == 1, x, 1 - x), jnp.where(as_ == 1, o, 1 - o)
        row = pl.multiple_of((k * 4 + cx * 2 + cc) * r, 16)
        col = pl.multiple_of(co * w, 128)
        return grads[p].at[pl.ds(row, r), pl.ds(col, w)]

    def a_dev(p):
        return device(o, z, 1 - x, c) if p % 2 == 0 else device(1 - o, z, x, c)

    def b_dev(p):
        return device(1 - o, z, x, c) if p % 2 == 0 else device(o, z, 1 - x, c)

    def send(p, src, dst, kind, rslot, target):
        return pltpu.make_async_remote_copy(
            src_ref=src, dst_ref=dst, send_sem=send_sem.at[p, kind], recv_sem=recv_sem.at[p, rslot],
            device_id=target, device_id_type=MESH)

    def wait(ref, sem):
        pltpu.make_async_copy(ref, ref, sem).wait()

    def loop(count, body):
        def step(s, carry):
            body(s)
            return carry
        lax.fori_loop(0, count, step, 0)

    def begin(p):
        def body(s):
            send(p, block(p, s, 1 - c), got_c[p].at[s], 0, s, device(o, z, x, 1 - c)).start()
            pltpu.make_async_copy(block(p, s, c), own[p].at[s], local_sem.at[p]).start()
        loop(16, body)

    def core_stage(p):
        wait(own[p], local_sem.at[p])

        def body(s):
            wait(got_c[p].at[s], recv_sem.at[p, s])
            own[p][s] = own[p][s] + got_c[p][s]

            @pl.when(s < 8)
            def _():
                send(p, own[p].at[s], got_b[p].at[s], 1, 16 + s, b_dev(p)).start()
        loop(16, body)

    def b_stage(p):
        def body(j):
            wait(got_b[p].at[j], recv_sem.at[p, 16 + j])
            own[p][8 + j] = own[p][8 + j] + got_b[p][j]

            @pl.when(j < 4)
            def _():
                send(p, own[p].at[8 + j], got_a[p].at[j], 2, 24 + j, a_dev(p)).start()
        loop(8, body)

    def send_z(p, k, step):
        t = z + step
        slot = jnp.where(k == t, jnp.where(step > 0, k, 4), k)
        send(p, own[p].at[12 + k], got_z[p].at[slot], 3, 28 + slot, device(o, t, x, c)).start()

    def a_stage(p):
        def body(k):
            wait(got_a[p].at[k], recv_sem.at[p, 24 + k])
            own[p][12 + k] = own[p][12 + k] + got_a[p][k]
        loop(4, body)

        @pl.when(z == 0)
        def _():
            for k in (3, 2, 1):
                send_z(p, k, 1)

        @pl.when(z == 3)
        def _():
            for k in (0, 1, 2):
                send_z(p, k, -1)

    def pass_on(p, k, step):
        wait(got_z[p].at[k], recv_sem.at[p, 28 + k])
        own[p][12 + k] = own[p][12 + k] + got_z[p][k]
        send_z(p, k, step)

    def z_stage(p, level):
        @pl.when(z == level)
        def _():
            for k in range(3, level, -1):
                pass_on(p, k, 1)

        @pl.when(z == 3 - level)
        def _():
            for k in range(0, 3 - level):
                pass_on(p, k, -1)

    def last(p):
        outs[p][...] = own[p][12 + z].astype(jnp.float32)

        @pl.when(z > 0)
        def _():
            wait(got_z[p].at[z], recv_sem.at[p, 28 + z])
            outs[p][...] += got_z[p][z].astype(jnp.float32)

        @pl.when(z < 3)
        def _():
            wait(got_z[p].at[4], recv_sem.at[p, 32])
            outs[p][...] += got_z[p][4].astype(jnp.float32)

        wait(own[p], send_sem.at[p, 0])
        wait(got_b[p], send_sem.at[p, 1])
        wait(got_a[p], send_sem.at[p, 2])
        wait(got_a[p].at[pl.ds(0, 3)], send_sem.at[p, 3])

    for p in range(n):
        begin(p)
    stages = [core_stage, b_stage, a_stage, lambda p: z_stage(p, 1), lambda p: z_stage(p, 2), last]
    for t in range(n + len(stages) - 1):
        for lag, stage in enumerate(stages):
            if 0 <= t - lag < n:
                stage(t - lag)


def scatter_all(grads, outer, inner, collective_id=1):
    n = len(grads)
    outs = [jax.ShapeDtypeStruct((g.shape[0] // inner, g.shape[1] // outer), jnp.float32) for g in grads]
    bufs = [pltpu.VMEM((m,) + s.shape, jnp.bfloat16) for m in (16, 16, 8, 4, 5) for s in outs]
    return pl.pallas_call(
        functools.partial(scatter_kernel, n),
        out_shape=outs,
        in_specs=[pl.BlockSpec(memory_space=pl.ANY)] * n,
        out_specs=[pl.BlockSpec(memory_space=pltpu.VMEM)] * n,
        scratch_shapes=bufs + [pltpu.SemaphoreType.DMA((n,)), pltpu.SemaphoreType.DMA((n, 4)), pltpu.SemaphoreType.DMA((n, 33))],
        compiler_params=pltpu.CompilerParams(collective_id=collective_id, has_side_effects=True, vmem_limit_bytes=60 * 2**20),
        name="scatter_gradients",
    )(*grads)


def gather_kernel(n, *refs):
    shards, outs = refs[:n], refs[n:2 * n]
    local_sem, send_sem, recv_sem = refs[2 * n:]
    o, z, x, c = place()

    greet(o, z, x, c)

    def block(p, co, cz, cx, cc):
        r, w = shards[p].shape
        row = pl.multiple_of((cz * 4 + cx * 2 + cc) * r, 16)
        col = pl.multiple_of(co * w, 128)
        return outs[p].at[pl.ds(row, r), pl.ds(col, w)]

    def send(p, src, dst, slot, rslot, target):
        return pltpu.make_async_remote_copy(
            src_ref=src, dst_ref=dst, send_sem=send_sem.at[p, slot], recv_sem=recv_sem.at[p, rslot],
            device_id=target, device_id_type=MESH)

    def up(p, k, src=None):
        b = block(p, o, k, x, c)
        return send(p, b if src is None else src, b, k, k, device(o, z + 1, x, c))

    def down(p, k, src=None):
        b = block(p, o, k, x, c)
        return send(p, b if src is None else src, b, 4 + k, k, device(o, z - 1, x, c))

    def first(p, k, src=None):
        b = block(p, o, k, x, c)
        t = device(o, z, 1 - x, c) if p % 2 == 0 else device(1 - o, z, x, c)
        return send(p, b if src is None else src, b, 8 + k, 4 + k, t)

    def second(p, k, a, src=None):
        if p % 2 == 0:
            b, t = block(p, o, k, a, c), device(1 - o, z, x, c)
        else:
            b, t = block(p, a, k, x, c), device(o, z, 1 - x, c)
        return send(p, b if src is None else src, b, 12 + 2 * k + a, 8 + 2 * k + a, t)

    def core(p, co, k, cx, src=None):
        b = block(p, co, k, cx, c)
        s = k * 4 + co * 2 + cx
        return send(p, b if src is None else src, b, 20 + s, 16 + s, device(o, z, x, 1 - c))

    def mine(p):
        return x if p % 2 == 0 else o

    def coords(p, k, a, b):
        return (b, k, a) if p % 2 == 0 else (a, k, b)

    def core_ab(p, k, a, b, src=None):
        co, ck, cx = coords(p, k, a, b)
        return core(p, co, ck, cx, src)

    def other(p):
        return o if p % 2 == 0 else x

    def own(p):
        s = shards[p]
        pltpu.make_async_copy(s, block(p, o, z, x, c), local_sem.at[p]).start()

        @pl.when(z < 3)
        def _():
            up(p, z, s).start()

        @pl.when(z > 0)
        def _():
            down(p, z, s).start()

        first(p, z, s).start()
        second(p, z, mine(p), s).start()
        core(p, o, z, x, s).start()

    def wait_block(p, rslot):
        b = block(p, o, z, x, c)
        pltpu.make_async_copy(shards[p], b, recv_sem.at[p, rslot]).wait()

    def z_phase(p):
        for d in range(1, 4):
            @pl.when(z >= d)
            def _():
                k = z - d
                wait_block(p, k)

                @pl.when(z < 3)
                def _():
                    up(p, k).start()

                first(p, k).start()
                second(p, k, mine(p)).start()
                core(p, o, k, x).start()

            @pl.when(z + d <= 3)
            def _():
                k = z + d
                wait_block(p, k)

                @pl.when(z > 0)
                def _():
                    down(p, k).start()

                first(p, k).start()
                second(p, k, mine(p)).start()
                core(p, o, k, x).start()

    def ks():
        return [(z + d) % 4 for d in range(4)]

    def a_phase(p):
        for k in ks():
            wait_block(p, 4 + k)
            a = 1 - mine(p)
            second(p, k, a).start()
            core_ab(p, k, a, other(p)).start()

    def b_phase(p):
        for k in ks():
            for a in (mine(p), 1 - mine(p)):
                wait_block(p, 8 + 2 * k + a)
                core_ab(p, k, a, 1 - other(p)).start()

    def c_phase(p):
        for s in range(16):
            wait_block(p, 16 + s)

    def ends(p):
        pltpu.make_async_copy(shards[p], block(p, o, z, x, c), local_sem.at[p]).wait()

        def done(slot):
            pltpu.make_async_copy(shards[p], block(p, o, z, x, c), send_sem.at[p, slot]).wait()

        for k in range(4):
            @pl.when(jnp.logical_and(z < 3, k <= z))
            def _():
                done(k)

            @pl.when(jnp.logical_and(z > 0, k >= z))
            def _():
                done(4 + k)
        for slot in range(8, 36):
            done(slot)

    own(0)
    for t in range(n + 3):
        if t + 1 < n:
            own(t + 1)
        if t < n:
            z_phase(t)
        if 0 <= t - 1 < n:
            a_phase(t - 1)
        if 0 <= t - 2 < n:
            b_phase(t - 2)
    for p in range(n):
        c_phase(p)
        ends(p)


def gather_all(shards, outer, inner, collective_id=0):
    n = len(shards)
    outs = [jax.ShapeDtypeStruct((s.shape[0] * inner, s.shape[1] * outer), s.dtype) for s in shards]
    return pl.pallas_call(
        functools.partial(gather_kernel, n),
        out_shape=outs,
        in_specs=[pl.BlockSpec(memory_space=pl.ANY)] * n,
        out_specs=[pl.BlockSpec(memory_space=pl.ANY)] * n,
        scratch_shapes=[pltpu.SemaphoreType.DMA((n,)), pltpu.SemaphoreType.DMA((n, 36)), pltpu.SemaphoreType.DMA((n, 32))],
        compiler_params=pltpu.CompilerParams(collective_id=collective_id, has_side_effects=True),
        name="gather_weights",
    )(*shards)


C = 0.125 * 1.4426950408889634
T = 256


def dg(a, b, ca, cb):
    return lax.dot_general(a, b, (((ca,), (cb,)), ((), ())), preferred_element_type=jnp.float32)


def split(x):
    lane = lax.broadcasted_iota(jnp.int32, x.shape, 1)
    z = jnp.zeros_like(x)
    return jnp.where(lane < 64, x, z), jnp.where(lane < 64, z, x)


def fwd_kernel(variant, q_ref, k_ref, v_ref, o_ref, lse_ref):
    L = q_ref.shape[0]
    lane = lax.broadcasted_iota(jnp.int32, (T, 128), 1)
    lane_t = lax.broadcasted_iota(jnp.int32, (128, T), 0)
    v0, v1 = split(v_ref[...])
    for i in range(L // T):
        n = (i + 1) * T
        q = q_ref[i * T:n, :]
        qs = split(q)
        k = k_ref[:n, :]
        acc = None
        for h in range(2):
            v = (v0, v1)[h][:n]
            if variant == 1:
                s = dg(qs[h], k, 1, 1)
                r = lax.broadcasted_iota(jnp.int32, (T, T), 0) >= lax.broadcasted_iota(jnp.int32, (T, T), 1)
                last = jnp.where(r, s[:, i * T:], -1e30)
                s = last if i == 0 else jnp.concatenate([s[:, :i * T], last], axis=1)
                m = jnp.max(s, axis=1, keepdims=True) * C
                p = jnp.exp2(s * C - m)
                l = jnp.sum(p, axis=1, keepdims=True)
                o = dg(p.astype(jnp.bfloat16), v, 1, 0) / l
                acc = o if acc is None else acc + o
                lse_ref[0, i * T:n, h:h + 1] = m + jnp.log2(l)
            else:
                s = dg(k, qs[h], 1, 1)
                r = lax.broadcasted_iota(jnp.int32, (T, T), 1) >= lax.broadcasted_iota(jnp.int32, (T, T), 0)
                last = jnp.where(r, s[i * T:], -1e30)
                s = last if i == 0 else jnp.concatenate([s[:i * T], last], axis=0)
                m = jnp.max(s, axis=0, keepdims=True) * C
                p = jnp.exp2(s * C - m)
                l = jnp.sum(p, axis=0, keepdims=True)
                lse_ref[0, h:h + 1, i * T:n] = m + jnp.log2(l)
                pb = p.astype(jnp.bfloat16)
                if variant == 2:
                    pb = (p * (1.0 / l)).astype(jnp.bfloat16)
                    o = dg(pb, v, 0, 0)
                else:
                    o = dg(v, pb, 0, 0) / l
                acc = o if acc is None else acc + o
        if variant == 3:
            acc = acc.T
        o_ref[i * T:n, :] = acc.astype(jnp.bfloat16)


def attend(projected, variant=2):
    L = projected.shape[0]
    lse_shape = (6, L, 8) if variant == 1 else (6, 8, L)
    return pl.pallas_call(
        functools.partial(fwd_kernel, variant),
        grid=(6,),
        in_specs=[pl.BlockSpec((L, 128), lambda h: (0, h)), pl.BlockSpec((L, 128), lambda h: (0, 6 + h)),
                  pl.BlockSpec((L, 128), lambda h: (0, 12 + h))],
        out_specs=[pl.BlockSpec((L, 128), lambda h: (0, h)), pl.BlockSpec((1,) + lse_shape[1:], lambda h: (h, 0, 0))],
        out_shape=[jax.ShapeDtypeStruct((L, 768), jnp.bfloat16), jax.ShapeDtypeStruct(lse_shape, jnp.float32)],
        compiler_params=pltpu.CompilerParams(vmem_limit_bytes=48 * 2**20),
        name="attend_forward",
    )(projected, projected, projected)


def bwd_kernel(variant, q_ref, k_ref, v_ref, o_ref, do_ref, lse_ref, dq_ref, dk_ref, dv_ref, dq_acc):
    L = q_ref.shape[0]
    q, do = q_ref[...], do_ref[...]
    qs, dos = split(q), split(do)
    dd = do.astype(jnp.float32) * o_ref[...].astype(jnp.float32)
    pick = lax.broadcasted_iota(jnp.int32, (8, 128), 0) == lax.broadcasted_iota(jnp.int32, (8, 128), 1) // 64
    delta = lax.dot_general(pick.astype(jnp.float32), dd, (((1,), (1,)), ((), ())), precision=lax.Precision.HIGHEST,
                            preferred_element_type=jnp.float32)
    for j in range(L // T):
        a = j * T
        ks, vs = split(k_ref[a:a + T, :]), split(v_ref[a:a + T, :])
        dk = dv = dq = None
        for h in range(2):
            s = dg(ks[h], q[a:], 1, 1)
            p = jnp.exp2(s * C - lse_ref[0, h:h + 1, a:])
            r = lax.broadcasted_iota(jnp.int32, (T, T), 1) >= lax.broadcasted_iota(jnp.int32, (T, T), 0)
            first = jnp.where(r, p[:, :T], 0.0)
            p = first if a + T == L else jnp.concatenate([first, p[:, T:]], axis=1)
            dp = dg(vs[h], do[a:], 1, 1)
            ds = (p * (dp - delta[h:h + 1, a:])).astype(jnp.bfloat16)
            dv_h = dg(p.astype(jnp.bfloat16), dos[h][a:], 1, 0)
            dk_h = dg(ds, qs[h][a:], 1, 0)
            if variant == 1:
                dq_h = dg(ds, ks[h], 0, 0)
            else:
                dq_h = dg(ks[h], ds, 0, 0)
            dk = dk_h if dk is None else dk + dk_h
            dv = dv_h if dv is None else dv + dv_h
            dq = dq_h if dq is None else dq + dq_h
        dk_ref[a:a + T, :] = (0.125 * dk).astype(jnp.bfloat16)
        dv_ref[a:a + T, :] = dv.astype(jnp.bfloat16)
        if variant == 1:
            if j == 0:
                dq_acc[...] = dq
            else:
                dq_acc[a:, :] += dq
        else:
            if j == 0:
                dq_acc[...] = dq
            else:
                dq_acc[:, a:] += dq
    res = dq_acc[...] if variant == 1 else dq_acc[...].T
    dq_ref[...] = (0.125 * res).astype(jnp.bfloat16)


def attend_back(projected, merged, grad_merged, lse, variant=2):
    L = projected.shape[0]
    b = lambda off: pl.BlockSpec((L, 128), lambda h: (0, off + h))
    return pl.pallas_call(
        functools.partial(bwd_kernel, variant),
        grid=(6,),
        in_specs=[b(0), b(6), b(12), b(0), b(0), pl.BlockSpec((1, 8, L), lambda h: (h, 0, 0))],
        out_specs=[b(0)] * 3,
        out_shape=[jax.ShapeDtypeStruct((L, 768), jnp.bfloat16)] * 3,
        scratch_shapes=[pltpu.VMEM((L, 128) if variant == 1 else (128, L), jnp.float32)],
        compiler_params=pltpu.CompilerParams(vmem_limit_bytes=48 * 2**20),
        name="attend_backward",
    )(projected, projected, projected, merged, grad_merged, lse)


def lowered(values):
    return values.astype(jnp.bfloat16)


def product(left, right, ca=1, cb=0):
    return lax.dot_general(left, right, (((ca,), (cb,)), ((), ())), preferred_element_type=jnp.float32)


def rms_scale(values):
    return lax.rsqrt(jnp.mean(values * values, axis=-1, keepdims=True) + 1e-06)


def rms_back(values, gain, grad):
    r = rms_scale(values)
    unit = values * r
    scaled = grad * gain
    back = r * (scaled - unit * jnp.mean(scaled * unit, axis=-1, keepdims=True))
    return back, jnp.sum(grad * unit, axis=0)


def gelu_and_slope(u):
    k = 0.7978845608028654
    t = jnp.tanh(k * (u + 0.044715 * u * u * u))
    half = 0.5 * (1.0 + t)
    return u * half, half + 0.5 * u * (1.0 - t * t) * k * (1.0 + 3 * 0.044715 * u * u)


def block_forward(hidden, params):
    gain_attn, qkv, out, gain_mlp, up, down = params
    normed = lowered(hidden * rms_scale(hidden) * gain_attn)
    projected = lowered(product(normed, qkv))
    merged, lse = attend(projected)
    branch = product(merged, out)
    middle = hidden + branch
    normed_mlp = lowered(middle * rms_scale(middle) * gain_mlp)
    inner_pre = product(normed_mlp, up)
    active = lowered(gelu_and_slope(inner_pre)[0])
    result = branch + product(active, down)
    return result, (hidden, normed, projected, merged, lse, middle, normed_mlp, inner_pre, active)


def block_backward(saved, params, grad_result):
    gain_attn, qkv, out, gain_mlp, up, down = params
    hidden, normed, projected, merged, lse, middle, normed_mlp, inner_pre, active = saved
    grad_low = lowered(grad_result)
    grad_active = product(grad_low, down, 1, 1)
    grad_down = lowered(product(active, grad_low, 0, 0))
    grad_inner = lowered(grad_active * gelu_and_slope(inner_pre)[1])
    grad_normed_mlp = product(grad_inner, up, 1, 1)
    grad_up = lowered(product(normed_mlp, grad_inner, 0, 0))
    grad_middle, grad_gain_mlp = rms_back(middle, gain_mlp, grad_normed_mlp)
    grad_branch = lowered(grad_result + grad_middle)
    grad_merged = lowered(product(grad_branch, out, 1, 1))
    grad_out = lowered(product(merged, grad_branch, 0, 0))
    grad_projected = jnp.concatenate(attend_back(projected, merged, grad_merged, lse), axis=1)
    grad_normed = product(grad_projected, qkv, 1, 1)
    grad_qkv = lowered(product(normed, grad_projected, 0, 0))
    grad_hidden, grad_gain_attn = rms_back(hidden, gain_attn, grad_normed)
    return grad_hidden + grad_middle, (grad_gain_attn, grad_qkv, grad_out, grad_gain_mlp, grad_up, grad_down)


def parts_of(values, count):
    pieces = []
    for _ in range(count):
        piece = lowered(values)
        pieces.append(piece)
        values = values - piece.astype(jnp.float32)
    return pieces


def pack_vectors(vectors):
    row = jnp.concatenate([v.astype(jnp.bfloat16) for v in vectors])
    return jnp.zeros((16, 128), jnp.bfloat16).at[0, : row.shape[0]].set(row)


def unpack_vectors(tiles, count, size, outer, inner):
    rows = tiles.reshape(inner, 16, outer, 128)[:, 0].transpose(1, 0, 2)
    each = size // (outer * inner)
    return [rows[:, :, j * each : (j + 1) * each].reshape(size) for j in range(count)]


def spread_vectors(vectors, outer, inner):
    each = [v.reshape(outer, inner, -1) for v in vectors]
    rows = lowered(jnp.concatenate(each, axis=2)).transpose(1, 0, 2)
    rows = jnp.pad(rows, ((0, 0), (0, 0), (0, 128 - rows.shape[2])))
    tiles = jnp.pad(rows[:, None], ((0, 0), (0, 15), (0, 0), (0, 0)))
    return tiles.reshape(inner * 16, outer * 128)


def fits(shards, outer, inner):
    return outer == 2 and inner == 16 and all(s[0] % 16 == 0 and s[1] % 128 == 0 for s in shards)


def per_device(outer, inner, *args):
    hidden, cotangent, capacity_class, token_index = args[:4]
    (gain_attn_a, qkv_a, out_a, gain_mlp_a, up_a, down_a, router_shard,
     gain_attn_b, qkv_b, out_b, gain_mlp_b, up_b, down_b) = args[4:]
    hidden, cotangent, seq_class, index = hidden[0], cotangent[0], capacity_class[0], token_index[0]
    length, width = hidden.shape
    vectors = (gain_attn_a, gain_mlp_a, router_shard, gain_attn_b, gain_mlp_b)
    shards = [qkv_a, out_a, up_a, down_a, pack_vectors(vectors), qkv_b, out_b, up_b, down_b]
    remote = fits([s.shape for s in shards], outer, inner)
    if remote:
        whole = gather_all(shards, outer, inner)
    else:
        whole = [lax.all_gather(lax.all_gather(s, "inner", axis=0, tiled=True), "outer", axis=1, tiled=True) for s in shards]
    gains = [v.astype(jnp.float32) for v in unpack_vectors(whole[4], 5, width, outer, inner)]
    params_a = (gains[0], whole[0], whole[1], gains[1], whole[2], whole[3])
    router = gains[2]
    params_b = (gains[3], whole[5], whole[6], gains[4], whole[7], whole[8])

    slots = index.shape[0]
    capacity = (length // 8) << seq_class
    spot = jnp.where(lax.iota(jnp.int32, slots) < capacity, index, -1)
    pick = lowered(spot[:, None] == lax.broadcasted_iota(jnp.int32, (slots, length), 1))

    def put(rows):
        return sum(product(pick, piece, 0, 0) for piece in parts_of(rows, 3))

    def take(rows):
        return sum(product(pick, piece) for piece in parts_of(rows, 3))

    sequence = hidden.astype(jnp.float32)
    picked = product(pick, hidden)
    gate = jax.nn.sigmoid(jnp.sum(picked * router, axis=-1))[:, None]
    change, saved_a = block_forward(picked, params_a)
    middle = sequence + put(gate * change)
    result, saved_b = block_forward(middle, params_b)
    output = lowered(middle + result)

    upstream = cotangent.astype(jnp.float32)
    grad_middle, grads_b = block_backward(saved_b, params_b, upstream)
    grad_middle = upstream + grad_middle
    grad_rows = take(grad_middle)
    grad_picked, grads_a = block_backward(saved_a, params_a, gate * grad_rows)
    grad_logits = jnp.sum(grad_rows * change, axis=-1, keepdims=True) * gate * (1.0 - gate)
    grad_router = jnp.sum(grad_logits * picked, axis=0)
    input_grad = grad_middle + put(grad_picked + grad_logits * router)

    spread = spread_vectors((grads_a[0], grads_a[3], grad_router, grads_b[0], grads_b[3]), outer, inner)
    sums = [grads_a[1], grads_a[2], grads_a[4], grads_a[5], spread, grads_b[1], grads_b[2], grads_b[4], grads_b[5]]
    if remote:
        done = scatter_all(sums, outer, inner)
    else:
        done = [
            lax.psum_scatter(
                lax.psum_scatter(s, "outer", scatter_dimension=1, tiled=True), "inner", scatter_dimension=0, tiled=True
            ).astype(jnp.float32)
            for s in sums
        ]
    each = gain_attn_a.shape[0]
    vec = [done[4][0, j * each : (j + 1) * each] for j in range(5)]
    return (output[None], input_grad[None], vec[0], done[0], done[1], vec[1], done[2], done[3], vec[2],
            vec[3], done[5], done[6], vec[4], done[7], done[8])


def solution(mesh):
    outer, inner = mesh.shape["outer"], mesh.shape["inner"]
    both = ("outer", "inner")
    rows, vector, matrix = P(both, None, None), P(both), P("inner", "outer")
    block = (vector, matrix, matrix, vector, matrix, matrix)
    return jax.shard_map(
        functools.partial(per_device, outer, inner),
        mesh=mesh,
        in_specs=(rows, rows, vector, P(both, None)) + block + (vector,) + block,
        out_specs=(rows, rows) + block + (vector,) + block,
        check_vma=False,
    )
```

time: 2020 us -> 556 us (0.28)
  waiting for transfers between devices: 1260 us -> 0 us
  Pallas kernels: 0 us -> 356 us
  matrix products: 367 us -> 144 us
  blocking collectives: 144 us -> 0 us
  local copies, waits for them, and re-layouts: 110 us -> 35.8 us
  other arithmetic: 77.2 us -> 8.71 us
  loops' own time: 26.4 us -> 0 us
    reduce_scatter x10 -> x0, waiting for transfers between devices: 549 us -> none  [the longest x1 64.6 us: per_device(): lax.psum_scatter(columns_b[5].astype(jnp.bfloat16), 'inner', scatter_dime...]
    all_gather x14 -> x0, waiting for transfers between devices: 408 us -> none  [the longest x1 64.2 us: per_device(): lax.all_gather(rows_a[4], 'outer', axis=1, tiled=True)]
    pallas_call x0 -> x6, Pallas kernels: none -> 356 us  [the longest x1 154 us: scatter_all(): pl.pallas_call(functools.partial(scatter_kernel, n), out_shape=outs, in_s...]
    unnamed x36 -> x0, waiting for transfers between devices: 302 us -> none
    dot_general x219 -> x34, matrix products: 367 us -> 144 us  [product(): lax.dot_general(left, right, (((ca,), (cb,)), ((), ())), preferred_elemen...]
    unnamed x3 -> x0, blocking collectives: 71.9 us -> none
    all_gather x7 -> x0, blocking collectives: 71.6 us -> none  [the longest x1 27.3 us: per_device(): lax.all_gather(out_weight_a, 'inner', axis=0, tiled=True)]
    unnamed x126 -> x139, local copies, waits for them, and re-layouts: 59.4 us -> 28.2 us
  transfers between devices with their start and end apart: 30 -> 0, of which waited for: 25 -> 0; matrix products, arithmetic and copies ran while one was open for 26% -> 0% of each run, Pallas kernels for 0% -> 0%
where the time goes in v1:
time: 556 us; the launch traced here: 548 us
  Pallas kernels  356 us (64%)
  matrix products  144 us (26%)
  local copies, waits for them, and re-layouts  35.8 us (6%)
  other arithmetic  8.71 us (2%)
    pallas_call x1, Pallas kernels, scatter_all(): pl.pallas_call(functools.partial(scatter_kernel, n), out_shape=outs, in_s...  154 us
    dot_general x34, matrix products, product(): lax.dot_general(left, right, (((ca,), (cb,)), ((), ())), preferred_elemen...  144 us
    pallas_call x1, Pallas kernels, gather_all(): pl.pallas_call(functools.partial(gather_kernel, n), out_shape=outs, in_sp...  138 us
    pallas_call x2, Pallas kernels, attend_back(): pl.pallas_call(functools.partial(bwd_kernel, variant), grid=(6,), in_spec...  37.5 us
    unnamed x139, local copies, waits for them, and re-layouts  28.2 us
    pallas_call x2, Pallas kernels, attend(): pl.pallas_call(functools.partial(fwd_kernel, variant), grid=(6,), in_spec...  26.8 us

profile of v1, /device:TPU:0, one launch (start us, length us, event | category | flops | bytes accessed | tf_op | source)
XLA Modules:
  0.0 548.2 jit_solution(18425968489981333745)
XLA Ops:
  1.4 3.4 concatenate.15
  9.5 138.4 %gather_weights.1 = (bf16[768,2304]{1,0:T(8,128)(2,1)}, bf16[768,768]{1,0:T(8,128)(2,1)}, bf16[768,3072]{1,0:T(8,128)(2,1)}, bf16[3072,768]{1,0:T(8,128)(2,1)}, ...) custom-call(bf16[48,1152]{1,0:T(8,128)(2,1)} %refs_0_.1, ...), custom_call_target="tpu_custom_call" | custom-call | tf_op jit(solution)/shard_map/gather_weights/pallas_call | solution.py:347
  153.6 7.7 %attend_forward.2 = (bf16[512,768]{1,0:T(8,128)(2,1)S(1)}, f32[6,8,512]{2,1,0:T(8,128)S(1)}) custom-call(bf16[512,2304]{1,0:T(8,128)(2,1)S(1)} %convolution_convert_fusion.7.q_ref.k_ref.v_ref, bf16[512,2304]{1,0:T(8,128)(2,1)S(1)} %convolution_convert_fusion.7.q_ref.k_ref.v_ref, bf16[512,2304]{1,0:T(8,128)(2,1)S(1)} %convolution_convert_fusion.7.q_ref.k_ref.v_ref), custom_call_target="tpu_custom_call" | custom-call | tf_op jit(solution)/shard_map/attend_forward/pallas_call | solution.py:420
  165.1 3.7 convolution_add_fusion
  173.4 6.0 %convolution_convert_fusion.q_ref.k_ref.v_ref = bf16[1024,2304]{1,0:T(8,128)(2,1)} fusion(bf16[768,2304]{1,0:T(8,128)(2,1)S(1)} %copy-done.44, f32[1024,768]{0,1:T(8,128)S(1)} %get-tuple-element.143, f32[768]{0:T(1024)S(1)} %reshape.212, f32[1024]{0:T(1024)S(1)} %add_rsqrt_fusion.1), kind=kOutput, calls=%fused_computation.22 | convolution fusion | flops 3628597248 | bytes 11410432 | tf_op jit(solution)/shard_map/dot_general | solution.py:497
  179.5 19.0 %attend_forward.3 = (bf16[1024,768]{1,0:T(8,128)(2,1)S(1)}, f32[6,8,1024]{2,1,0:T(8,128)S(1)}) custom-call(bf16[1024,2304]{1,0:T(8,128)(2,1)} %convolution_convert_fusion.q_ref.k_ref.v_ref, bf16[1024,2304]{1,0:T(8,128)(2,1)} %convolution_convert_fusion.q_ref.k_ref.v_ref, bf16[1024,2304]{1,0:T(8,128)(2,1)} %convolution_convert_fusion.q_ref.k_ref.v_ref), custom_call_target="tpu_custom_call" | custom-call | tf_op jit(solution)/shard_map/attend_forward/pallas_call | solution.py:420
  198.5 3.4 multiply_reduce_fusion.4
  202.0 8.2 %fusion.54 = f32[1024,3072]{1,0:T(8,128)} fusion(bf16[768,3072]{1,0:T(8,128)(2,1)S(1)} %bitcast.83, f32[1024,768]{0,1:T(8,128)S(1)} %get-tuple-element.125, f32[768]{0:T(1024)S(1)} %reshape.213, f32[1024]{0:T(1024)S(1)} %add_rsqrt_fusion), kind=kOutput, calls=%fused_computation.138 | convolution fusion | flops 4834197504 | bytes 20454400 | tf_op jit(solution)/shard_map/dot_general | solution.py:497
  210.2 11.2 %fusion.31 = bf16[1,1024,768]{1,2,0:T(8,128)(2,1)} fusion(f32[1024,768]{0,1:T(8,128)S(1)} %get-tuple-element.143, f32[1024,768]{0,1:T(8,128)S(1)} %get-tuple-element.144, bf16[3072,768]{1,0:T(8,128)(2,1)} %get-tuple-element.65, f32[1024,3072]{1,0:T(8,128)} %fusion.54), kind=kOutput, calls=%fused_computation.85 | convolution fusion | flops 4862509056 | bytes 25165824 | tf_op jit(solution)/shard_map/dot_general | solution.py:497
  224.2 16.9 %fusion.6 = bf16[1024,3072]{1,0:T(8,128)(2,1)S(1)} fusion(f32[1024,3072]{1,0:T(8,128)} %fusion.54, bf16[3072,768]{1,0:T(8,128)(2,1)} %get-tuple-element.65, bf16[1,1024,768]{2,1,0:T(8,128)(2,1)} %param.20), kind=kOutput, calls=%fused_computation.8 | convolution fusion | flops 4891607040 | bytes 25165824 | tf_op jit(solution)/shard_map/dot_general | solution.py:497
  241.2 11.7 %convolution_convert_fusion.1.refs_8_ = bf16[3072,768]{1,0:T(8,128)(2,1)} fusion(bf16[1,1024,768]{2,1,0:T(8,128)(2,1)S(1)} %copy-done.23, f32[1024,3072]{1,0:T(8,128)} %fusion.54), kind=kOutput, calls=%fused_computation.23 | convolution fusion | flops 4862509056 | bytes 18874368 | tf_op jit(solution)/shard_map/dot_general | solution.py:497
  252.8 8.5 %multiply_reduce_fusion = (bf16[768]{0:T(1024)(128)(2,1)S(1)}, f32[1024]{0:T(1024)S(1)}, f32[1024,768]{0,1:T(8,128)}) fusion(f32[1024,768]{0,1:T(8,128)S(1)} %get-tuple-element.125, f32[1024]{0:T(1024)S(1)} %add_rsqrt_fusion, f32[768]{0:T(1024)S(1)} %reshape.213, bf16[1024,3072]{1,0:T(8,128)(2,1)S(1)} %fusion.6, bf16[768,3072]{1,0:T(8,128)(2,1)} %get-tuple-element.64), kind=kOutput, calls=%fused_computation.33 | convolution fusion | flops 4836554752 | bytes 17314304 | tf_op jit(solution)/shard_map/dot_general | solution.py:497
  261.3 7.4 %convolution_convert_fusion.2.refs_7_ = bf16[768,3072]{1,0:T(8,128)(2,1)} fusion(bf16[1024,3072]{1,0:T(8,128)(2,1)S(1)} %fusion.6, f32[1024,768]{0,1:T(8,128)S(1)} %get-tuple-element.125, f32[768]{0:T(1024)S(1)} %reshape.213, f32[1024]{0:T(1024)S(1)} %add_rsqrt_fusion), kind=kOutput, calls=%fused_computation.24 | convolution fusion | flops 4836556800 | bytes 14162944 | tf_op jit(solution)/shard_map/dot_general | solution.py:497
  268.8 3.3 fusion.14
  274.8 26.2 %attend_backward.2 = (bf16[1024,768]{1,0:T(8,128)(2,1)S(1)}, bf16[1024,768]{1,0:T(8,128)(2,1)S(1)}, bf16[1024,768]{1,0:T(8,128)(2,1)S(1)}) custom-call(bf16[1024,2304]{1,0:T(8,128)(2,1)} %convolution_convert_fusion.q_ref.k_ref.v_ref, bf16[1024,2304]{1,0:T(8,128)(2,1)} %convolution_convert_fusion.q_ref.k_ref.v_ref, ...), custom_call_target="tpu_custom_call" | custom-call | tf_op jit(solution)/shard_map/attend_backward/pallas_call | solution.py:480
  306.5 4.1 multiply_reduce_fusion.1
  310.6 5.5 convolution_convert_fusion.3.refs_5_
  319.2 4.2 fusion.23
  326.4 7.5 %fusion.13 = bf16[512,3072]{1,0:T(8,128)(2,1)S(1)} fusion(f32[512,3072]{1,0:T(8,128)S(1)} %bitcast.81, bf16[3072,768]{1,0:T(8,128)(2,1)S(1)} %bitcast.97, f32[512,768]{1,0:T(8,128)S(1)} %add_add_fusion.1, f32[512]{0:T(512)S(1)} %get-tuple-element.150), kind=kOutput, calls=%fused_computation.19 | convolution fusion | flops 2446589952 | bytes 15730688 | tf_op jit(solution)/shard_map/dot_general | solution.py:497
  336.9 5.1 convolution_convert_fusion.4.refs_3_
  344.5 11.3 %attend_backward.3 = (bf16[512,768]{1,0:T(8,128)(2,1)S(1)}, bf16[512,768]{1,0:T(8,128)(2,1)S(1)}, bf16[512,768]{1,0:T(8,128)(2,1)S(1)}) custom-call(bf16[512,2304]{1,0:T(8,128)(2,1)} %copy-done, bf16[512,2304]{1,0:T(8,128)(2,1)} %copy-done, bf16[512,2304]{1,0:T(8,128)(2,1)} %copy-done, bf16[512,768]{1,0:T(8,128)(2,1)S(1)} %copy-done.4, ...), custom_call_target="tpu_custom_call" | custom-call | tf_op jit(solution)/shard_map/attend_backward/pallas_call | solution.py:480
  363.6 3.9 convolution_convert_fusion.6.refs_0_
  367.5 4.6 convolution_convert_fusion.5.refs_2_
  373.1 153.7 %scatter_gradients.1 = (f32[48,1152]{1,0:T(8,128)}, f32[48,384]{1,0:T(8,128)}, f32[48,1536]{1,0:T(8,128)}, f32[192,384]{1,0:T(8,128)}, f32[16,128]{1,0:T(8,128)}...) custom-call(bf16[768,2304]{1,0:T(8,128)(2,1)} %convolution_convert_fusion.6.refs_0_, ...), custom_call_target="tpu_custom_call" | custom-call | tf_op jit(solution)/shard_map/scatter_gradients/pallas_call | solution.py:177
  (196 shorter events, 70.0 us)
Async XLA Ops:
  0.6 8.1 %copy-start.22 = (bf16[1,1024,768]{2,1,0:T(8,128)(2,1)S(1)}, bf16[1,1024,768]{2,1,0:T(8,128)(2,1)}, u32[]{:S(2)}) copy-start(bf16[1,1024,768]{2,1,0:T(8,128)(2,1)} %param.19) | copy-start | bytes 4718596
  149.2 13.1 %copy-start.29 = (f32[768]{0:T(1024)}, f32[768]{0:T(1024)S(1)}, u32[]{:S(2)}) copy-start(f32[768]{0:T(1024)S(1)} %reshape.211) | copy-start | bytes 9220
  150.7 10.7 %copy-start.15 = (f32[512,768]{1,0:T(8,128)}, f32[512,768]{1,0:T(8,128)S(1)}, u32[]{:S(2)}) copy-start(f32[512,768]{1,0:T(8,128)S(1)} %get-tuple-element.140) | copy-start | bytes 4718596
  151.5 10.8 %slice-start.4 = ((s8[4718592]{0:T(1024)(128)(4,1)}), s8[4194304]{0:T(1024)(128)(4,1)S(1)}, s32[]{:S(2)}) async-start(s8[4718592]{0:T(1024)(128)(4,1)} %bitcast.84), calls=%async_computation.4 | async-start | bytes 8388608
  153.6 7.8 %copy-start = (bf16[512,2304]{1,0:T(8,128)(2,1)}, bf16[512,2304]{1,0:T(8,128)(2,1)S(1)}, u32[]{:S(2)}) copy-start(bf16[512,2304]{1,0:T(8,128)(2,1)S(1)} %convolution_convert_fusion.7.q_ref.k_ref.v_ref) | copy-start | bytes 7077892
  153.6 7.8 %copy-start.24 = (bf16[768,768]{1,0:T(8,128)(2,1)S(1)}, bf16[768,768]{1,0:T(8,128)(2,1)}, u32[]{:S(2)}) copy-start(bf16[768,768]{1,0:T(8,128)(2,1)} %get-tuple-element.58) | copy-start | bytes 3538948
  153.6 8.7 %slice-start.5 = ((s8[4718592]{0:T(1024)(128)(4,1)}), s8[524288]{0:T(1024)(128)(4,1)S(1)}, s32[]{:S(2)}) async-start(s8[4718592]{0:T(1024)(128)(4,1)} %bitcast.84), calls=%async_computation.5 | async-start | bytes 1048576
  173.0 37.2 %copy-start.5 = (f32[1024,768]{0,1:T(8,128)}, f32[1024,768]{0,1:T(8,128)S(1)}, u32[]{:S(2)}) copy-start(f32[1024,768]{0,1:T(8,128)S(1)} %get-tuple-element.143) | copy-start | bytes 9437188
  173.4 28.5 %slice-start.2 = ((s8[4718592]{0:T(1024)(128)(4,1)}), s8[4194304]{0:T(1024)(128)(4,1)S(1)}, s32[]{:S(2)}) async-start(s8[4718592]{0:T(1024)(128)(4,1)} %bitcast.82), calls=%async_computation.2 | async-start | bytes 8388608
  179.5 22.5 %slice-start.3 = ((s8[4718592]{0:T(1024)(128)(4,1)}), s8[524288]{0:T(1024)(128)(4,1)S(1)}, s32[]{:S(2)}) async-start(s8[4718592]{0:T(1024)(128)(4,1)} %bitcast.82), calls=%async_computation.3 | async-start | bytes 1048576
  224.2 17.0 %copy-start.23 = (bf16[1,1024,768]{2,1,0:T(8,128)(2,1)S(1)}, bf16[1,1024,768]{2,1,0:T(8,128)(2,1)}, u32[]{:S(2)}) copy-start(bf16[1,1024,768]{2,1,0:T(8,128)(2,1)} %param.20) | copy-start | bytes 4718596
  274.8 26.3 %copy-start.2 = (bf16[1024,768]{1,0:T(8,128)(2,1)S(1)}, bf16[1024,768]{1,0:T(8,128)(2,1)}, u32[]{:S(2)}) copy-start(bf16[1024,768]{1,0:T(8,128)(2,1)} %copy-done.1) | copy-start | bytes 4718596
  310.6 5.5 %copy-start.12 = (bf16[1,1024,768]{1,2,0:T(8,128)(2,1)S(1)}, bf16[1,1024,768]{1,2,0:T(8,128)(2,1)}, u32[]{:S(2)}) copy-start(bf16[1,1024,768]{1,2,0:T(8,128)(2,1)} %copy.48) | copy-start | bytes 4718596
  319.2 6.5 %slice-start = ((s8[6291456]{0:T(1024)(128)(4,1)}), s8[4194304]{0:T(1024)(128)(4,1)S(1)}, s32[]{:S(2)}) async-start(s8[6291456]{0:T(1024)(128)(4,1)} %bitcast.80), calls=%async_computation | async-start | bytes 8388608
  319.2 6.5 %slice-start.10 = ((s8[4718592]{0:T(1024)(128)(4,1)}), s8[4194304]{0:T(1024)(128)(4,1)S(1)}, s32[]{:S(2)}) async-start(s8[4718592]{0:T(1024)(128)(4,1)} %bitcast.96), calls=%async_computation.10 | async-start | bytes 8388608
  324.6 9.3 %slice-start.6 = ((s8[4718592]{0:T(1024)(128)(4,1)}), s8[4194304]{0:T(1024)(128)(4,1)S(1)}, s32[]{:S(2)}) async-start(s8[4718592]{0:T(1024)(128)(4,1)} %bitcast.86), calls=%async_computation.6 | async-start | bytes 8388608
  326.4 7.6 %copy-start.10 = (f32[512,768]{1,0:T(8,128)S(1)}, f32[512,768]{1,0:T(8,128)}, u32[]{:S(2)}) copy-start(f32[512,768]{1,0:T(8,128)} %copy-done.9) | copy-start | bytes 4718596
  326.4 7.6 %slice-start.7 = ((s8[4718592]{0:T(1024)(128)(4,1)}), s8[524288]{0:T(1024)(128)(4,1)S(1)}, s32[]{:S(2)}) async-start(s8[4718592]{0:T(1024)(128)(4,1)} %bitcast.86), calls=%async_computation.7 | async-start | bytes 1048576
  326.4 7.6 %copy-start.30 = (f32[768]{0:T(1024)S(1)}, f32[768]{0:T(1024)}, u32[]{:S(2)}) copy-start(f32[768]{0:T(1024)} %copy-done.29) | copy-start | bytes 9220
  326.4 7.6 %copy-start.33 = (f32[512]{0:T(512)S(1)}, f32[512]{0:T(512)}, u32[]{:S(2)}) copy-start(f32[512]{0:T(512)} %copy-done.32) | copy-start | bytes 6148
  344.5 11.3 %copy-start.39 = (f32[512]{0:T(512)S(1)}, f32[512]{0:T(512)}, u32[]{:S(2)}) copy-start(f32[512]{0:T(512)} %copy-done.38) | copy-start | bytes 6148
  363.6 165.9 %copy-start.19 = (f32[512,768]{1,0:T(8,128)}, f32[512,768]{1,0:T(8,128)S(1)}, u32[]{:S(2)}) copy-start(f32[512,768]{1,0:T(8,128)S(1)} %multiply_add_fusion.2) | copy-start | bytes 4718596
  534.1 10.6 %copy-start.31 = (f32[48,384]{1,0:T(8,128)S(1)}, f32[48,384]{1,0:T(8,128)}, u32[]{:S(2)}) copy-start(f32[48,384]{1,0:T(8,128)} %get-tuple-element.177) | copy-start | bytes 221188
  534.1 12.9 %copy-start.28 = (f32[192,384]{1,0:T(8,128)S(1)}, f32[192,384]{1,0:T(8,128)}, u32[]{:S(2)}) copy-start(f32[192,384]{1,0:T(8,128)} %get-tuple-element.180) | copy-start | bytes 884740
  (36 other events, 101.6 us)

commit v2 on v1

v2 whole, which is shorter than its diff:
```python
import functools

import jax
import jax.numpy as jnp
from jax import lax
from jax.experimental import pallas as pl
from jax.experimental.pallas import tpu as pltpu
from jax.sharding import PartitionSpec as P

MESH = pl.DeviceIdType.MESH


def place():
    o, i = lax.axis_index("outer"), lax.axis_index("inner")
    return o, i // 4, (i // 2) % 2, i % 2


def device(o, z, x, c):
    return (o, z * 4 + x * 2 + c)


def greet(o, z, x, c):
    barrier = pltpu.get_barrier_semaphore()
    signal = functools.partial(pl.semaphore_signal, barrier, inc=1, device_id_type=MESH)
    signal(device_id=device(1 - o, z, x, c))
    signal(device_id=device(o, z, 1 - x, c))
    signal(device_id=device(o, z, x, 1 - c))

    @pl.when(z > 0)
    def _():
        signal(device_id=device(o, z - 1, x, c))

    @pl.when(z < 3)
    def _():
        signal(device_id=device(o, z + 1, x, c))

    pl.semaphore_wait(barrier, 3 + jnp.where(z > 0, 1, 0) + jnp.where(z < 3, 1, 0))


def scatter_kernel(n, *refs):
    grads, outs = refs[:n], refs[n:2 * n]
    rest = refs[2 * n:]
    own, got_c, got_b, got_a, got_z = (rest[j * n:(j + 1) * n] for j in range(5))
    local_sem, send_sem, recv_sem = rest[5 * n:]
    o, z, x, c = place()
    greet(o, z, x, c)

    def block(p, s, cc):
        r, w = outs[p].shape
        bs, as_, k = s // 8, (s // 4) % 2, s % 4
        if p % 2 == 0:
            co, cx = jnp.where(bs == 1, o, 1 - o), jnp.where(as_ == 1, x, 1 - x)
        else:
            cx, co = jnp.where(bs == 1, x, 1 - x), jnp.where(as_ == 1, o, 1 - o)
        row = pl.multiple_of((k * 4 + cx * 2 + cc) * r, 16)
        col = pl.multiple_of(co * w, 128)
        return grads[p].at[pl.ds(row, r), pl.ds(col, w)]

    def a_dev(p):
        return device(o, z, 1 - x, c) if p % 2 == 0 else device(1 - o, z, x, c)

    def b_dev(p):
        return device(1 - o, z, x, c) if p % 2 == 0 else device(o, z, 1 - x, c)

    def send(p, src, dst, kind, rslot, target):
        return pltpu.make_async_remote_copy(
            src_ref=src, dst_ref=dst, send_sem=send_sem.at[p, kind], recv_sem=recv_sem.at[p, rslot],
            device_id=target, device_id_type=MESH)

    def wait(ref, sem):
        pltpu.make_async_copy(ref, ref, sem).wait()

    def loop(count, body):
        def step(s, carry):
            body(s)
            return carry
        lax.fori_loop(0, count, step, 0)

    def begin(p):
        def body(s):
            send(p, block(p, s, 1 - c), got_c[p].at[s], 0, s, device(o, z, x, 1 - c)).start()
            pltpu.make_async_copy(block(p, s, c), own[p].at[s], local_sem.at[p]).start()
        loop(16, body)

    def core_stage(p):
        wait(own[p], local_sem.at[p])

        def body(s):
            wait(got_c[p].at[s], recv_sem.at[p, s])
            own[p][s] = own[p][s] + got_c[p][s]

            @pl.when(s < 8)
            def _():
                send(p, own[p].at[s], got_b[p].at[s], 1, 16 + s, b_dev(p)).start()
        loop(16, body)

    def b_stage(p):
        def body(j):
            wait(got_b[p].at[j], recv_sem.at[p, 16 + j])
            own[p][8 + j] = own[p][8 + j] + got_b[p][j]

            @pl.when(j < 4)
            def _():
                send(p, own[p].at[8 + j], got_a[p].at[j], 2, 24 + j, a_dev(p)).start()
        loop(8, body)

    def send_z(p, k, step):
        t = z + step
        slot = jnp.where(k == t, jnp.where(step > 0, k, 4), k)
        send(p, own[p].at[12 + k], got_z[p].at[slot], 3, 28 + slot, device(o, t, x, c)).start()

    def a_stage(p):
        def body(k):
            wait(got_a[p].at[k], recv_sem.at[p, 24 + k])
            own[p][12 + k] = own[p][12 + k] + got_a[p][k]
        loop(4, body)

        @pl.when(z == 0)
        def _():
            for k in (3, 2, 1):
                send_z(p, k, 1)

        @pl.when(z == 3)
        def _():
            for k in (0, 1, 2):
                send_z(p, k, -1)

    def pass_on(p, k, step):
        wait(got_z[p].at[k], recv_sem.at[p, 28 + k])
        own[p][12 + k] = own[p][12 + k] + got_z[p][k]
        send_z(p, k, step)

    def z_stage(p, level):
        @pl.when(z == level)
        def _():
            for k in range(3, level, -1):
                pass_on(p, k, 1)

        @pl.when(z == 3 - level)
        def _():
            for k in range(0, 3 - level):
                pass_on(p, k, -1)

    def last(p):
        outs[p][...] = own[p][12 + z].astype(jnp.float32)

        @pl.when(z > 0)
        def _():
            wait(got_z[p].at[z], recv_sem.at[p, 28 + z])
            outs[p][...] += got_z[p][z].astype(jnp.float32)

        @pl.when(z < 3)
        def _():
            wait(got_z[p].at[4], recv_sem.at[p, 32])
            outs[p][...] += got_z[p][4].astype(jnp.float32)

        wait(own[p], send_sem.at[p, 0])
        wait(got_b[p], send_sem.at[p, 1])
        wait(got_a[p], send_sem.at[p, 2])
        wait(got_a[p].at[pl.ds(0, 3)], send_sem.at[p, 3])

    for p in range(n):
        begin(p)
    stages = [core_stage, b_stage, a_stage, lambda p: z_stage(p, 1), lambda p: z_stage(p, 2), last]
    for t in range(n + len(stages) - 1):
        for lag, stage in enumerate(stages):
            if 0 <= t - lag < n:
                stage(t - lag)


def scatter_all(grads, outer, inner, collective_id=1):
    n = len(grads)
    outs = [jax.ShapeDtypeStruct((g.shape[0] // inner, g.shape[1] // outer), jnp.float32) for g in grads]
    bufs = [pltpu.VMEM((m,) + s.shape, jnp.bfloat16) for m in (16, 16, 8, 4, 5) for s in outs]
    return pl.pallas_call(
        functools.partial(scatter_kernel, n),
        out_shape=outs,
        in_specs=[pl.BlockSpec(memory_space=pl.ANY)] * n,
        out_specs=[pl.BlockSpec(memory_space=pltpu.VMEM)] * n,
        scratch_shapes=bufs + [pltpu.SemaphoreType.DMA((n,)), pltpu.SemaphoreType.DMA((n, 4)), pltpu.SemaphoreType.DMA((n, 33))],
        compiler_params=pltpu.CompilerParams(collective_id=collective_id, has_side_effects=True, vmem_limit_bytes=60 * 2**20),
        name="scatter_gradients",
    )(*grads)


def gather_kernel(n, *refs):
    shards, outs = refs[:n], refs[n:2 * n]
    local_sem, send_sem, recv_sem = refs[2 * n:]
    o, z, x, c = place()

    greet(o, z, x, c)

    def block(p, co, cz, cx, cc):
        r, w = shards[p].shape
        row = pl.multiple_of((cz * 4 + cx * 2 + cc) * r, 16)
        col = pl.multiple_of(co * w, 128)
        return outs[p].at[pl.ds(row, r), pl.ds(col, w)]

    def send(p, src, dst, slot, rslot, target):
        return pltpu.make_async_remote_copy(
            src_ref=src, dst_ref=dst, send_sem=send_sem.at[p, slot], recv_sem=recv_sem.at[p, rslot],
            device_id=target, device_id_type=MESH)

    def up(p, k, src=None):
        b = block(p, o, k, x, c)
        return send(p, b if src is None else src, b, k, k, device(o, z + 1, x, c))

    def down(p, k, src=None):
        b = block(p, o, k, x, c)
        return send(p, b if src is None else src, b, 4 + k, k, device(o, z - 1, x, c))

    def first(p, k, src=None):
        b = block(p, o, k, x, c)
        t = device(o, z, 1 - x, c) if p % 2 == 0 else device(1 - o, z, x, c)
        return send(p, b if src is None else src, b, 8 + k, 4 + k, t)

    def second(p, k, a, src=None):
        if p % 2 == 0:
            b, t = block(p, o, k, a, c), device(1 - o, z, x, c)
        else:
            b, t = block(p, a, k, x, c), device(o, z, 1 - x, c)
        return send(p, b if src is None else src, b, 12 + 2 * k + a, 8 + 2 * k + a, t)

    def core(p, co, k, cx, src=None):
        b = block(p, co, k, cx, c)
        s = k * 4 + co * 2 + cx
        return send(p, b if src is None else src, b, 20 + s, 16 + s, device(o, z, x, 1 - c))

    def mine(p):
        return x if p % 2 == 0 else o

    def coords(p, k, a, b):
        return (b, k, a) if p % 2 == 0 else (a, k, b)

    def core_ab(p, k, a, b, src=None):
        co, ck, cx = coords(p, k, a, b)
        return core(p, co, ck, cx, src)

    def other(p):
        return o if p % 2 == 0 else x

    def own(p):
        s = shards[p]
        pltpu.make_async_copy(s, block(p, o, z, x, c), local_sem.at[p]).start()

        @pl.when(z < 3)
        def _():
            up(p, z, s).start()

        @pl.when(z > 0)
        def _():
            down(p, z, s).start()

        first(p, z, s).start()
        second(p, z, mine(p), s).start()
        core(p, o, z, x, s).start()

    def wait_block(p, rslot):
        b = block(p, o, z, x, c)
        pltpu.make_async_copy(shards[p], b, recv_sem.at[p, rslot]).wait()

    def z_phase(p):
        for d in range(1, 4):
            @pl.when(z >= d)
            def _():
                k = z - d
                wait_block(p, k)

                @pl.when(z < 3)
                def _():
                    up(p, k).start()

                first(p, k).start()
                second(p, k, mine(p)).start()
                core(p, o, k, x).start()

            @pl.when(z + d <= 3)
            def _():
                k = z + d
                wait_block(p, k)

                @pl.when(z > 0)
                def _():
                    down(p, k).start()

                first(p, k).start()
                second(p, k, mine(p)).start()
                core(p, o, k, x).start()

    def ks():
        return [(z + d) % 4 for d in range(4)]

    def a_phase(p):
        for k in ks():
            wait_block(p, 4 + k)
            a = 1 - mine(p)
            second(p, k, a).start()
            core_ab(p, k, a, other(p)).start()

    def b_phase(p):
        for k in ks():
            for a in (mine(p), 1 - mine(p)):
                wait_block(p, 8 + 2 * k + a)
                core_ab(p, k, a, 1 - other(p)).start()

    def c_phase(p):
        for s in range(16):
            wait_block(p, 16 + s)

    def ends(p):
        pltpu.make_async_copy(shards[p], block(p, o, z, x, c), local_sem.at[p]).wait()

        def done(slot):
            pltpu.make_async_copy(shards[p], block(p, o, z, x, c), send_sem.at[p, slot]).wait()

        for k in range(4):
            @pl.when(jnp.logical_and(z < 3, k <= z))
            def _():
                done(k)

            @pl.when(jnp.logical_and(z > 0, k >= z))
            def _():
                done(4 + k)
        for slot in range(8, 36):
            done(slot)

    own(0)
    for t in range(n + 3):
        if t + 1 < n:
            own(t + 1)
        if t < n:
            z_phase(t)
        if 0 <= t - 1 < n:
            a_phase(t - 1)
        if 0 <= t - 2 < n:
            b_phase(t - 2)
    for p in range(n):
        c_phase(p)
        ends(p)


def gather_all(shards, outer, inner, collective_id=0):
    n = len(shards)
    outs = [jax.ShapeDtypeStruct((s.shape[0] * inner, s.shape[1] * outer), s.dtype) for s in shards]
    return pl.pallas_call(
        functools.partial(gather_kernel, n),
        out_shape=outs,
        in_specs=[pl.BlockSpec(memory_space=pl.ANY)] * n,
        out_specs=[pl.BlockSpec(memory_space=pl.ANY)] * n,
        scratch_shapes=[pltpu.SemaphoreType.DMA((n,)), pltpu.SemaphoreType.DMA((n, 36)), pltpu.SemaphoreType.DMA((n, 32))],
        compiler_params=pltpu.CompilerParams(collective_id=collective_id, has_side_effects=True),
        name="gather_weights",
    )(*shards)


D = 768
SCALE = 0.125 * 1.4426950408889634
ROWS = 256
VMEM_BYTES = 63 * 2**20


def mul(a, b, ca=1, cb=0):
    return lax.dot_general(a, b, (((ca,), (cb,)), ((), ())), preferred_element_type=jnp.float32)


def low(v):
    return v.astype(jnp.bfloat16)


def cols(j):
    return pl.ds(pl.multiple_of(j * D, D), D)


def rms_scale(v):
    return lax.rsqrt(jnp.mean(v * v, axis=-1, keepdims=True) + 1e-06)


def rms_back(v, gain, grad):
    r = rms_scale(v)
    unit = v * r
    scaled = grad * gain
    back = r * (scaled - unit * jnp.mean(scaled * unit, axis=-1, keepdims=True))
    return back, jnp.sum((grad * unit).reshape(-1, 8, v.shape[-1]), axis=0)


def gelu_and_slope(u):
    k = 0.7978845608028654
    square = u * u
    t = jnp.tanh(u * (k + k * 0.044715 * square))
    half = 0.5 + 0.5 * t
    return u * half, half + u * (0.5 - 0.5 * t * t) * (k + 3 * 0.044715 * k * square)


def halves(v):
    lane = lax.broadcasted_iota(jnp.int32, v.shape, 1)
    zero = jnp.zeros_like(v)
    return jnp.where(lane < 64, v, zero), jnp.where(lane < 64, zero, v)


def two(v):
    first = low(v)
    return first, low(v - first.astype(jnp.float32))


class Block:
    def __init__(self, rows, refs):
        self.rows = rows
        self.__dict__.update(refs)

    @staticmethod
    def scratch(rows):
        f32, b16 = jnp.float32, jnp.bfloat16
        return dict(
            branch=((rows, D), f32), projected=((rows, 3 * D), b16), merged=((rows, D), b16), lse=((6, 8, rows), f32),
            active=((rows, 4 * D), b16), slope=((rows, 4 * D), b16), normed=((rows, D), b16), normed_mlp=((rows, D), b16))

    def tiles(self):
        return [slice(i, i + ROWS) for i in range(0, self.rows, ROWS)]

    def norm(self):
        for t in self.tiles():
            x = self.x[t]
            self.normed[t] = low(x * rms_scale(x) * self.gain_attn[...])

    def project(self, j):
        c = cols(j)
        self.projected[:, c] = low(mul(self.normed[...], self.qkv[:, c]))

    def pair(self, ref, part, pair, rows=slice(None)):
        return ref[rows, pl.ds(pl.multiple_of(part * D + pair * 128, 128), 128)]

    def attend(self, pair):
        v0, v1 = halves(self.pair(self.projected, 2, pair))
        causal = lax.broadcasted_iota(jnp.int32, (ROWS, ROWS), 1) >= lax.broadcasted_iota(jnp.int32, (ROWS, ROWS), 0)
        for t in self.tiles():
            n = t.stop
            qs = halves(self.pair(self.projected, 0, pair, t))
            k = self.pair(self.projected, 1, pair, slice(0, n))
            total = None
            for h in range(2):
                s = mul(k, qs[h], 1, 1)
                last = jnp.where(causal, s[t.start:], -1e30)
                s = last if t.start == 0 else jnp.concatenate([s[: t.start], last], axis=0)
                m = jnp.max(s, axis=0, keepdims=True) * SCALE
                p = jnp.exp2(s * SCALE - m)
                l = jnp.sum(p, axis=0, keepdims=True)
                self.lse[pair, h : h + 1, t] = m + jnp.log2(l)
                o = mul(low(p * (1.0 / l)), (v0, v1)[h][:n], 0, 0)
                total = o if total is None else total + o
            self.merged[t, pl.ds(pl.multiple_of(pair * 128, 128), 128)] = low(total)

    def join(self):
        for t in self.tiles():
            branch = mul(self.merged[t], self.out[...])
            self.branch[t] = branch
            middle = self.x[t] + branch
            self.normed_mlp[t] = low(middle * rms_scale(middle) * self.gain_mlp[...])

    def widen(self, j):
        c = cols(j)
        for t in self.tiles():
            active, slope = gelu_and_slope(mul(self.normed_mlp[t], self.up[:, c]))
            self.active[t, c] = low(active)
            self.slope[t, c] = low(slope)

    def narrow(self, t):
        return mul(self.active[t], self.down[...])

    def back_wide(self, j):
        c = cols(j)
        for t in self.tiles():
            grad = mul(self.grad_low[t], self.down[c, :], 1, 1)
            self.slope[t, c] = low(grad * self.slope[t, c].astype(jnp.float32))

    def grad_down(self, j):
        return low(mul(self.active[:, cols(j)], self.grad_low[...], 0, 0))

    def grad_up(self, j):
        return low(mul(self.normed_mlp[...], self.slope[:, cols(j)], 0, 0))

    def back_mlp(self, grad_of):
        total = jnp.zeros((8, D), jnp.float32)
        for t in self.tiles():
            grad = mul(self.slope[t], self.up[...], 1, 1)
            back, gain = rms_back(self.x[t] + self.branch[t], self.gain_mlp[...], grad)
            total = total + gain
            self.branch[t] = back
            self.normed_mlp[t] = low(grad_of(t) + back)
        return jnp.sum(total, axis=0, keepdims=True)

    def grad_out(self):
        return low(mul(self.merged[...], self.normed_mlp[...], 0, 0))

    def back_merged(self):
        self.active[:, :D] = low(mul(self.normed_mlp[...], self.out[...], 1, 1))

    def attend_back(self, pair, turned):
        rows = self.rows
        q, do = self.pair(self.projected, 0, pair), self.pair(self.active, 0, pair)
        qs, dos = halves(q), halves(do)
        dd = do.astype(jnp.float32) * self.pair(self.merged, 0, pair).astype(jnp.float32)
        pick = lax.broadcasted_iota(jnp.int32, (8, 128), 0) == lax.broadcasted_iota(jnp.int32, (8, 128), 1) // 64
        delta = lax.dot_general(pick.astype(jnp.float32), dd, (((1,), (1,)), ((), ())), precision=lax.Precision.HIGHEST,
                                preferred_element_type=jnp.float32)
        causal = lax.broadcasted_iota(jnp.int32, (ROWS, ROWS), 1) >= lax.broadcasted_iota(jnp.int32, (ROWS, ROWS), 0)
        for t in self.tiles():
            a = t.start
            ks, vs = halves(self.pair(self.projected, 1, pair, t)), halves(self.pair(self.projected, 2, pair, t))
            dk = dv = dq = 0.0
            for h in range(2):
                s = mul(ks[h], q[a:], 1, 1)
                p = jnp.exp2(s * SCALE - self.lse[pair, h : h + 1, a:])
                first = jnp.where(causal, p[:, :ROWS], 0.0)
                p = first if t.stop == rows else jnp.concatenate([first, p[:, ROWS:]], axis=1)
                dp = mul(vs[h], do[a:], 1, 1)
                ds = low(p * (dp - delta[h : h + 1, a:]))
                dv = dv + mul(low(p), dos[h][a:])
                dk = dk + mul(ds, qs[h][a:])
                dq = dq + mul(ks[h], ds, 0, 0)
            lanes = pl.multiple_of(pair * 128, 128)
            self.projected[t, pl.ds(D + lanes, 128)] = low(0.125 * dk)
            self.projected[t, pl.ds(2 * D + lanes, 128)] = low(dv)
            if a == 0:
                turned[:, :rows] = dq
            else:
                turned[:, a:rows] += dq
        self.projected[:, pl.ds(lanes, 128)] = low(0.125 * turned[:, :rows].T)

    def grad_qkv(self, j):
        return low(mul(self.normed[...], self.projected[:, cols(j)], 0, 0))

    def back_norm(self, finish):
        total = jnp.zeros((8, D), jnp.float32)
        for t in self.tiles():
            grad = mul(self.projected[t], self.qkv[...], 1, 1)
            back, gain = rms_back(self.x[t], self.gain_attn[...], grad)
            total = total + gain
            finish(t, back + self.branch[t])
        return jnp.sum(total, axis=0, keepdims=True)


SAVED = ("branch", "projected", "merged", "lse", "active", "slope", "normed", "normed_mlp")


def run(steps, hooks=None):
    at = 0
    for count, body in steps:
        if count == 0:
            body(0)
            continue
        after = [hooks[at + k] if hooks else [] for k in range(count)]
        at += count
        if count == 1:
            body(0)
            for f in after[0]:
                f()
            continue

        @pl.loop(0, count)
        def _(j):
            body(j)
            for k in range(count):
                if after[k]:
                    @pl.when(j == k)
                    def _():
                        for f in after[k]:
                            f()


class Loads:
    def __init__(self, pairs, sems):
        self.copies = {k: pltpu.make_async_copy(a, b, sems.at[j]) for j, (k, a, b) in enumerate(pairs)}
        for c in self.copies.values():
            c.start()

    def need(self, *names):
        for n in names:
            self.copies[n].wait()


class Ship:
    def __init__(self, stage, sems):
        self.stage, self.sems = stage, sems

    def wait(self, slot):
        pltpu.make_async_copy(self.stage.at[slot], self.stage.at[slot], self.sems.at[slot]).wait()

    def send(self, slot, value, target, busy):
        if busy is True:
            self.wait(slot)
        elif busy is not False:
            pl.when(busy)(lambda: self.wait(slot))
        self.stage[slot] = value
        pltpu.make_async_copy(self.stage.at[slot], target, self.sems.at[slot]).start()


def backward_steps(b, grad_of, ship, targets, vec, finish, turned):
    gqkv, gout, gup, gdown = targets

    def wide(j):
        b.back_wide(j)
        ship.send(0, b.grad_down(j), gdown.at[cols(j), :], j > 0)
        ship.send(1, b.grad_up(j), gup.at[:, cols(j)], j > 0)

    def mlp(_):
        vec(1, b.back_mlp(grad_of))

    def out(_):
        ship.send(0, b.grad_out(), gout, True)
        b.back_merged()

    def qkv(j):
        @pl.when(j == 0)
        def _():
            ship.wait(0)
        ship.send(1, b.grad_qkv(j), gqkv.at[:, cols(j)], True)

    def norm(_):
        vec(0, b.back_norm(finish))
        ship.wait(1)

    return [(4, wide), (1, mlp), (1, out), (6, lambda j: b.attend_back(j, turned)), (3, qkv), (1, norm)]


def dense_kernel(x_hbm, cot_hbm, vec_ref, qkv_hbm, out_hbm, up_hbm, down_hbm,
                 y_hbm, grad_hbm, gvec_ref, gqkv_hbm, gout_hbm, gup_hbm, gdown_hbm,
                 x, cot, qkv, out, up, down, y, turned, stage, load_sem, stage_sem, row_sem, *kept):
    loads = Loads((("x", x_hbm, x), ("qkv", qkv_hbm, qkv), ("out", out_hbm, out), ("up", up_hbm, up),
                   ("down", down_hbm, down), ("cot", cot_hbm, cot)), load_sem)
    b = Block(x.shape[0], dict(zip(SAVED, kept), x=x, grad_low=cot, qkv=qkv, out=out, up=up, down=down,
                               gain_attn=vec_ref.at[3:4], gain_mlp=vec_ref.at[4:5]))

    def norm(_):
        loads.need("x")
        b.norm()
        loads.need("qkv")

    def join(_):
        loads.need("out")
        b.join()
        loads.need("up")

    def narrow(_):
        loads.need("down", "cot")
        for t in b.tiles():
            y[t] = low(x[t] + b.branch[t] + b.narrow(t))
        pltpu.make_async_copy(y, y_hbm, row_sem.at[0]).start()

    def vec(j, value):
        gvec_ref[j : j + 1] = value

    def finish(t, grad):
        x[t] = grad + cot[t].astype(jnp.float32)
        pltpu.make_async_copy(x.at[t], grad_hbm.at[t], row_sem.at[1]).start()

    run([(1, norm), (3, b.project), (6, b.attend), (1, join), (4, b.widen), (1, narrow)]
        + backward_steps(b, lambda t: cot[t].astype(jnp.float32), Ship(stage, stage_sem),
                         (gqkv_hbm, gout_hbm, gup_hbm, gdown_hbm), vec, finish, turned))
    pltpu.make_async_copy(y, y_hbm, row_sem.at[0]).wait()
    pltpu.make_async_copy(x, grad_hbm, row_sem.at[1]).wait()


def shape(*dims, dtype=jnp.bfloat16):
    return jax.ShapeDtypeStruct(dims, dtype)


def any_specs(n):
    return [pl.BlockSpec(memory_space=pl.ANY)] * n


def vmem_specs(n):
    return [pl.BlockSpec(memory_space=pltpu.VMEM)] * n


WEIGHTS = [((D, 3 * D), jnp.bfloat16), ((D, D), jnp.bfloat16), ((D, 4 * D), jnp.bfloat16), ((4 * D, D), jnp.bfloat16)]


def buffers(*pairs):
    return [pltpu.VMEM(dims, dtype) for dims, dtype in pairs]


def kept_buffers(rows):
    s = Block.scratch(rows)
    return [s[k] for k in SAVED]


def dense_block(x, cot, vec, weights):
    rows = x.shape[0]
    f32, b16 = jnp.float32, jnp.bfloat16
    return pl.pallas_call(
        dense_kernel,
        in_specs=any_specs(2) + vmem_specs(1) + any_specs(4),
        out_specs=any_specs(2) + vmem_specs(1) + any_specs(4),
        out_shape=[shape(rows, D), shape(rows, D, dtype=f32), shape(2, D, dtype=f32)] + [shape(*s) for s, _ in WEIGHTS],
        scratch_shapes=buffers(((rows, D), f32), ((rows, D), b16), *WEIGHTS, ((rows, D), b16), ((128, rows), f32), ((2, D, D), b16))
        + [pltpu.SemaphoreType.DMA((6,)), pltpu.SemaphoreType.DMA((2,)), pltpu.SemaphoreType.DMA((2,))]
        + buffers(*kept_buffers(rows)),
        compiler_params=pltpu.CompilerParams(vmem_limit_bytes=VMEM_BYTES),
        name="dense_block",
    )(x, cot, vec, *weights)


def spots(length, spot_ref):
    at = lax.broadcasted_iota(jnp.int32, (length, spot_ref.shape[1]), 0)
    return low(jnp.where(at == spot_ref[...], 1.0, 0.0))


def lane_map(outer, inner):
    each = D // (outer * inner)
    d = jnp.arange(D, dtype=jnp.int32)
    return jnp.stack([d // each % inner, d // (each * inner) * 128 + d % each])


def spread_map(tiles_columns, map_ref):
    at = lax.broadcasted_iota(jnp.int32, (tiles_columns, D), 0)
    return low(jnp.where(at == map_ref[1:2], 1.0, 0.0))


def read_vectors(tiles, map_ref):
    rows, columns = tiles.shape
    every = mul(tiles[...], spread_map(columns, map_ref))
    inner = lax.broadcasted_iota(jnp.int32, (rows, D), 0) // 16
    return jnp.sum(jnp.where(inner == map_ref[0:1], every, 0.0).reshape(rows // 16, 16, D), axis=0)


def write_vectors(vectors, rows, columns, map_ref):
    every = jnp.broadcast_to(vectors[None], (rows // 16, 16, D)).reshape(rows, D)
    inner = lax.broadcasted_iota(jnp.int32, (rows, D), 0) // 16
    return low(mul(low(jnp.where(inner == map_ref[0:1], every, 0.0)), spread_map(columns, map_ref), 1, 1))


def gate_of(x, router):
    return jax.nn.sigmoid(jnp.sum(x * router, axis=-1, keepdims=True))


def routed_forward_steps(b, need, hidden, spot_ref, chosen, vec_ref, extra, middle_hbm, middle_sem, keep):
    length = hidden.shape[0]

    def pick(_):
        chosen[...] = spots(length, spot_ref)
        need("hidden")
        for t in b.tiles():
            b.x[t] = mul(chosen[:, t], hidden[...], 0, 0)
        need("vectors")
        b.norm()
        keep("x", "normed")
        need("qkv")

    def project(j):
        b.project(j)

    def join(_):
        keep("projected", "merged", "lse")
        need("out")
        b.join()
        keep("branch", "normed_mlp")
        need("up")

    def narrow(_):
        keep("active", "slope")
        need("down")
        for t in b.tiles():
            extra[t] = b.branch[t] + b.narrow(t)
        keep("change")

    def put(_):
        rows = [gate_of(b.x[t], vec_ref[2:3]) * extra[t] for t in b.tiles()]
        pieces = [two(r) for r in rows]
        for i in range(0, length, ROWS):
            t = slice(i, i + ROWS)
            total = hidden[t].astype(jnp.float32)
            for piece, s in zip(pieces, b.tiles()):
                for p in piece:
                    total = total + mul(chosen[t, s], p)
            b.middle[t] = total
            pltpu.make_async_copy(b.middle.at[t], middle_hbm.at[t], middle_sem).start()

    return [(1, pick), (3, project), (6, b.attend), (1, join), (4, b.widen), (1, narrow), (1, put)]


KEPT = ("x", "change") + SAVED


def routed_forward_kernel(hidden_hbm, spot_ref, map_ref, tiles_ref, qkv_hbm, out_hbm, up_hbm, down_hbm, *rest):
    n = len(KEPT)
    middle_hbm, vec_ref = rest[:2]
    kept_hbm = dict(zip(KEPT, rest[2 : 2 + n]))
    rest = rest[2 + n :]
    hidden, chosen, middle, qkv, out, up, down, load_sem, keep_sem, middle_sem = rest[:10]
    kept = dict(zip(KEPT, rest[10:]))
    loads = Loads((("hidden", hidden_hbm, hidden), ("qkv", qkv_hbm, qkv), ("out", out_hbm, out), ("up", up_hbm, up),
                   ("down", down_hbm, down)), load_sem)

    def need(name):
        if name == "vectors":
            vec_ref[...] = read_vectors(tiles_ref, map_ref)
        else:
            loads.need(name)

    saves = {k: pltpu.make_async_copy(kept[k], kept_hbm[k], keep_sem.at[j]) for j, k in enumerate(KEPT)}

    def keep(*names):
        for k in names:
            saves[k].start()

    b = Block(spot_ref.shape[1], dict(kept, middle=middle, qkv=qkv, out=out, up=up, down=down,
                                      gain_attn=vec_ref.at[0:1], gain_mlp=vec_ref.at[1:2]))
    run(routed_forward_steps(b, need, hidden, spot_ref, chosen, vec_ref, kept["change"], middle_hbm, middle_sem, keep))
    for k in KEPT:
        saves[k].wait()
    pltpu.make_async_copy(middle, middle_hbm, middle_sem).wait()


def kept_shapes(rows):
    return [((rows, D), jnp.float32)] * 2 + kept_buffers(rows)


def routed_forward(hidden, spot, place_map, tiles, weights):
    length, rows = hidden.shape[0], spot.shape[1]
    f32, b16 = jnp.float32, jnp.bfloat16
    kept = kept_shapes(rows)
    results = pl.pallas_call(
        routed_forward_kernel,
        in_specs=any_specs(1) + vmem_specs(3) + any_specs(4),
        out_specs=any_specs(1) + vmem_specs(1) + any_specs(len(kept)),
        out_shape=[shape(length, D, dtype=f32), shape(16, D, dtype=f32)] + [shape(*s, dtype=t) for s, t in kept],
        scratch_shapes=buffers(((length, D), b16), ((length, rows), b16), ((length, D), f32), *WEIGHTS)
        + [pltpu.SemaphoreType.DMA((5,)), pltpu.SemaphoreType.DMA((len(kept),)), pltpu.SemaphoreType.DMA]
        + buffers(*kept),
        compiler_params=pltpu.CompilerParams(vmem_limit_bytes=VMEM_BYTES),
        name="routed_forward",
    )(hidden, spot, place_map, tiles, *weights)
    return results[0], results[1], results[2:]


def routed_backward_steps(b, need, grad, spot_ref, chosen, vec_ref, change, grad_rows, gate, ship, targets, vec, turned,
                          grad_hbm, grad_sem):
    length = grad.shape[0]
    router = vec_ref.at[2:3]

    def take(_):
        chosen[...] = spots(length, spot_ref)
        need("grad")
        pieces = two(grad[...])
        need("x", "change")
        for t in b.tiles():
            rows = mul(chosen[:, t], pieces[0], 0, 0) + mul(chosen[:, t], pieces[1], 0, 0)
            g = gate_of(b.x[t], router[...])
            grad_rows[t] = g * rows
            b.grad_low[t] = low(g * rows)
            logits = jnp.sum(rows * change[t], axis=-1, keepdims=True) * g * (1.0 - g)
            gate[t] = jnp.broadcast_to(logits, (ROWS, 128))
        need("down", "active", "slope", "normed_mlp")

    def finish(t, g):
        change[t] = g + gate[t, 0:1] * router[...]

    def put(_):
        pieces = [two(change[t]) for t in b.tiles()]
        for i in range(0, length, ROWS):
            t = slice(i, i + ROWS)
            total = grad[t]
            for piece, s in zip(pieces, b.tiles()):
                for p in piece:
                    total = total + mul(chosen[t, s], p)
            grad[t] = total
            pltpu.make_async_copy(grad.at[t], grad_hbm.at[t], grad_sem).start()

    def route(_):
        total = jnp.zeros((8, D), jnp.float32)
        for t in b.tiles():
            total = total + jnp.sum((gate[t, 0:1] * b.x[t]).reshape(-1, 8, D), axis=0)
        vec(2, jnp.sum(total, axis=0, keepdims=True))

    back = backward_steps(b, lambda t: grad_rows[t], ship, targets, vec, finish, turned)
    waits = [None, ("up", "branch"), ("out", "merged"), ("projected", "lse"), ("normed",), ("qkv",)]
    steps = [(1, take)]
    for (count, body), names in zip(back, waits):
        if names is not None:
            steps.append((0, lambda _, names=names: need(*names)))
        steps.append((count, body))
    return steps + [(1, route), (1, put)]


def routed_backward_kernel(grad_hbm, spot_ref, vec_ref, qkv_hbm, out_hbm, up_hbm, down_hbm, *rest):
    n = len(KEPT)
    kept_hbm, rest = rest[:n], rest[n:]
    input_hbm, gvec_ref, gqkv_hbm, gout_hbm, gup_hbm, gdown_hbm = rest[:6]
    (grad, chosen, grad_low, grad_rows, gate, turned, stage, qkv, out, up, down, load_sem, stage_sem, row_sem) = rest[6:20]
    kept = rest[20:]
    order = ("grad", "x", "change", "down", "active", "slope", "normed_mlp", "up", "branch", "out", "merged", "projected",
             "lse", "normed", "qkv")
    where = dict(zip(KEPT, zip(kept_hbm, kept)), grad=(grad_hbm, grad), qkv=(qkv_hbm, qkv), out=(out_hbm, out),
                 up=(up_hbm, up), down=(down_hbm, down))
    loads = Loads([(k,) + where[k] for k in order], load_sem)
    named = dict(zip(KEPT, kept))
    b = Block(spot_ref.shape[1], dict(named, grad_low=grad_low, qkv=qkv, out=out, up=up, down=down,
                                      gain_attn=vec_ref.at[0:1], gain_mlp=vec_ref.at[1:2]))

    def vec(j, value):
        gvec_ref[j : j + 1] = value

    run(routed_backward_steps(b, loads.need, grad, spot_ref, chosen, vec_ref, named["change"], grad_rows, gate,
                              Ship(stage, stage_sem), (gqkv_hbm, gout_hbm, gup_hbm, gdown_hbm), vec, turned,
                              input_hbm, row_sem))
    pltpu.make_async_copy(grad, input_hbm, row_sem).wait()


def routed_backward(grad, spot, vec, weights, kept):
    length, rows = grad.shape[0], spot.shape[1]
    f32, b16 = jnp.float32, jnp.bfloat16
    return pl.pallas_call(
        routed_backward_kernel,
        in_specs=any_specs(1) + vmem_specs(2) + any_specs(4 + len(kept)),
        out_specs=any_specs(1) + vmem_specs(1) + any_specs(4),
        out_shape=[shape(length, D, dtype=f32), shape(3, D, dtype=f32)] + [shape(*s) for s, _ in WEIGHTS],
        scratch_shapes=buffers(((length, D), f32), ((length, rows), b16), ((rows, D), b16), ((rows, D), f32), ((rows, 128), f32),
                               ((128, rows), f32), ((2, D, D), b16), *WEIGHTS)
        + [pltpu.SemaphoreType.DMA((15,)), pltpu.SemaphoreType.DMA((2,)), pltpu.SemaphoreType.DMA]
        + buffers(*kept_shapes(rows)),
        compiler_params=pltpu.CompilerParams(vmem_limit_bytes=VMEM_BYTES),
        name="routed_backward",
    )(grad, spot, vec, *weights, *kept)


def pack_vectors(vectors):
    rows = jnp.stack([jnp.pad(v, (0, 128 - v.shape[0])) for v in vectors])
    return jnp.pad(rows, ((0, 16 - rows.shape[0]), (0, 0)))


def spread_vectors(vectors, outer, inner):
    rows = vectors.reshape(vectors.shape[0], outer, inner, -1).transpose(2, 0, 1, 3).astype(jnp.bfloat16)
    tiles = jnp.pad(rows, ((0, 0), (0, 16 - rows.shape[1]), (0, 0), (0, 128 - rows.shape[3])))
    return tiles.reshape(inner * 16, outer * 128)


def deliver_kernel(n, *refs):
    tile, sums, outs, vectors, sem = refs[0], refs[1 : n + 1], refs[n + 1 : 2 * n + 1], refs[2 * n + 1 : -1], refs[-1]
    copies = [pltpu.make_async_copy(a, b, sem.at[j]) for j, (a, b) in enumerate(zip(sums, outs))]
    for c in copies:
        c.start()
    for j, v in enumerate(vectors):
        v[...] = tile[j : j + 1, : v.shape[1]]
    for c in copies:
        c.wait()


def deliver(tile, sums, each, count):
    n = len(sums)
    return pl.pallas_call(
        functools.partial(deliver_kernel, n),
        in_specs=vmem_specs(1) + any_specs(n),
        out_specs=any_specs(n) + vmem_specs(count),
        out_shape=[shape(*s.shape, dtype=s.dtype) for s in sums] + [shape(1, each, dtype=jnp.float32)] * count,
        scratch_shapes=[pltpu.SemaphoreType.DMA((n,))],
        name="deliver",
    )(tile, *sums)


def fits(shards, outer, inner):
    return outer == 2 and inner == 16 and all(s.shape[0] % 16 == 0 and s.shape[1] % 128 == 0 for s in shards)


def per_device(outer, inner, *args):
    hidden, cotangent, capacity_class, token_index = args[:4]
    (gain_attn_a, qkv_a, out_a, gain_mlp_a, up_a, down_a, router_shard,
     gain_attn_b, qkv_b, out_b, gain_mlp_b, up_b, down_b) = args[4:]
    hidden, cotangent = hidden[0], cotangent[0]
    length = hidden.shape[0]
    tile = pack_vectors((gain_attn_a, gain_mlp_a, router_shard, gain_attn_b, gain_mlp_b))
    shards = [qkv_a, out_a, up_a, down_a, tile, qkv_b, out_b, up_b, down_b]
    remote = fits(shards, outer, inner)
    if remote:
        whole = gather_all(shards, outer, inner)
    else:
        whole = [lax.all_gather(lax.all_gather(s, "inner", axis=0, tiled=True), "outer", axis=1, tiled=True) for s in shards]
    weights_a, tiles, weights_b = whole[:4], whole[4], whole[5:]

    capacity = (length // 8) << capacity_class[0]
    slots = lax.broadcasted_iota(jnp.int32, token_index.shape, 1)
    spot = jnp.where(slots < capacity, token_index, -1)
    middle, vec, kept = routed_forward(hidden, spot, lane_map(outer, inner), tiles, weights_a)
    output, grad, gvec_b, *grads_b = dense_block(middle, cotangent, vec, weights_b)
    input_grad, gvec_a, *grads_a = routed_backward(grad, spot, vec, weights_a, kept)

    gtile = spread_vectors(jnp.concatenate([gvec_a, gvec_b]), outer, inner)
    sums = grads_a + [gtile] + grads_b
    if remote:
        done = scatter_all(sums, outer, inner)
    else:
        done = [
            lax.psum_scatter(
                lax.psum_scatter(s, "outer", scatter_dimension=1, tiled=True), "inner", scatter_dimension=0, tiled=True
            ).astype(jnp.float32)
            for s in sums
        ]
    each = gain_attn_a.shape[0]
    res = deliver(done[4], done[:4] + done[5:], each, 5)
    ga, gb, v = res[:4], res[4:8], [r[0] for r in res[8:]]
    return (output[None], input_grad[None], v[0], ga[0], ga[1], v[1], ga[2], ga[3], v[2], v[3], gb[0], gb[1], v[4], gb[2], gb[3])


def solution(mesh):
    outer, inner = mesh.shape["outer"], mesh.shape["inner"]
    both = ("outer", "inner")
    rows, vector, matrix = P(both, None, None), P(both), P("inner", "outer")
    block = (vector, matrix, matrix, vector, matrix, matrix)
    return jax.shard_map(
        functools.partial(per_device, outer, inner),
        mesh=mesh,
        in_specs=(rows, rows, vector, P(both, None)) + block + (vector,) + block,
        out_specs=(rows, rows) + block + (vector,) + block,
        check_vma=False,
    )
```

time: 556 us -> 540 us (0.971)
  Pallas kernels: 356 us -> 526 us
  matrix products: 144 us -> 0 us
  local copies, waits for them, and re-layouts: 35.8 us -> 3.56 us
  other arithmetic: 8.71 us -> 2.63 us
    pallas_call x4, Pallas kernels: 64.3 us -> 234 us  [the longest x1 109 us: dense_block(): pl.pallas_call(dense_kernel, in_specs=any_specs(2) + vmem_specs(1) + any_...]
    dot_general x34 -> x0, matrix products: 144 us -> none  [product(): lax.dot_general(left, right, (((ca,), (cb,)), ((), ())), preferred_elemen...]
    unnamed x139 -> x3, local copies, waits for them, and re-layouts: 28.2 us -> 0.68 us
where the time goes in v2:
time: 540 us; the launch traced here: 534 us
  Pallas kernels  526 us (97%)
    pallas_call x1, Pallas kernels, scatter_all(): pl.pallas_call(functools.partial(scatter_kernel, n), out_shape=outs, in_s...  153 us
    pallas_call x1, Pallas kernels, gather_all(): pl.pallas_call(functools.partial(gather_kernel, n), out_shape=outs, in_sp...  138 us
    pallas_call x1, Pallas kernels, dense_block(): pl.pallas_call(dense_kernel, in_specs=any_specs(2) + vmem_specs(1) + any_...  109 us
    pallas_call x1, Pallas kernels, deliver(): pl.pallas_call(functools.partial(deliver_kernel, n), in_specs=vmem_specs(...  56 us
    pallas_call x1, Pallas kernels, routed_backward(): pl.pallas_call(routed_backward_kernel, in_specs=any_specs(1) + vmem_specs...  42.6 us
    pallas_call x1, Pallas kernels, routed_forward(): pl.pallas_call(routed_forward_kernel, in_specs=any_specs(1) + vmem_specs(...  26.5 us

profile of v2, /device:TPU:0, one launch (start us, length us, event | category | flops | bytes accessed | tf_op | source)
XLA Modules:
  0.0 534.1 jit_solution(6842469676948696782)
XLA Ops:
  1.3 0.7 pad_bitcast_fusion.4
  2.0 0.7 pad_bitcast_fusion.2
  2.6 0.7 pad_bitcast_fusion
  3.3 1.3 compare_select_fusion.2.spot_ref
  4.6 0.6 pad.29.refs_4_
  5.2 0.6 pad_add_fusion.map_ref
  5.8 138.4 %gather_weights.1 = (bf16[768,2304]{1,0:T(8,128)(2,1)}, bf16[768,768]{1,0:T(8,128)(2,1)}, bf16[768,3072]{1,0:T(8,128)(2,1)}, bf16[3072,768]{1,0:T(8,128)(2,1)}, ...) custom-call(bf16[48,1152]{1,0:T(8,128)(2,1)} %refs_0_.1, ...), custom_call_target="tpu_custom_call" | custom-call | tf_op jit(solution)/shard_map/gather_weights/pallas_call | solution.py:345
  144.2 26.5 %routed_forward.1 = (f32[1024,768]{1,0:T(8,128)}, f32[16,768]{1,0:T(8,128)}, f32[512,768]{1,0:T(8,128)}, f32[512,768]{1,0:T(8,128)}, f32[512,768]{1,0:T(8,128)},...) custom-call(bf16[1024,768]{1,0:T(8,128)(2,1)} %bitcast.28, ...), custom_call_target="tpu_custom_call" | custom-call | tf_op jit(solution)/shard_map/routed_forward/pallas_call | solution.py:822
  170.7 109.2 %dense_block.1 = (bf16[1024,768]{1,0:T(8,128)(2,1)}, f32[1024,768]{1,0:T(8,128)}, f32[2,768]{1,0:T(2,128)}, bf16[768,2304]{1,0:T(8,128)(2,1)}, bf16[768,768]{1,0...) custom-call(f32[1024,768]{1,0:T(8,128)} %get-tuple-element.76.x_hbm, bf16[1024,768]{1,0:T(8,128)(2,1)} %bitcast.29, ...), custom_call_target="tpu_custom_call" | custom-call | tf_op jit(solution)/shard_map/dense_block/pallas_call | solution.py:690
  279.9 0.0 copy-start
  279.9 42.6 %routed_backward.1 = (f32[1024,768]{1,0:T(8,128)}, f32[3,768]{1,0:T(4,128)}, bf16[768,2304]{1,0:T(8,128)(2,1)}, bf16[768,768]{1,0:T(8,128)(2,1)}, bf16[768,3072]{1,0:T(8,128)(2,1)}, /*index=5*/bf16[3072,768]{1,0:T(8,128)(2,1)}) custom-call(f32[1024,768]{1,0:T(8,128)} %get-tuple-element.83.grad_hbm, s32[1,512]{1,0:T(1,128)} %compare_select_fusion.2.spot_ref, ...), custom_call_target="tpu_custom_call" | custom-call | tf_op jit(solution)/shard_map/routed_backward/pallas_call | solution.py:912
  322.6 0.0 copy-done
  322.6 0.7 convert.6
  323.3 0.1 convert_element_type.17
  323.5 0.1 pad.30
  323.6 0.7 copy.36
  324.3 153.4 %scatter_gradients.1 = (f32[48,1152]{1,0:T(8,128)}, f32[48,384]{1,0:T(8,128)}, f32[48,1536]{1,0:T(8,128)}, f32[192,384]{1,0:T(8,128)}, f32[16,128]{1,0:T(8,128)}...) custom-call(bf16[768,2304]{1,0:T(8,128)(2,1)} %get-tuple-element.95.refs_0_, ...), custom_call_target="tpu_custom_call" | custom-call | tf_op jit(solution)/shard_map/scatter_gradients/pallas_call | solution.py:175
  477.6 56.0 %deliver.1 = (f32[48,1152]{1,0:T(8,128)}, f32[48,384]{1,0:T(8,128)}, f32[48,1536]{1,0:T(8,128)}, f32[192,384]{1,0:T(8,128)}, f32[48,1152]{1,0:T(8,128)}, /*index...) custom-call(f32[16,128]{1,0:T(8,128)} %get-tuple-element.105.refs_0_, ...), custom_call_target="tpu_custom_call" | custom-call | tf_op jit(solution)/shard_map/deliver/pallas_call | solution.py:950
  (5 shorter events, 0.1 us)
Async XLA Ops:
  279.9 42.6 %copy-start = (f32[2,768]{1,0:T(2,128)S(1)}, f32[2,768]{1,0:T(2,128)}, u32[]{:S(2)}) copy-start(f32[2,768]{1,0:T(2,128)} %get-tuple-element.100) | copy-start | bytes 18436

commit v3 on v2

--- a/solution.py
+++ b/solution.py
@@ -183,174 +183,167 @@
     )(*grads)
 
 
-def gather_kernel(n, *refs):
-    shards, outs = refs[:n], refs[n:2 * n]
-    local_sem, send_sem, recv_sem = refs[2 * n:]
-    o, z, x, c = place()
-
-    greet(o, z, x, c)
-
-    def block(p, co, cz, cx, cc):
-        r, w = shards[p].shape
-        row = pl.multiple_of((cz * 4 + cx * 2 + cc) * r, 16)
-        col = pl.multiple_of(co * w, 128)
-        return outs[p].at[pl.ds(row, r), pl.ds(col, w)]
-
-    def send(p, src, dst, slot, rslot, target):
-        return pltpu.make_async_remote_copy(
-            src_ref=src, dst_ref=dst, send_sem=send_sem.at[p, slot], recv_sem=recv_sem.at[p, rslot],
-            device_id=target, device_id_type=MESH)
-
-    def up(p, k, src=None):
-        b = block(p, o, k, x, c)
-        return send(p, b if src is None else src, b, k, k, device(o, z + 1, x, c))
-
-    def down(p, k, src=None):
-        b = block(p, o, k, x, c)
-        return send(p, b if src is None else src, b, 4 + k, k, device(o, z - 1, x, c))
-
-    def first(p, k, src=None):
-        b = block(p, o, k, x, c)
-        t = device(o, z, 1 - x, c) if p % 2 == 0 else device(1 - o, z, x, c)
-        return send(p, b if src is None else src, b, 8 + k, 4 + k, t)
-
-    def second(p, k, a, src=None):
-        if p % 2 == 0:
-            b, t = block(p, o, k, a, c), device(1 - o, z, x, c)
-        else:
-            b, t = block(p, a, k, x, c), device(o, z, 1 - x, c)
-        return send(p, b if src is None else src, b, 12 + 2 * k + a, 8 + 2 * k + a, t)
-
-    def core(p, co, k, cx, src=None):
-        b = block(p, co, k, cx, c)
-        s = k * 4 + co * 2 + cx
-        return send(p, b if src is None else src, b, 20 + s, 16 + s, device(o, z, x, 1 - c))
-
-    def mine(p):
-        return x if p % 2 == 0 else o
-
-    def coords(p, k, a, b):
-        return (b, k, a) if p % 2 == 0 else (a, k, b)
-
-    def core_ab(p, k, a, b, src=None):
-        co, ck, cx = coords(p, k, a, b)
-        return core(p, co, ck, cx, src)
-
-    def other(p):
-        return o if p % 2 == 0 else x
-
-    def own(p):
-        s = shards[p]
-        pltpu.make_async_copy(s, block(p, o, z, x, c), local_sem.at[p]).start()
-
-        @pl.when(z < 3)
-        def _():
-            up(p, z, s).start()
-
-        @pl.when(z > 0)
-        def _():
-            down(p, z, s).start()
-
-        first(p, z, s).start()
-        second(p, z, mine(p), s).start()
-        core(p, o, z, x, s).start()
-
-    def wait_block(p, rslot):
-        b = block(p, o, z, x, c)
-        pltpu.make_async_copy(shards[p], b, recv_sem.at[p, rslot]).wait()
-
-    def z_phase(p):
-        for d in range(1, 4):
-            @pl.when(z >= d)
+FIRST_X = (True, True, False, True, False, False, True, True, False)
+
+
+class Gather:
+    @staticmethod
+    def semaphores(n):
+        return [pltpu.SemaphoreType.DMA((n,)), pltpu.SemaphoreType.DMA((n, 36)), pltpu.SemaphoreType.DMA((n, 32))]
+
+    def __init__(self, shards, outs, local_sem, send_sem, recv_sem):
+        o, z, x, c = place()
+        n = len(shards)
+
+        def block(p, co, cz, cx, cc):
+            r, w = shards[p].shape
+            row = pl.multiple_of((cz * 4 + cx * 2 + cc) * r, 16)
+            col = pl.multiple_of(co * w, 128)
+            return outs[p].at[pl.ds(row, r), pl.ds(col, w)]
+
+        def send(p, src, dst, slot, rslot, target):
+            return pltpu.make_async_remote_copy(
+                src_ref=src, dst_ref=dst, send_sem=send_sem.at[p, slot], recv_sem=recv_sem.at[p, rslot],
+                device_id=target, device_id_type=MESH)
+
+        def up(p, k, src=None):
+            b = block(p, o, k, x, c)
+            return send(p, b if src is None else src, b, k, k, device(o, z + 1, x, c))
+
+        def down(p, k, src=None):
+            b = block(p, o, k, x, c)
+            return send(p, b if src is None else src, b, 4 + k, k, device(o, z - 1, x, c))
+
+        def first(p, k, src=None):
+            b = block(p, o, k, x, c)
+            t = device(o, z, 1 - x, c) if FIRST_X[p] else device(1 - o, z, x, c)
+            return send(p, b if src is None else src, b, 8 + k, 4 + k, t)
+
+        def second(p, k, a, src=None):
+            if FIRST_X[p]:
+                b, t = block(p, o, k, a, c), device(1 - o, z, x, c)
+            else:
+                b, t = block(p, a, k, x, c), device(o, z, 1 - x, c)
+            return send(p, b if src is None else src, b, 12 + 2 * k + a, 8 + 2 * k + a, t)
+
+        def core(p, co, k, cx, src=None):
+            b = block(p, co, k, cx, c)
+            s = k * 4 + co * 2 + cx
+            return send(p, b if src is None else src, b, 20 + s, 16 + s, device(o, z, x, 1 - c))
+
+        def mine(p):
+            return x if FIRST_X[p] else o
+
+        def coords(p, k, a, b):
+            return (b, k, a) if FIRST_X[p] else (a, k, b)
+
+        def core_ab(p, k, a, b, src=None):
+            co, ck, cx = coords(p, k, a, b)
+            return core(p, co, ck, cx, src)
+
+        def other(p):
+            return o if FIRST_X[p] else x
+
+        def own(p):
+            s = shards[p]
+            pltpu.make_async_copy(s, block(p, o, z, x, c), local_sem.at[p]).start()
+
+            @pl.when(z < 3)
             def _():
-                k = z - d
-                wait_block(p, k)
-
-                @pl.when(z < 3)
+                up(p, z, s).start()
+
+            @pl.when(z > 0)
+            def _():
+                down(p, z, s).start()
+
+            first(p, z, s).start()
+            second(p, z, mine(p), s).start()
+            core(p, o, z, x, s).start()
+
+        def wait_block(p, rslot):
+            b = block(p, o, z, x, c)
+            pltpu.make_async_copy(shards[p], b, recv_sem.at[p, rslot]).wait()
+
+        def z_phase(p):
+            for d in range(1, 4):
+                @pl.when(z >= d)
                 def _():
-                    up(p, k).start()
-
-                first(p, k).start()
-                second(p, k, mine(p)).start()
-                core(p, o, k, x).start()
-
-            @pl.when(z + d <= 3)
-            def _():
-                k = z + d
-                wait_block(p, k)
-
-                @pl.when(z > 0)
+                    k = z - d
+                    wait_block(p, k)
+
+                    @pl.when(z < 3)
+                    def _():
+                        up(p, k).start()
+
+                    first(p, k).start()
+                    second(p, k, mine(p)).start()
+                    core(p, o, k, x).start()
+
+                @pl.when(z + d <= 3)
                 def _():
-                    down(p, k).start()
-
-                first(p, k).start()
-                second(p, k, mine(p)).start()
-                core(p, o, k, x).start()
-
-    def ks():
-        return [(z + d) % 4 for d in range(4)]
-
-    def a_phase(p):
-        for k in ks():
-            wait_block(p, 4 + k)
-            a = 1 - mine(p)
-            second(p, k, a).start()
-            core_ab(p, k, a, other(p)).start()
-
-    def b_phase(p):
-        for k in ks():
-            for a in (mine(p), 1 - mine(p)):
-                wait_block(p, 8 + 2 * k + a)
-                core_ab(p, k, a, 1 - other(p)).start()
-
-    def c_phase(p):
-        for s in range(16):
-            wait_block(p, 16 + s)
-
-    def ends(p):
-        pltpu.make_async_copy(shards[p], block(p, o, z, x, c), local_sem.at[p]).wait()
-
-        def done(slot):
-            pltpu.make_async_copy(shards[p], block(p, o, z, x, c), send_sem.at[p, slot]).wait()
-
-        for k in range(4):
-            @pl.when(jnp.logical_and(z < 3, k <= z))
-            def _():
-                done(k)
-
-            @pl.when(jnp.logical_and(z > 0, k >= z))
-            def _():
-                done(4 + k)
-        for slot in range(8, 36):
-            done(slot)
-
-    own(0)
-    for t in range(n + 3):
-        if t + 1 < n:
-            own(t + 1)
-        if t < n:
-            z_phase(t)
-        if 0 <= t - 1 < n:
-            a_phase(t - 1)
-        if 0 <= t - 2 < n:
-            b_phase(t - 2)
-    for p in range(n):
-        c_phase(p)
-        ends(p)
-
-
-def gather_all(shards, outer, inner, collective_id=0):
-    n = len(shards)
-    outs = [jax.ShapeDtypeStruct((s.shape[0] * inner, s.shape[1] * outer), s.dtype) for s in shards]
-    return pl.pallas_call(
-        functools.partial(gather_kernel, n),
-        out_shape=outs,
-        in_specs=[pl.BlockSpec(memory_space=pl.ANY)] * n,
-        out_specs=[pl.BlockSpec(memory_space=pl.ANY)] * n,
-        scratch_shapes=[pltpu.SemaphoreType.DMA((n,)), pltpu.SemaphoreType.DMA((n, 36)), pltpu.SemaphoreType.DMA((n, 32))],
-        compiler_params=pltpu.CompilerParams(collective_id=collective_id, has_side_effects=True),
-        name="gather_weights",
-    )(*shards)
+                    k = z + d
+                    wait_block(p, k)
+
+                    @pl.when(z > 0)
+                    def _():
+                        down(p, k).start()
+
+                    first(p, k).start()
+                    second(p, k, mine(p)).start()
+                    core(p, o, k, x).start()
+
+        def ks():
+            return [(z + d) % 4 for d in range(4)]
+
+        def a_phase(p):
+            for k in ks():
+                wait_block(p, 4 + k)
+                a = 1 - mine(p)
+                second(p, k, a).start()
+                core_ab(p, k, a, other(p)).start()
+
+        def b_phase(p):
+            for k in ks():
+                for a in (mine(p), 1 - mine(p)):
+                    wait_block(p, 8 + 2 * k + a)
+                    core_ab(p, k, a, 1 - other(p)).start()
+
+        def c_phase(p):
+            for s in range(16):
+                wait_block(p, 16 + s)
+
+        def ends(p):
+            def done(slot):
+                pltpu.make_async_copy(shards[p], block(p, o, z, x, c), send_sem.at[p, slot]).wait()
+
+            for k in range(4):
+                @pl.when(jnp.logical_and(z < 3, k <= z))
+                def _():
+                    done(k)
+
+                @pl.when(jnp.logical_and(z > 0, k >= z))
+                def _():
+                    done(4 + k)
+            for slot in range(8, 36):
+                done(slot)
+
+        def only(f):
+            return lambda p: f(p) if 0 <= p < n else None
+
+        def begin():
+            greet(o, z, x, c)
+            own(0)
+
+        def arrived(p):
+            c_phase(p)
+            pltpu.make_async_copy(shards[p], block(p, o, z, x, c), local_sem.at[p]).wait()
+
+        def finish():
+            for p in range(n):
+                ends(p)
+
+        self.begin, self.finish = begin, finish
+        self.own, self.z_phase, self.a_phase, self.b_phase, self.arrived = map(only, (own, z_phase, a_phase, b_phase, arrived))
 
 
 D = 768
@@ -622,29 +615,29 @@
     return [(4, wide), (1, mlp), (1, out), (6, lambda j: b.attend_back(j, turned)), (3, qkv), (1, norm)]
 
 
-def dense_kernel(x_hbm, cot_hbm, vec_ref, qkv_hbm, out_hbm, up_hbm, down_hbm,
-                 y_hbm, grad_hbm, gvec_ref, gqkv_hbm, gout_hbm, gup_hbm, gdown_hbm,
-                 x, cot, qkv, out, up, down, y, turned, stage, load_sem, stage_sem, row_sem, *kept):
-    loads = Loads((("x", x_hbm, x), ("qkv", qkv_hbm, qkv), ("out", out_hbm, out), ("up", up_hbm, up),
-                   ("down", down_hbm, down), ("cot", cot_hbm, cot)), load_sem)
-    b = Block(x.shape[0], dict(zip(SAVED, kept), x=x, grad_low=cot, qkv=qkv, out=out, up=up, down=down,
-                               gain_attn=vec_ref.at[3:4], gain_mlp=vec_ref.at[4:5]))
-
-    def norm(_):
-        loads.need("x")
-        b.norm()
-        loads.need("qkv")
-
-    def join(_):
-        loads.need("out")
-        b.join()
-        loads.need("up")
+KEPT_DENSE = ("x", "branch", "projected", "merged", "lse", "normed_mlp")
+
+
+def dense_kernel(cot_hbm, vec_ref, qkv_hbm, out_hbm, up_hbm, down_hbm, *rest):
+    n = len(KEPT_DENSE)
+    kept_hbm, rest = rest[:n], rest[n:]
+    y_hbm, grad_hbm, gvec_ref, gqkv_hbm, gout_hbm, gup_hbm, gdown_hbm = rest[:7]
+    cot, qkv, out, up, down, active, slope, normed, y, turned, stage, load_sem, stage_sem, row_sem = rest[7:21]
+    kept = dict(zip(KEPT_DENSE, rest[21:]))
+    where = dict(zip(KEPT_DENSE, zip(kept_hbm, rest[21:])), cot=(cot_hbm, cot), qkv=(qkv_hbm, qkv), out=(out_hbm, out),
+                 up=(up_hbm, up), down=(down_hbm, down))
+    order = ("normed_mlp", "up", "down", "x", "branch", "cot", "out", "merged", "projected", "lse", "qkv")
+    loads = Loads([(k,) + where[k] for k in order], load_sem)
+    b = Block(cot.shape[0], dict(kept, active=active, slope=slope, normed=normed, grad_low=cot, qkv=qkv, out=out, up=up, down=down,
+                                 gain_attn=vec_ref.at[3:4], gain_mlp=vec_ref.at[4:5]))
+    x = b.x
 
     def narrow(_):
-        loads.need("down", "cot")
+        loads.need("x", "branch", "down")
         for t in b.tiles():
             y[t] = low(x[t] + b.branch[t] + b.narrow(t))
         pltpu.make_async_copy(y, y_hbm, row_sem.at[0]).start()
+        loads.need("cot")
 
     def vec(j, value):
         gvec_ref[j : j + 1] = value
@@ -653,9 +646,11 @@
         x[t] = grad + cot[t].astype(jnp.float32)
         pltpu.make_async_copy(x.at[t], grad_hbm.at[t], row_sem.at[1]).start()
 
-    run([(1, norm), (3, b.project), (6, b.attend), (1, join), (4, b.widen), (1, narrow)]
-        + backward_steps(b, lambda t: cot[t].astype(jnp.float32), Ship(stage, stage_sem),
-                         (gqkv_hbm, gout_hbm, gup_hbm, gdown_hbm), vec, finish, turned))
+    back = backward_steps(b, lambda t: cot[t].astype(jnp.float32), Ship(stage, stage_sem),
+                          (gqkv_hbm, gout_hbm, gup_hbm, gdown_hbm), vec, finish, turned)
+    run([(0, lambda _: loads.need("normed_mlp", "up")), (4, b.widen), (1, narrow)] + back[:2]
+        + [(0, lambda _: loads.need("out", "merged"))] + back[2:3] + [(0, lambda _: loads.need("projected", "lse"))]
+        + back[3:4] + [(0, lambda _: b.norm())] + back[4:5] + [(0, lambda _: loads.need("qkv"))] + back[5:])
     pltpu.make_async_copy(y, y_hbm, row_sem.at[0]).wait()
     pltpu.make_async_copy(x, grad_hbm, row_sem.at[1]).wait()
 
@@ -684,20 +679,22 @@
     return [s[k] for k in SAVED]
 
 
-def dense_block(x, cot, vec, weights):
-    rows = x.shape[0]
+def dense_block(cot, vec, weights, kept):
+    rows = cot.shape[0]
     f32, b16 = jnp.float32, jnp.bfloat16
+    every = dict(Block.scratch(rows), x=((rows, D), f32))
     return pl.pallas_call(
         dense_kernel,
-        in_specs=any_specs(2) + vmem_specs(1) + any_specs(4),
+        in_specs=any_specs(1) + vmem_specs(1) + any_specs(4 + len(kept)),
         out_specs=any_specs(2) + vmem_specs(1) + any_specs(4),
         out_shape=[shape(rows, D), shape(rows, D, dtype=f32), shape(2, D, dtype=f32)] + [shape(*s) for s, _ in WEIGHTS],
-        scratch_shapes=buffers(((rows, D), f32), ((rows, D), b16), *WEIGHTS, ((rows, D), b16), ((128, rows), f32), ((2, D, D), b16))
-        + [pltpu.SemaphoreType.DMA((6,)), pltpu.SemaphoreType.DMA((2,)), pltpu.SemaphoreType.DMA((2,))]
-        + buffers(*kept_buffers(rows)),
+        scratch_shapes=buffers(((rows, D), b16), *WEIGHTS, every["active"], every["slope"], every["normed"], ((rows, D), b16),
+                               ((128, rows), f32), ((2, D, D), b16))
+        + [pltpu.SemaphoreType.DMA((11,)), pltpu.SemaphoreType.DMA((2,)), pltpu.SemaphoreType.DMA((2,))]
+        + buffers(*[every[k] for k in KEPT_DENSE]),
         compiler_params=pltpu.CompilerParams(vmem_limit_bytes=VMEM_BYTES),
         name="dense_block",
-    )(x, cot, vec, *weights)
+    )(cot, vec, *weights, *kept)
 
 
 def spots(length, spot_ref):
@@ -733,7 +730,7 @@
     return jax.nn.sigmoid(jnp.sum(x * router, axis=-1, keepdims=True))
 
 
-def routed_forward_steps(b, need, hidden, spot_ref, chosen, vec_ref, extra, middle_hbm, middle_sem, keep):
+def routed_forward_steps(b, need, hidden, spot_ref, chosen, vec_ref, extra, keep):
     length = hidden.shape[0]
 
     def pick(_):
@@ -773,64 +770,15 @@
                 for p in piece:
                     total = total + mul(chosen[t, s], p)
             b.middle[t] = total
-            pltpu.make_async_copy(b.middle.at[t], middle_hbm.at[t], middle_sem).start()
 
     return [(1, pick), (3, project), (6, b.attend), (1, join), (4, b.widen), (1, narrow), (1, put)]
 
 
 KEPT = ("x", "change") + SAVED
-
-
-def routed_forward_kernel(hidden_hbm, spot_ref, map_ref, tiles_ref, qkv_hbm, out_hbm, up_hbm, down_hbm, *rest):
-    n = len(KEPT)
-    middle_hbm, vec_ref = rest[:2]
-    kept_hbm = dict(zip(KEPT, rest[2 : 2 + n]))
-    rest = rest[2 + n :]
-    hidden, chosen, middle, qkv, out, up, down, load_sem, keep_sem, middle_sem = rest[:10]
-    kept = dict(zip(KEPT, rest[10:]))
-    loads = Loads((("hidden", hidden_hbm, hidden), ("qkv", qkv_hbm, qkv), ("out", out_hbm, out), ("up", up_hbm, up),
-                   ("down", down_hbm, down)), load_sem)
-
-    def need(name):
-        if name == "vectors":
-            vec_ref[...] = read_vectors(tiles_ref, map_ref)
-        else:
-            loads.need(name)
-
-    saves = {k: pltpu.make_async_copy(kept[k], kept_hbm[k], keep_sem.at[j]) for j, k in enumerate(KEPT)}
-
-    def keep(*names):
-        for k in names:
-            saves[k].start()
-
-    b = Block(spot_ref.shape[1], dict(kept, middle=middle, qkv=qkv, out=out, up=up, down=down,
-                                      gain_attn=vec_ref.at[0:1], gain_mlp=vec_ref.at[1:2]))
-    run(routed_forward_steps(b, need, hidden, spot_ref, chosen, vec_ref, kept["change"], middle_hbm, middle_sem, keep))
-    for k in KEPT:
-        saves[k].wait()
-    pltpu.make_async_copy(middle, middle_hbm, middle_sem).wait()
 
 
 def kept_shapes(rows):
     return [((rows, D), jnp.float32)] * 2 + kept_buffers(rows)
-
-
-def routed_forward(hidden, spot, place_map, tiles, weights):
-    length, rows = hidden.shape[0], spot.shape[1]
-    f32, b16 = jnp.float32, jnp.bfloat16
-    kept = kept_shapes(rows)
-    results = pl.pallas_call(
-        routed_forward_kernel,
-        in_specs=any_specs(1) + vmem_specs(3) + any_specs(4),
-        out_specs=any_specs(1) + vmem_specs(1) + any_specs(len(kept)),
-        out_shape=[shape(length, D, dtype=f32), shape(16, D, dtype=f32)] + [shape(*s, dtype=t) for s, t in kept],
-        scratch_shapes=buffers(((length, D), b16), ((length, rows), b16), ((length, D), f32), *WEIGHTS)
-        + [pltpu.SemaphoreType.DMA((5,)), pltpu.SemaphoreType.DMA((len(kept),)), pltpu.SemaphoreType.DMA]
-        + buffers(*kept),
-        compiler_params=pltpu.CompilerParams(vmem_limit_bytes=VMEM_BYTES),
-        name="routed_forward",
-    )(hidden, spot, place_map, tiles, *weights)
-    return results[0], results[1], results[2:]
 
 
 def routed_backward_steps(b, need, grad, spot_ref, chosen, vec_ref, change, grad_rows, gate, ship, targets, vec, turned,
@@ -923,6 +871,122 @@
     )(grad, spot, vec, *weights, *kept)
 
 
+def forward_kernel(remote, *refs):
+    hidden_hbm, spot_ref, map_ref, *refs = refs
+    given, refs = refs[:9], refs[9:]
+    if remote:
+        whole, refs = refs[:9], refs[9:]
+    else:
+        whole = given
+    vec_ref, *refs = refs
+    n, m = len(KEPT), len(KEPT_DENSE)
+    kept_hbm, refs = dict(zip(KEPT, refs[:n])), refs[n:]
+    dense_hbm, refs = dict(zip(KEPT_DENSE, refs[:m])), refs[m:]
+    hidden, chosen, tiles, *refs = refs
+    weights, refs = refs[:6], refs[6:]
+    kept, refs = dict(zip(KEPT, refs[:n])), refs[n:]
+    dense, refs = dict(zip(KEPT_DENSE, refs[:m])), refs[m:]
+    normed, load_sem, keep_sem, dense_sem = refs[:4]
+    names = ("vectors", "qkv", "out", "up", "down", "qkv_b", "out_b")
+    first = pltpu.make_async_copy(hidden_hbm, hidden, load_sem.at[7])
+    first.start()
+    loads = {k: pltpu.make_async_copy(whole[j], dst, load_sem.at[j])
+             for j, (k, dst) in enumerate(zip(names, [tiles] + weights))}
+    flow = Gather(given, whole, *refs[4:]) if remote else None
+    if not remote:
+        for c in loads.values():
+            c.start()
+
+    def need(*wanted):
+        for k in wanted:
+            if k == "hidden":
+                first.wait()
+                continue
+            loads[k].wait()
+            if k == "vectors":
+                vec_ref[...] = read_vectors(tiles, map_ref)
+
+    saves = {k: pltpu.make_async_copy(kept[k], kept_hbm[k], keep_sem.at[j]) for j, k in enumerate(KEPT)}
+    dense_saves = {k: pltpu.make_async_copy(dense[k], dense_hbm[k], dense_sem.at[j]) for j, k in enumerate(KEPT_DENSE)}
+
+    def keep(*wanted):
+        for k in wanted:
+            saves[k].start()
+
+    def keep_dense(*wanted):
+        for k in wanted:
+            dense_saves[k].start()
+
+    qkv, out, up, down, qkv_b, out_b = weights
+    b = Block(spot_ref.shape[1], dict(kept, middle=dense["x"], qkv=qkv, out=out, up=up, down=down,
+                                      gain_attn=vec_ref.at[0:1], gain_mlp=vec_ref.at[1:2]))
+    d = Block(hidden.shape[0], dict(dense, qkv=qkv_b, out=out_b, normed=normed,
+                                    gain_attn=vec_ref.at[3:4], gain_mlp=vec_ref.at[4:5]))
+
+    def norm(_):
+        keep_dense("x")
+        d.norm()
+        need("qkv_b")
+
+    def join(_):
+        keep_dense("projected", "merged", "lse")
+        need("out_b")
+        d.join()
+        keep_dense("branch", "normed_mlp")
+
+    routed = routed_forward_steps(b, need, hidden, spot_ref, chosen, vec_ref, kept["change"], keep)
+    steps = routed + [(1, norm), (3, d.project), (6, d.attend), (1, join)]
+    if remote:
+        def arrive(p):
+            flow.arrived(p)
+            if 0 <= p < len(names):
+                loads[names[p]].start()
+
+        flow.begin()
+        slots = [[lambda t=t: flow.own(t + 1), lambda t=t: flow.z_phase(t), lambda t=t: flow.a_phase(t - 1),
+                  lambda t=t: flow.b_phase(t - 2), lambda t=t: arrive(t - 3)] for t in range(12)]
+        for t in range(6):
+            for f in slots[t]:
+                f()
+        units = [[] for _ in range(sum(c for c, _ in steps))]
+        plan = {6: (0, 2, 4, 5, 6), 7: (7, 8, 9, 9, 9), 8: (11, 12, 13, 14, 15), 9: (16, 16, 16, 16, 16), 10: (19, 20, 21, 22, 23), 11: (24, 25, 26, 26, 26)}
+        for t, at in plan.items():
+            for f, u in zip(slots[t], at):
+                units[u].append(f)
+        run(steps, units)
+        flow.finish()
+    else:
+        run(steps)
+    for c in list(saves.values()) + list(dense_saves.values()):
+        c.wait()
+
+
+def forward(remote, hidden, spot, place_map, weights, outer, inner):
+    length, rows = hidden.shape[0], spot.shape[1]
+    f32, b16 = jnp.float32, jnp.bfloat16
+    kept = kept_shapes(rows)
+    every = dict(Block.scratch(length), x=((length, D), f32))
+    dense = [every[k] for k in KEPT_DENSE]
+    whole = [shape(w.shape[0] * inner, w.shape[1] * outer) for w in weights] if remote else []
+    tiles = (16 * inner, 128 * outer)
+    scratch = (buffers(((length, D), b16), ((length, rows), b16), (tiles, b16), *WEIGHTS, *WEIGHTS[:2], *kept, *dense, ((length, D), b16))
+               + [pltpu.SemaphoreType.DMA((k,)) for k in (8, len(kept), len(dense))])
+    if remote:
+        scratch += Gather.semaphores(len(weights))
+    results = pl.pallas_call(
+        functools.partial(forward_kernel, remote),
+        in_specs=any_specs(1) + vmem_specs(2) + any_specs(9),
+        out_specs=any_specs(len(whole)) + vmem_specs(1) + any_specs(len(kept) + len(dense)),
+        out_shape=whole + [shape(16, D, dtype=f32)] + [shape(*s, dtype=t) for s, t in kept + dense],
+        scratch_shapes=scratch,
+        compiler_params=pltpu.CompilerParams(vmem_limit_bytes=VMEM_BYTES, **(dict(collective_id=0, has_side_effects=True) if remote else {})),
+        name="forward",
+    )(hidden, spot, place_map, *weights)
+    if remote:
+        weights, results = results[:9], results[9:]
+    return weights, results[0], results[1 : 1 + len(kept)], results[1 + len(kept) :]
+
+
 def pack_vectors(vectors):
     rows = jnp.stack([jnp.pad(v, (0, 128 - v.shape[0])) for v in vectors])
     return jnp.pad(rows, ((0, 16 - rows.shape[0]), (0, 0)))
@@ -935,24 +999,20 @@
 
 
 def deliver_kernel(n, *refs):
-    tile, sums, outs, vectors, sem = refs[0], refs[1 : n + 1], refs[n + 1 : 2 * n + 1], refs[2 * n + 1 : -1], refs[-1]
-    copies = [pltpu.make_async_copy(a, b, sem.at[j]) for j, (a, b) in enumerate(zip(sums, outs))]
-    for c in copies:
-        c.start()
+    tile, sums, outs, vectors = refs[0], refs[1 : n + 1], refs[n + 1 : 2 * n + 1], refs[2 * n + 1 :]
+    for a, b in zip(sums, outs):
+        b[...] = a[...]
     for j, v in enumerate(vectors):
         v[...] = tile[j : j + 1, : v.shape[1]]
-    for c in copies:
-        c.wait()
 
 
 def deliver(tile, sums, each, count):
     n = len(sums)
     return pl.pallas_call(
         functools.partial(deliver_kernel, n),
-        in_specs=vmem_specs(1) + any_specs(n),
-        out_specs=any_specs(n) + vmem_specs(count),
+        in_specs=vmem_specs(1 + n),
+        out_specs=vmem_specs(n + count),
         out_shape=[shape(*s.shape, dtype=s.dtype) for s in sums] + [shape(1, each, dtype=jnp.float32)] * count,
-        scratch_shapes=[pltpu.SemaphoreType.DMA((n,))],
         name="deliver",
     )(tile, *sums)
 
@@ -968,20 +1028,17 @@
     hidden, cotangent = hidden[0], cotangent[0]
     length = hidden.shape[0]
     tile = pack_vectors((gain_attn_a, gain_mlp_a, router_shard, gain_attn_b, gain_mlp_b))
-    shards = [qkv_a, out_a, up_a, down_a, tile, qkv_b, out_b, up_b, down_b]
+    shards = [tile, qkv_a, out_a, up_a, down_a, qkv_b, out_b, up_b, down_b]
     remote = fits(shards, outer, inner)
-    if remote:
-        whole = gather_all(shards, outer, inner)
-    else:
-        whole = [lax.all_gather(lax.all_gather(s, "inner", axis=0, tiled=True), "outer", axis=1, tiled=True) for s in shards]
-    weights_a, tiles, weights_b = whole[:4], whole[4], whole[5:]
+    if not remote:
+        shards = [lax.all_gather(lax.all_gather(s, "inner", axis=0, tiled=True), "outer", axis=1, tiled=True) for s in shards]
 
     capacity = (length // 8) << capacity_class[0]
     slots = lax.broadcasted_iota(jnp.int32, token_index.shape, 1)
     spot = jnp.where(slots < capacity, token_index, -1)
-    middle, vec, kept = routed_forward(hidden, spot, lane_map(outer, inner), tiles, weights_a)
-    output, grad, gvec_b, *grads_b = dense_block(middle, cotangent, vec, weights_b)
-    input_grad, gvec_a, *grads_a = routed_backward(grad, spot, vec, weights_a, kept)
+    whole, vec, kept, kept_dense = forward(remote, hidden, spot, lane_map(outer, inner), shards, outer, inner)
+    output, grad, gvec_b, *grads_b = dense_block(cotangent, vec, whole[5:], kept_dense)
+    input_grad, gvec_a, *grads_a = routed_backward(grad, spot, vec, whole[1:5], kept)
 
     gtile = spread_vectors(jnp.concatenate([gvec_a, gvec_b]), outer, inner)
     sums = grads_a + [gtile] + grads_b

time: 540 us -> 453 us (0.84)
  Pallas kernels: 526 us -> 440 us
    pallas_call x1, Pallas kernels: 56 us -> 2.71 us  [deliver(): pl.pallas_call(functools.partial(deliver_kernel, n), in_specs=vmem_specs(...]
    pallas_call x3 -> x2, Pallas kernels: 274 us -> 247 us  [the longest x1 160 us: forward(): pl.pallas_call(functools.partial(forward_kernel, remote), in_specs=any_sp...]
    pallas_call x1, Pallas kernels: 153 us -> 147 us  [scatter_all(): pl.pallas_call(functools.partial(scatter_kernel, n), out_shape=outs, in_s...]
where the time goes in v3:
time: 453 us; the launch traced here: 448 us
  Pallas kernels  440 us (97%)
    pallas_call x1, Pallas kernels, forward(): pl.pallas_call(functools.partial(forward_kernel, remote), in_specs=any_sp...  160 us
    pallas_call x1, Pallas kernels, scatter_all(): pl.pallas_call(functools.partial(scatter_kernel, n), out_shape=outs, in_s...  147 us
    pallas_call x1, Pallas kernels, dense_block(): pl.pallas_call(dense_kernel, in_specs=any_specs(1) + vmem_specs(1) + any_...  87 us
    pallas_call x1, Pallas kernels, routed_backward(): pl.pallas_call(routed_backward_kernel, in_specs=any_specs(1) + vmem_specs...  43 us

profile of v3, /device:TPU:0, one launch (start us, length us, event | category | flops | bytes accessed | tf_op | source)
XLA Modules:
  0.0 447.7 jit_solution(16208457113104125220)
XLA Ops:
  1.3 0.7 pad_bitcast_fusion.4
  2.0 0.7 pad_bitcast_fusion.2
  2.6 0.7 pad_bitcast_fusion
  3.3 1.3 compare_select_fusion.2.refs_1_.spot_ref
  4.6 0.6 pad.29.refs_3_
  5.2 0.6 pad_add_fusion.refs_2_
  5.8 160.0 %forward.1 = (bf16[256,256]{1,0:T(8,128)(2,1)}, bf16[768,2304]{1,0:T(8,128)(2,1)}, bf16[768,768]{1,0:T(8,128)(2,1)}, bf16[768,3072]{1,0:T(8,128)(2,1)}, bf16[307...) custom-call(bf16[1024,768]{1,0:T(8,128)(2,1)} %bitcast.29, ...), custom_call_target="tpu_custom_call" | custom-call | tf_op jit(solution)/shard_map/forward/pallas_call | solution.py:976
  165.8 87.0 %dense_block.1 = (bf16[1024,768]{1,0:T(8,128)(2,1)}, f32[1024,768]{1,0:T(8,128)}, f32[2,768]{1,0:T(2,128)}, bf16[768,2304]{1,0:T(8,128)(2,1)}, bf16[768,768]{1,0...) custom-call(bf16[1024,768]{1,0:T(8,128)(2,1)} %bitcast.28, f32[16,768]{1,0:T(8,128)} %get-tuple-element.75.vec_ref, ...), custom_call_target="tpu_custom_call" | custom-call | tf_op jit(solution)/shard_map/dense_block/pallas_call | solution.py:686
  252.8 0.0 copy-start
  252.8 43.0 %routed_backward.1 = (f32[1024,768]{1,0:T(8,128)}, f32[3,768]{1,0:T(4,128)}, bf16[768,2304]{1,0:T(8,128)(2,1)}, bf16[768,768]{1,0:T(8,128)(2,1)}, bf16[768,3072]{1,0:T(8,128)(2,1)}, /*index=5*/bf16[3072,768]{1,0:T(8,128)(2,1)}) custom-call(f32[1024,768]{1,0:T(8,128)} %get-tuple-element.87.grad_hbm, s32[1,512]{1,0:T(1,128)} %compare_select_fusion.2.refs_1_.spot_ref, ...), custom_call_target="tpu_custom_call" | custom-call | tf_op jit(solution)/shard_map/routed_backward/pallas_call | solution.py:860
  295.8 0.0 copy-done
  295.8 0.7 convert.6
  296.5 0.1 convert_element_type.17
  296.7 0.1 pad.30
  296.8 0.7 copy.36
  297.5 147.0 %scatter_gradients.1 = (f32[48,1152]{1,0:T(8,128)}, f32[48,384]{1,0:T(8,128)}, f32[48,1536]{1,0:T(8,128)}, f32[192,384]{1,0:T(8,128)}, f32[16,128]{1,0:T(8,128)}...) custom-call(bf16[768,2304]{1,0:T(8,128)(2,1)} %get-tuple-element.103.refs_0_, ...), custom_call_target="tpu_custom_call" | custom-call | tf_op jit(solution)/shard_map/scatter_gradients/pallas_call | solution.py:175
  444.5 2.7 deliver.1
  (5 shorter events, 0.1 us)
Async XLA Ops:
  252.8 43.0 %copy-start = (f32[2,768]{1,0:T(2,128)S(1)}, f32[2,768]{1,0:T(2,128)}, u32[]{:S(2)}) copy-start(f32[2,768]{1,0:T(2,128)} %get-tuple-element.108) | copy-start | bytes 18436

commit v4 on v3

v4 whole, which is shorter than its diff:
```python
import functools

import jax
import jax.numpy as jnp
from jax import lax
from jax.experimental import pallas as pl
from jax.experimental.pallas import tpu as pltpu
from jax.sharding import PartitionSpec as P

MESH = pl.DeviceIdType.MESH


def place():
    o, i = lax.axis_index("outer"), lax.axis_index("inner")
    return o, i // 4, (i // 2) % 2, i % 2


def device(o, z, x, c):
    return (o, z * 4 + x * 2 + c)


def greet(o, z, x, c):
    barrier = pltpu.get_barrier_semaphore()
    signal = functools.partial(pl.semaphore_signal, barrier, inc=1, device_id_type=MESH)
    signal(device_id=device(1 - o, z, x, c))
    signal(device_id=device(o, z, 1 - x, c))
    signal(device_id=device(o, z, x, 1 - c))

    @pl.when(z > 0)
    def _():
        signal(device_id=device(o, z - 1, x, c))

    @pl.when(z < 3)
    def _():
        signal(device_id=device(o, z + 1, x, c))

    pl.semaphore_wait(barrier, 3 + jnp.where(z > 0, 1, 0) + jnp.where(z < 3, 1, 0))


GATHER_PARTS = (
        (0, 0, 16, 0, 128, False), (1, 0, 48, 0, 640, True), (1, 0, 48, 640, 512, False), (2, 0, 48, 0, 384, True), (3,
    0, 48, 0, 768, True), (3, 0, 48, 768, 768, False), (4, 0, 96, 0, 384, False), (4, 96, 96, 0, 384, True), (5, 0, 48,
    0, 640, False), (5, 0, 48, 640, 512, True), (6, 0, 48, 0, 384, False), (7, 0, 48, 0, 768, True), (7, 0, 48, 768,
    768, False), (8, 0, 96, 0, 384, False), (8, 96, 96, 0, 384, True))
GATHER_PLAN = (
        (0, 0, 0), (0, 0, 1), (0, 0, 2), (0, 1, 0), (0, 1, 1), (0, 1, 2), (0, 2, 0), (0, 2, 1), (0, 2, 2), (0, 3, 0),
    (0, 0, 3), (0, 3, 1), (0, 4, 0), (0, 3, 2), (0, 1, 3), (0, 0, 4), (0, 0, 5), (0, 2, 3), (0, 1, 4), (0, 4, 1), (0, 5,
    0), (0, 1, 5), (0, 3, 3), (0, 6, 0), (0, 2, 4), (0, 4, 2), (0, 2, 5), (0, 0, 6), (1, 5, 1), (1, 4, 3), (1, 3, 4),
    (1, 5, 2), (1, 6, 1), (1, 3, 5), (1, 1, 6), (1, 6, 2), (1, 0, 7), (1, 5, 3), (1, 0, 8), (1, 2, 6), (2, 6, 3), (2, 4,
    4), (2, 1, 7), (2, 1, 8), (3, 3, 6), (3, 2, 7), (3, 0, 9), (3, 2, 8), (5, 3, 7), (5, 4, 5), (5, 3, 8), (5, 1, 9),
    (5, 0, 10), (5, 0, 11), (6, 2, 9), (6, 1, 10), (6, 5, 4), (6, 1, 11), (6, 3, 9), (6, 2, 10), (6, 6, 4), (6, 4, 7),
    (6, 2, 11), (6, 3, 10), (6, 0, 12), (6, 4, 6), (6, 0, 13), (6, 3, 11), (6, 0, 14), (6, 5, 5), (6, 1, 12), (6, 1,
    13), (7, 6, 5), (7, 1, 14), (7, 2, 12), (8, 2, 13), (8, 2, 14), (8, 4, 8), (9, 4, 9), (9, 3, 12), (9, 3, 13), (9, 3,
    14), (14, 5, 6), (14, 5, 7), (15, 4, 10), (15, 6, 6), (15, 6, 7), (15, 4, 11), (17, 5, 8), (18, 5, 9), (18, 6, 8),
    (18, 6, 9), (20, 4, 12), (22, 4, 13), (24, 4, 14), (24, 5, 10), (25, 6, 10), (26, 5, 11), (26, 5, 12), (27, 6, 11),
    (27, 6, 12), (27, 5, 14), (27, 5, 13), (28, 6, 14), (28, 6, 13))


class Gather:
    @staticmethod
    def semaphores(n):
        return [pltpu.SemaphoreType.DMA(k) for k in ((n,), (n, 13), (n, 11))]

    def __init__(self, parts, shards, outs, local_sem, send_sem, recv_sem):
        o, z, x, c = place()
        n = len(parts)

        def shard(p):
            a, r0, r, c0, w, _ = parts[p]
            return shards[a].at[pl.ds(r0, r), pl.ds(c0, w)]

        def blocks(p, oo):
            a, r0, r, c0, w, _ = parts[p]
            rows, each = shards[a].shape
            view = outs[a].reshape(4, 2, 2, rows, 2 * each)
            return view, pl.ds(r0, r), pl.ds(pl.multiple_of(oo * each + c0, 128), w)

        def chunk(p, k):
            view, rows, columns = blocks(p, o)
            return view.at[k, x, c, rows, columns]

        def group(p, second, first):
            first_x = parts[p][5]
            px, po = (first, second) if first_x else (second, first)
            view, rows, columns = blocks(p, o if po else 1 - o)
            return view.at[:, x if px else 1 - x, c, rows, columns]

        def send(p, src, dst, slot, target):
            return pltpu.make_async_remote_copy(
                src_ref=src, dst_ref=dst, send_sem=send_sem.at[p, slot[0]], recv_sem=recv_sem.at[p, slot[1]],
                device_id=target, device_id_type=MESH)

        def wait(ref, sem):
            pltpu.make_async_copy(ref, ref, sem).wait()

        def up(p, k, hop, src=None):
            b = chunk(p, k)
            return send(p, b if src is None else src, b, (hop, k), device(o, z + 1, x, c))

        def down(p, k, hop, src=None):
            b = chunk(p, k)
            return send(p, b if src is None else src, b, (3 + hop, k), device(o, z - 1, x, c))

        def near(p, second):
            return device(o, z, 1 - x, c) if parts[p][5] != second else device(1 - o, z, x, c)

        def to_core(p, second, first):
            b = group(p, second, first)
            send(p, b, b, (9 + 2 * second + first, 7 + 2 * second + first), device(o, z, x, 1 - c)).start()

        def to_second(p, first):
            b = group(p, 1, first)
            send(p, b, b, (7 + first, 5 + first), near(p, True)).start()

        def local(p):
            return pltpu.make_async_copy(shard(p), chunk(p, z), local_sem.at[p])

        def own(p):
            @pl.when(z < 3)
            def _():
                up(p, z, 0, shard(p)).start()

            @pl.when(z > 0)
            def _():
                down(p, z, 0, shard(p)).start()

            local(p).start()

        def hop(d):
            def go(p):
                @pl.when(z >= d)
                def _():
                    wait(chunk(p, z - d), recv_sem.at[p, z - d])
                    if d < 3:
                        @pl.when(z < 3)
                        def _():
                            up(p, z - d, d).start()

                @pl.when(z + d <= 3)
                def _():
                    wait(chunk(p, z + d), recv_sem.at[p, z + d])
                    if d < 3:
                        @pl.when(z > 0)
                        def _():
                            down(p, z + d, d).start()
            return go

        third = hop(3)

        def first(p):
            third(p)
            local(p).wait()
            b = group(p, 1, 1)
            send(p, b, b, (6, 4), near(p, False)).start()
            to_second(p, 1)
            to_core(p, 1, 1)

        def second(p):
            wait(group(p, 1, 0), recv_sem.at[p, 4])
            to_second(p, 0)
            to_core(p, 1, 0)

        def cores(p):
            for f in (1, 0):
                wait(group(p, 0, f), recv_sem.at[p, 5 + f])
                to_core(p, 0, f)

        def arrived(p):
            for slot in range(4):
                wait(group(p, 1, 1), recv_sem.at[p, 7 + slot])

        def finish():
            for p in range(n):
                for d in range(3):
                    @pl.when(jnp.logical_and(z < 3, z >= d))
                    def _():
                        wait(chunk(p, z), send_sem.at[p, d])

                    @pl.when(jnp.logical_and(z > 0, z + d <= 3))
                    def _():
                        wait(chunk(p, z), send_sem.at[p, 3 + d])
                b = group(p, 1, 1)
                for slot in range(6, 13):
                    wait(b, send_sem.at[p, slot])

        self.finish = finish
        self.steps = (own, hop(1), hop(2), first, second, cores, arrived)

    def begin(self):
        greet(*place())


PARTS = (
        (2, 0, 48, 0, 768, True, 1), (3, 96, 96, 0, 384, False, 2), (3, 0, 96, 0, 384, False, 0), (2, 0, 48, 768, 768,
    True, 3), (1, 0, 48, 0, 384, False, 4), (0, 0, 48, 0, 640, True, 5), (0, 0, 48, 640, 512, False, 6), (6, 0, 48, 768,
    768, True, 3), (6, 0, 48, 0, 768, False, 1), (7, 96, 96, 0, 384, True, 2), (7, 0, 96, 0, 384, False, 0), (4, 0, 48,
    0, 640, True, 5), (4, 0, 48, 640, 512, False, 6), (5, 0, 48, 0, 384, True, 4), (8, 0, 16, 0, 128, False, 7))
BACK_PLAN = (
        (0, 0, 0), (0, 0, 1), (0, 0, 2), (0, 0, 3), (0, 0, 4), (1, 1, 0), (2, 2, 0), (2, 1, 1), (3, 2, 1), (3, 1, 2),
    (3, 1, 3), (4, 2, 2), (4, 2, 3), (5, 3, 0), (6, 4, 0), (6, 3, 1), (6, 1, 4), (7, 4, 1), (7, 2, 4), (10, 3, 3), (10,
    0, 5), (10, 0, 6), (11, 3, 2), (11, 4, 3), (12, 5, 1), (12, 4, 2), (12, 1, 5), (13, 5, 0), (13, 6, 1), (13, 2, 5),
    (14, 6, 0), (15, 7, 1), (15, 5, 2), (15, 3, 4), (16, 7, 0), (16, 6, 2), (16, 4, 4), (16, 1, 6), (16, 8, 1), (17, 5,
    3), (17, 2, 6), (18, 8, 0), (18, 9, 1), (18, 6, 3), (18, 7, 2), (18, 0, 9), (19, 3, 5), (20, 9, 0), (20, 8, 2), (20,
    5, 4), (20, 4, 5), (20, 7, 3), (20, 0, 8), (20, 1, 9), (21, 6, 4), (21, 2, 9), (21, 9, 2), (21, 3, 6), (21, 0, 10),
    (22, 8, 3), (22, 4, 6), (22, 1, 8), (22, 7, 4), (23, 2, 8), (23, 1, 10), (24, 9, 3), (24, 8, 4), (24, 5, 5), (24, 0,
    7), (24, 2, 10), (25, 6, 5), (26, 9, 4), (26, 0, 13), (27, 1, 7), (28, 7, 5), (29, 2, 7), (29, 3, 9), (29, 8, 5),
    (29, 0, 14), (29, 4, 9), (29, 5, 6), (29, 9, 5), (29, 0, 11), (29, 3, 8), (29, 6, 6), (29, 4, 8), (29, 7, 6), (29,
    8, 6), (29, 9, 6), (29, 0, 12), (29, 1, 11), (29, 2, 11), (29, 3, 7), (29, 3, 10), (29, 4, 7), (29, 4, 10), (29, 1,
    12), (29, 2, 12), (29, 5, 8), (29, 5, 9), (29, 6, 8), (29, 6, 9), (29, 7, 8), (29, 5, 7), (29, 6, 7), (29, 1, 13),
    (29, 8, 8), (29, 7, 9), (29, 2, 13), (29, 3, 11), (29, 4, 11), (29, 9, 8), (29, 8, 9), (29, 1, 14), (29, 7, 7), (29,
    2, 14), (29, 3, 12), (29, 4, 12), (29, 5, 10), (29, 9, 9), (29, 6, 10), (29, 8, 7), (29, 5, 11), (29, 3, 14), (29,
    6, 11), (29, 9, 7), (29, 4, 14), (29, 7, 10), (29, 3, 13), (29, 4, 13), (29, 8, 10), (29, 7, 11), (29, 5, 12), (29,
    6, 12), (29, 5, 14), (29, 6, 14), (29, 5, 13), (29, 9, 10), (29, 8, 11), (29, 6, 13), (29, 7, 12), (29, 9, 11), (29,
    7, 14), (29, 7, 13), (29, 8, 12), (29, 8, 14), (29, 8, 13), (29, 9, 12), (29, 9, 14), (29, 9, 13))


class Scatter:
    def __init__(self, parts, grads, outs, core_in, second_in, first_in, buffers, sems):
        o, z, x, c = place()
        acc, z_in, stage_own, stage_got, stage_second, stage_first, stage_out = buffers
        send_sem, recv_sem, own_sem, stage_sem, out_sem = sems
        n = len(parts)

        def kind(p):
            return 1 if parts[p][2] == 96 else 0

        def of(p):
            return parts[p][2], parts[p][4]

        def part(ref, p):
            r, w = of(p)
            return ref.at[:, pl.ds(0, r), pl.ds(0, w)]

        def group(p, second, first, core):
            g, r0, r, c0, w, first_x, _ = parts[p]
            px, po = (first, second) if first_x else (second, first)
            xx = x if px else 1 - x
            oo = o if po else 1 - o
            height, width = grads[g].shape
            each = width // 2
            return grads[g].reshape(4, 2, 2, height // 16, width).at[:, xx, core, pl.ds(r0, r), pl.ds(pl.multiple_of(oo * each + c0, 128), w)]

        def far(p, second):
            return device(o, z, 1 - x, c) if parts[p][5] != second else device(1 - o, z, x, c)

        def send(p, src, dst, kind_, slot, target):
            return pltpu.make_async_remote_copy(
                src_ref=src, dst_ref=dst, send_sem=send_sem.at[p, kind_], recv_sem=recv_sem.at[p, slot],
                device_id=target, device_id_type=MESH)

        def wait(ref, sem):
            pltpu.make_async_copy(ref, ref, sem).wait()

        slots, last_user = {}, {}
        turn = [0, 0]
        for p in range(n):
            k = kind(p)
            slots[p] = turn[k] % 2
            last_user[p] = next((q for q in range(p - 1, -1, -1) if kind(q) == k and slots[q] == slots[p]), None)
            turn[k] += 1

        def own_of(p):
            return part(stage_own[kind(p)].at[slots[p]], p)

        def total(p):
            return acc[parts[p][6]]

        def begin(p):
            for second in (0, 1):
                for first in (0, 1):
                    send(p, group(p, second, first, 1 - c), core_in[p].at[pl.ds(second * 8 + first * 4, 4)], 0, 0,
                         device(o, z, x, 1 - c)).start()
            for first in (0, 1):
                pltpu.make_async_copy(group(p, 1, first, c), total(p).at[pl.ds(first * 4, 4)], own_sem.at[p]).start()

        def core_fetch(p):
            k = kind(p)
            if last_user[p] is not None:
                q = last_user[p]
                wait(own_of(q), send_sem.at[q, 1])
            for first in (0, 1):
                pltpu.make_async_copy(group(p, 0, first, c), own_of(p).at[pl.ds(first * 4, 4)], stage_sem.at[kind(p), 0]).start()
            wait(core_in[p], recv_sem.at[p, 0])
            pltpu.make_async_copy(core_in[p].at[pl.ds(0, 8)], part(stage_got[k], p), stage_sem.at[kind(p), 1]).start()
            pltpu.make_async_copy(core_in[p].at[pl.ds(8, 8)], part(stage_second[k], p), stage_sem.at[kind(p), 2]).start()

        def core_add(p):
            own, got = own_of(p), part(stage_got[kind(p)], p)
            wait(own, stage_sem.at[kind(p), 0])
            wait(got, stage_sem.at[kind(p), 1])
            for first in (0, 1):
                s = pl.ds(first * 4, 4)
                own[s] = own[s] + got[s]
                send(p, own.at[s], second_in[p].at[s], 1, 1 + first, far(p, True)).start()
            mine = part(stage_second[kind(p)], p)
            wait(total(p), own_sem.at[p])
            wait(mine, stage_sem.at[kind(p), 2])
            total(p)[...] = total(p)[...] + mine[...]

        def second_fetch(p):
            got = part(stage_second[kind(p)], p)
            for first in (0, 1):
                s = pl.ds(first * 4, 4)
                wait(second_in[p].at[s], recv_sem.at[p, 1 + first])
            pltpu.make_async_copy(second_in[p], got, stage_sem.at[kind(p), 2]).start()

        def second_add(p):
            got = part(stage_second[kind(p)], p)
            wait(got, stage_sem.at[kind(p), 2])
            t = total(p)
            t[0:4] = t[0:4] + got[0:4]
            send(p, t.at[pl.ds(0, 4)], first_in[p], 2, 3, far(p, False)).start()
            t[4:8] = t[4:8] + got[4:8]

        def send_z(p, k, step):
            to = z + step
            slot = jnp.where(k == to, jnp.where(step > 0, k, 4), k)
            send(p, total(p).at[4 + k], z_in[p].at[slot], 3, 4 + slot, device(o, to, x, c)).start()

        def first_fetch(p):
            wait(first_in[p], recv_sem.at[p, 3])
            pltpu.make_async_copy(first_in[p], part(stage_first[kind(p)], p), stage_sem.at[kind(p), 3]).start()

        def first_add(p):
            got = part(stage_first[kind(p)], p)
            wait(got, stage_sem.at[kind(p), 3])
            t = total(p)
            t[4:8] = t[4:8] + got[...]

            @pl.when(z == 0)
            def _():
                for k in (3, 2, 1):
                    send_z(p, k, 1)

            @pl.when(z == 3)
            def _():
                for k in (0, 1, 2):
                    send_z(p, k, -1)

        def pass_on(p, k, step):
            wait(z_in[p].at[k], recv_sem.at[p, 4 + k])
            total(p)[4 + k] = total(p)[4 + k] + z_in[p][k]
            send_z(p, k, step)

        def along(level):
            def go(p):
                @pl.when(z == level)
                def _():
                    for k in range(3, level, -1):
                        pass_on(p, k, 1)

                @pl.when(z == 3 - level)
                def _():
                    for k in range(0, 3 - level):
                        pass_on(p, k, -1)
            return go

        out_user = [None, None]

        def copy_out(p):
            g, r0, r, c0, w, _, _ = parts[p]
            return pltpu.make_async_copy(stage_out[kind(p)].at[pl.ds(0, r), pl.ds(0, w)],
                                         outs[g].at[pl.ds(r0, r), pl.ds(c0, w)], out_sem.at[kind(p)])

        def finish():
            for p in out_user:
                copy_out(p).wait()

        def last(p):
            g, r0, r, c0, w, _, _ = parts[p]
            out = stage_out[kind(p)].at[pl.ds(0, r), pl.ds(0, w)]
            if out_user[kind(p)] is not None:
                copy_out(out_user[kind(p)]).wait()
            out_user[kind(p)] = p
            out[...] = total(p)[4 + z].astype(jnp.float32)

            @pl.when(z > 0)
            def _():
                wait(z_in[p].at[z], recv_sem.at[p, 4 + z])
                out[...] += z_in[p][z].astype(jnp.float32)

            @pl.when(z < 3)
            def _():
                wait(z_in[p].at[4], recv_sem.at[p, 8])
                out[...] += z_in[p][4].astype(jnp.float32)

            copy_out(p).start()
            wait(core_in[p], send_sem.at[p, 0])
            if all(last_user[q] != p for q in range(n)):
                wait(own_of(p), send_sem.at[p, 1])
            wait(first_in[p], send_sem.at[p, 2])
            wait(first_in[p].at[pl.ds(0, 3)], send_sem.at[p, 3])

        self.finish = finish
        self.steps = (begin, core_fetch, core_add, second_fetch, second_add, first_fetch, first_add, along(1), along(2), last)

    @staticmethod
    def shapes(parts):
        return [shape(m, s[2], s[4]) for m in (16, 8, 4) for s in parts]

    @staticmethod
    def scratch(parts):
        b16 = jnp.bfloat16
        sizes = {s[6]: (8, s[2], s[4]) for s in parts}
        acc = [(sizes[k], b16) for k in sorted(sizes)]
        lands = [((m, s[2], s[4]), b16) for m in (5,) for s in parts]
        stages = [((m, 48, 768), b16) if k == 0 else ((m, 96, 384), b16) for m in (8, 8, 4) for k in (0, 1)]
        stages = [((2, 8, 48, 768), b16), ((2, 8, 96, 384), b16)] + stages
        stages += [((48, 768), jnp.float32), ((96, 384), jnp.float32)]
        n = len(parts)
        return buffers(*acc, *lands, *stages) + [pltpu.SemaphoreType.DMA(k) for k in ((n, 4), (n, 9), (n,), (2, 4), (2,))]

    @staticmethod
    def unpack(parts, refs):
        n, m = len(parts), len({s[6] for s in parts})
        acc, refs = refs[:m], refs[m:]
        z_in, refs = refs[:n], refs[n:]
        return (acc, z_in, refs[0:2], refs[2:4], refs[4:6], refs[6:8], refs[8:10]), refs[10:15]


D = 768
SCALE = 0.125 * 1.4426950408889634
ROWS = 256
VMEM_BYTES = 127 * 2**19


def mul(a, b, ca=1, cb=0):
    return lax.dot_general(a, b, (((ca,), (cb,)), ((), ())), preferred_element_type=jnp.float32)


def low(v):
    return v.astype(jnp.bfloat16)


def cols(j):
    return pl.ds(pl.multiple_of(j * D, D), D)


def rms_scale(v):
    return lax.rsqrt(jnp.mean(v * v, axis=-1, keepdims=True) + 1e-06)


def rms_back(v, gain, grad):
    r = rms_scale(v)
    unit = v * r
    scaled = grad * gain
    back = r * (scaled - unit * jnp.mean(scaled * unit, axis=-1, keepdims=True))
    return back, jnp.sum((grad * unit).reshape(-1, 8, v.shape[-1]), axis=0)


def gelu_and_slope(u):
    k = 0.7978845608028654
    square = u * u
    t = jnp.tanh(u * (k + k * 0.044715 * square))
    half = 0.5 + 0.5 * t
    return u * half, half + u * (0.5 - 0.5 * t * t) * (k + 3 * 0.044715 * k * square)


def halves(v):
    lane = lax.broadcasted_iota(jnp.int32, v.shape, 1)
    zero = jnp.zeros_like(v)
    return jnp.where(lane < 64, v, zero), jnp.where(lane < 64, zero, v)


def two(v):
    first = low(v)
    return first, low(v - first.astype(jnp.float32))


class Block:
    def __init__(self, rows, refs):
        self.rows = rows
        self.__dict__.update(refs)

    @staticmethod
    def scratch(rows):
        f32, b16 = jnp.float32, jnp.bfloat16
        return dict(
            branch=((rows, D), f32), projected=((rows, 3 * D), b16), merged=((rows, D), b16), lse=((6, 8, rows), f32),
            active=((rows, 4 * D), b16), slope=((rows, 4 * D), b16), normed=((rows, D), b16), normed_mlp=((rows, D), b16))

    def rows_of(self, t):
        return self.x[t].astype(jnp.float32)

    def tiles(self):
        return [slice(i, i + ROWS) for i in range(0, self.rows, ROWS)]

    def norm(self):
        for t in self.tiles():
            x = self.rows_of(t)
            self.normed[t] = low(x * rms_scale(x) * self.gain_attn[...])

    def project(self, j):
        c = cols(j)
        self.projected[:, c] = low(mul(self.normed[...], self.qkv[:, c]))

    def pair(self, ref, part, pair, rows=slice(None)):
        return ref[rows, pl.ds(pl.multiple_of(part * D + pair * 128, 128), 128)]

    def attend(self, pair):
        v0, v1 = halves(self.pair(self.projected, 2, pair))
        causal = lax.broadcasted_iota(jnp.int32, (ROWS, ROWS), 1) >= lax.broadcasted_iota(jnp.int32, (ROWS, ROWS), 0)
        for t in self.tiles():
            n = t.stop
            qs = halves(self.pair(self.projected, 0, pair, t))
            k = self.pair(self.projected, 1, pair, slice(0, n))
            total = None
            for h in range(2):
                s = mul(k, qs[h], 1, 1)
                last = jnp.where(causal, s[t.start:], -1e30)
                s = last if t.start == 0 else jnp.concatenate([s[: t.start], last], axis=0)
                m = jnp.max(s, axis=0, keepdims=True) * SCALE
                p = jnp.exp2(s * SCALE - m)
                l = jnp.sum(p, axis=0, keepdims=True)
                self.lse[pair, h : h + 1, t] = m + jnp.log2(l)
                o = mul(low(p * (1.0 / l)), (v0, v1)[h][:n], 0, 0)
                total = o if total is None else total + o
            self.merged[t, pl.ds(pl.multiple_of(pair * 128, 128), 128)] = low(total)

    def join(self):
        for t in self.tiles():
            branch = mul(self.merged[t], self.out[...])
            self.branch[t] = branch
            middle = self.rows_of(t) + branch
            self.normed_mlp[t] = low(middle * rms_scale(middle) * self.gain_mlp[...])

    def widen(self, j):
        c = cols(j)
        for t in self.tiles():
            active, slope = gelu_and_slope(mul(self.normed_mlp[t], self.up[:, c]))
            self.active[t, c] = low(active)
            self.slope[t, c] = low(slope)

    def narrow(self, t):
        return mul(self.active[t], self.down[...])

    def back_wide(self, j):
        c = cols(j)
        for t in self.tiles():
            grad = mul(self.grad_low[t], self.down[c, :], 1, 1)
            self.slope[t, c] = low(grad * self.slope[t, c].astype(jnp.float32))

    def grad_down(self, j):
        return low(mul(self.active[:, cols(j)], self.grad_low[...], 0, 0))

    def grad_up(self, j):
        return low(mul(self.normed_mlp[...], self.slope[:, cols(j)], 0, 0))

    def back_mlp(self, grad_of):
        total = jnp.zeros((8, D), jnp.float32)
        for t in self.tiles():
            grad = mul(self.slope[t], self.up[...], 1, 1)
            back, gain = rms_back(self.rows_of(t) + self.branch[t], self.gain_mlp[...], grad)
            total = total + gain
            self.branch[t] = back
            self.normed_mlp[t] = low(grad_of(t) + back)
        return jnp.sum(total, axis=0, keepdims=True)

    def grad_out(self):
        return low(mul(self.merged[...], self.normed_mlp[...], 0, 0))

    def back_merged(self):
        self.active[:, :D] = low(mul(self.normed_mlp[...], self.out[...], 1, 1))

    def attend_back(self, pair, turned):
        rows = self.rows
        q, do = self.pair(self.projected, 0, pair), self.pair(self.active, 0, pair)
        qs, dos = halves(q), halves(do)
        dd = do.astype(jnp.float32) * self.pair(self.merged, 0, pair).astype(jnp.float32)
        pick = lax.broadcasted_iota(jnp.int32, (8, 128), 0) == lax.broadcasted_iota(jnp.int32, (8, 128), 1) // 64
        delta = lax.dot_general(pick.astype(jnp.float32), dd, (((1,), (1,)), ((), ())), precision=lax.Precision.HIGHEST,
                                preferred_element_type=jnp.float32)
        causal = lax.broadcasted_iota(jnp.int32, (ROWS, ROWS), 1) >= lax.broadcasted_iota(jnp.int32, (ROWS, ROWS), 0)
        for t in self.tiles():
            a = t.start
            ks, vs = halves(self.pair(self.projected, 1, pair, t)), halves(self.pair(self.projected, 2, pair, t))
            dk = dv = dq = 0.0
            for h in range(2):
                s = mul(ks[h], q[a:], 1, 1)
                p = jnp.exp2(s * SCALE - self.lse[pair, h : h + 1, a:])
                first = jnp.where(causal, p[:, :ROWS], 0.0)
                p = first if t.stop == rows else jnp.concatenate([first, p[:, ROWS:]], axis=1)
                dp = mul(vs[h], do[a:], 1, 1)
                ds = low(p * (dp - delta[h : h + 1, a:]))
                dv = dv + mul(low(p), dos[h][a:])
                dk = dk + mul(ds, qs[h][a:])
                dq = dq + mul(ks[h], ds, 0, 0)
            lanes = pl.multiple_of(pair * 128, 128)
            self.projected[t, pl.ds(D + lanes, 128)] = low(0.125 * dk)
            self.projected[t, pl.ds(2 * D + lanes, 128)] = low(dv)
            if a == 0:
                turned[:, :rows] = dq
            else:
                turned[:, a:rows] += dq
        self.projected[:, pl.ds(lanes, 128)] = low(0.125 * turned[:, :rows].T)

    def grad_qkv(self, j):
        return low(mul(self.normed[...], self.projected[:, cols(j)], 0, 0))

    def back_norm(self, finish):
        total = jnp.zeros((8, D), jnp.float32)
        for t in self.tiles():
            grad = mul(self.projected[t], self.qkv[...], 1, 1)
            back, gain = rms_back(self.rows_of(t), self.gain_attn[...], grad)
            total = total + gain
            finish(t, back + self.branch[t])
        return jnp.sum(total, axis=0, keepdims=True)


SAVED = ("branch", "projected", "merged", "lse", "active", "slope", "normed", "normed_mlp")


def run(steps, hooks=None):
    at = 0
    waits = []
    for count, body in steps:
        if count == 0:
            waits.append(body)
            continue
        before = [list(hooks[at + k]) if hooks else [] for k in range(count)]
        at += count
        for f in before[0]:
            f()
        for f in waits:
            f(0)
        waits = []
        if count == 1:
            body(0)
            continue

        @pl.loop(0, count)
        def _(j):
            for k in range(1, count):
                if before[k]:
                    @pl.when(j == k)
                    def _():
                        for f in before[k]:
                            f()
            body(j)


class Loads:
    def __init__(self, pairs, sems):
        self.copies = {k: pltpu.make_async_copy(a, b, sems.at[j]) for j, (k, a, b) in enumerate(pairs)}
        for c in self.copies.values():
            c.start()

    def need(self, *names):
        for n in names:
            self.copies[n].wait()


class Ship:
    def __init__(self, stages, sems):
        self.stages, self.sems, self.single = stages, sems, len(stages) == 1

    def wait(self, slot):
        slot = min(slot, len(self.stages) - 1)
        pltpu.make_async_copy(self.stages[slot], self.stages[slot], self.sems.at[slot]).wait()

    def send(self, slot, value, target, busy):
        slot = min(slot, len(self.stages) - 1)
        if busy is True:
            self.wait(slot)
        elif busy is not False:
            pl.when(busy)(lambda: self.wait(slot))
        self.stages[slot][...] = value()
        pltpu.make_async_copy(self.stages[slot], target, self.sems.at[slot]).start()


def wide_steps(b, grad_of, ship, targets, vec):
    gout, gup, gdown = targets

    def wide(j):
        b.back_wide(j)
        ship.send(0, lambda: b.grad_down(j), gdown.at[cols(j), :], j > 0)
        ship.send(1, lambda: b.grad_up(j), gup.at[:, cols(j)], ship.single or j > 0)

    def mlp(_):
        ship.wait(0)
        if not ship.single:
            ship.wait(1)
        vec(b.back_mlp(grad_of))

    def out(_):
        ship.send(1, b.grad_out, gout, False)
        b.back_merged()

    return [(4, wide), (1, mlp), (1, out)]


def attend_steps(b, ship, gqkv, vec, finish, turned, busy):
    def qkv(j):
        ship.send(1, lambda: b.grad_qkv(j), gqkv.at[:, cols(j)], True if busy else j > 0)

    def norm(_):
        vec(b.back_norm(finish))
        ship.wait(1)

    return [(6, lambda j: b.attend_back(j, turned)), (3, qkv), (1, norm)]


KEPT_DENSE = ("x", "branch", "projected", "merged", "lse", "normed_mlp")


MIDDLE_IN = ("x", "branch", "merged", "normed_mlp")


def middle_kernel(cot_hbm, vec_ref, out_hbm, up_hbm, down_hbm, *rest):
    n = len(MIDDLE_IN)
    kept_hbm, rest = rest[:n], rest[n:]
    y_hbm, grad_hbm, gmerged_hbm, gvec_ref, gout_hbm, gup_hbm, gdown_hbm = rest[:7]
    cot, out, up, down, active, slope, y, stage_0, stage_1, load_sem, stage_sem, row_sem = rest[7:19]
    kept = dict(zip(MIDDLE_IN, rest[19:]))
    where = dict(zip(MIDDLE_IN, zip(kept_hbm, rest[19:])), cot=(cot_hbm, cot), out=(out_hbm, out), up=(up_hbm, up), down=(down_hbm, down))
    order = ("normed_mlp", "up", "down", "x", "branch", "cot", "out", "merged")
    loads = Loads([(k,) + where[k] for k in order], load_sem)
    b = Block(cot.shape[0], dict(kept, active=active, slope=slope, grad_low=cot, out=out, up=up, down=down,
                                 gain_mlp=vec_ref.at[4:5]))

    def narrow(_):
        loads.need("x", "branch", "down")
        for t in b.tiles():
            y[t] = low(b.x[t] + b.branch[t] + b.narrow(t))
        pltpu.make_async_copy(y, y_hbm, row_sem.at[0]).start()
        loads.need("cot")

    def vec(value):
        gvec_ref[...] = value

    def cot_of(t):
        return cot[t].astype(jnp.float32)

    def grad(_):
        for t in b.tiles():
            b.branch[t] += cot_of(t)
        pltpu.make_async_copy(b.branch, grad_hbm, row_sem.at[1]).start()
        loads.need("out", "merged")

    ship = Ship((stage_0, stage_1), stage_sem)
    wide, mlp, last = wide_steps(b, cot_of, ship, (gout_hbm, gup_hbm, gdown_hbm), vec)
    run([(0, lambda _: loads.need("normed_mlp", "up")), (4, b.widen), (1, narrow), wide, mlp, (0, grad), last])
    pltpu.make_async_copy(active.at[:, pl.ds(0, D)], gmerged_hbm, row_sem.at[2]).start()
    ship.wait(1)
    for src, dst, j in ((y, y_hbm, 0), (b.branch, grad_hbm, 1), (active.at[:, pl.ds(0, D)], gmerged_hbm, 2)):
        pltpu.make_async_copy(src, dst, row_sem.at[j]).wait()


def shape(*dims, dtype=jnp.bfloat16):
    return jax.ShapeDtypeStruct(dims, dtype)


def any_specs(n):
    return [pl.BlockSpec(memory_space=pl.ANY)] * n


def vmem_specs(n):
    return [pl.BlockSpec(memory_space=pltpu.VMEM)] * n


WEIGHTS = [((D, 3 * D), jnp.bfloat16), ((D, D), jnp.bfloat16), ((D, 4 * D), jnp.bfloat16), ((4 * D, D), jnp.bfloat16)]


def buffers(*pairs):
    return [pltpu.VMEM(dims, dtype) for dims, dtype in pairs]


def kept_buffers(rows):
    s = Block.scratch(rows)
    return [s[k] for k in SAVED]


def dense_middle(cot, vec, weights, kept):
    rows = cot.shape[0]
    f32, b16 = jnp.float32, jnp.bfloat16
    every = dict(Block.scratch(rows), x=((rows, D), f32))
    return pl.pallas_call(
        middle_kernel,
        in_specs=any_specs(1) + vmem_specs(1) + any_specs(3 + len(kept)),
        out_specs=any_specs(3) + vmem_specs(1) + any_specs(3),
        out_shape=[shape(rows, D), shape(rows, D, dtype=f32), shape(rows, D), shape(1, D, dtype=f32)]
        + [shape(*s) for s, _ in WEIGHTS[1:]],
        scratch_shapes=buffers(((rows, D), b16), *WEIGHTS[1:], every["active"], every["slope"], ((rows, D), b16),
                               ((D, D), b16), ((D, D), b16))
        + [pltpu.SemaphoreType.DMA((8,)), pltpu.SemaphoreType.DMA((2,)), pltpu.SemaphoreType.DMA((3,))]
        + buffers(*[every[k] for k in MIDDLE_IN]),
        compiler_params=pltpu.CompilerParams(vmem_limit_bytes=VMEM_BYTES),
        name="dense_middle",
    )(cot, vec, *weights, *kept)


def spots(start, count, spot):
    at = lax.broadcasted_iota(jnp.int32, (count, spot.shape[1]), 0) + start
    return low(jnp.where(at == spot, 1.0, 0.0))


def lane_map(outer, inner):
    each = D // (outer * inner)
    d = jnp.arange(D, dtype=jnp.int32)
    return jnp.stack([d // each % inner, d // (each * inner) * 128 + d % each])


def spread_map(tiles_columns, map_ref):
    at = lax.broadcasted_iota(jnp.int32, (tiles_columns, D), 0)
    return low(jnp.where(at == map_ref[1:2], 1.0, 0.0))


def read_vectors(tiles, map_ref):
    rows, columns = tiles.shape
    every = mul(tiles[...], spread_map(columns, map_ref))
    inner = lax.broadcasted_iota(jnp.int32, (rows, D), 0) // 16
    return jnp.sum(jnp.where(inner == map_ref[0:1], every, 0.0).reshape(rows // 16, 16, D), axis=0)


def write_vectors(vectors, rows, columns, map_ref):
    every = jnp.broadcast_to(vectors[None], (rows // 16, 16, D)).reshape(rows, D)
    inner = lax.broadcasted_iota(jnp.int32, (rows, D), 0) // 16
    return low(mul(low(jnp.where(inner == map_ref[0:1], every, 0.0)), spread_map(columns, map_ref), 1, 1))


def gate_of(x, router):
    return jax.nn.sigmoid(jnp.sum(x * router, axis=-1, keepdims=True))


def routed_forward_steps(b, need, hidden, spot_ref, chosen, vec_ref, extra, keep):
    length = hidden.shape[0]

    def pick(_):
        chosen[...] = spots(0, length, spot_ref[...])
        need("hidden")
        for t in b.tiles():
            b.x[t] = low(mul(chosen[:, t], hidden[...], 0, 0))
        need("vectors")
        b.norm()
        keep("x", "normed")

    def join(_):
        keep("projected", "merged", "lse")
        need("out")
        b.join()
        keep("branch", "normed_mlp")

    def narrow(_):
        keep("active", "slope")
        need("down")
        for t in b.tiles():
            extra[t] = b.branch[t] + b.narrow(t)
        keep("change")

    def put(_):
        rows = [gate_of(b.rows_of(t), vec_ref[2:3]) * extra[t] for t in b.tiles()]
        pieces = [two(r) for r in rows]
        for i in range(0, length, ROWS):
            t = slice(i, i + ROWS)
            total = hidden[t].astype(jnp.float32)
            for piece, s in zip(pieces, b.tiles()):
                for p in piece:
                    total = total + mul(chosen[t, s], p)
            b.middle[t] = total

    return [(1, pick), (0, lambda _: need("qkv")), (3, b.project), (6, b.attend), (1, join), (0, lambda _: need("up")), (4, b.widen),
            (1, narrow), (1, put)]


KEPT = ("x", "change") + SAVED


def kept_shapes(rows):
    return [((rows, D), jnp.bfloat16), ((rows, D), jnp.float32)] + kept_buffers(rows)


def routed_backward_steps(b, need, grad, spot_ref, vec_ref, change, grad_rows, gate, ship, targets, vec, turned,
                          grad_hbm, grad_sem):
    length = grad.shape[0]
    router = vec_ref.at[2:3]
    gqkv, *others = targets

    def take(_):
        pieces = two(grad[...])
        need("x", "change")
        for t in b.tiles():
            chosen = spots(0, length, spot_ref[:, t])
            rows = mul(chosen, pieces[0], 0, 0) + mul(chosen, pieces[1], 0, 0)
            g = gate_of(b.rows_of(t), router[...])
            b.grad_low[t], grad_rows[t] = two(g * rows)
            logits = jnp.sum(rows * change[t], axis=-1, keepdims=True) * g * (1.0 - g)
            gate[t] = jnp.broadcast_to(logits, (ROWS, 128))
        need("down", "active", "slope", "normed_mlp")

    def finish(t, g):
        change[t] = g + gate[t, 0:1] * router[...]

    def put(_):
        pieces = [two(change[t]) for t in b.tiles()]
        for i in range(0, length, ROWS):
            t = slice(i, i + ROWS)
            total = grad[t]
            for piece, s in zip(pieces, b.tiles()):
                chosen = spots(i, ROWS, spot_ref[:, s])
                for p in piece:
                    total = total + mul(chosen, p)
            grad[t] = total
            pltpu.make_async_copy(grad.at[t], grad_hbm.at[t], grad_sem).start()

    def route(_):
        total = jnp.zeros((8, D), jnp.float32)
        for t in b.tiles():
            total = total + jnp.sum((gate[t, 0:1] * b.rows_of(t)).reshape(-1, 8, D), axis=0)
        vec(2, jnp.sum(total, axis=0, keepdims=True))

    wide, mlp, out = wide_steps(b, lambda t: b.grad_low[t].astype(jnp.float32) + grad_rows[t].astype(jnp.float32), ship, others, lambda v: vec(1, v))
    attend, qkv, norm = attend_steps(b, ship, gqkv, lambda v: vec(0, v), finish, turned, True)

    def wants(*names):
        return (0, lambda _: need(*names))

    return [(1, take), wide, wants("up", "branch"), mlp, wants("out", "merged"), out, wants("projected", "lse"), attend,
            wants("normed"), qkv, wants("qkv"), norm, (1, route), (1, put)]


def forward_kernel(remote, *refs):
    hidden_hbm, spot_ref, map_ref, *refs = refs
    given, refs = refs[:9], refs[9:]
    if remote:
        whole, refs = refs[:9], refs[9:]
    else:
        whole = given
    vec_ref, *refs = refs
    n, m = len(KEPT), len(KEPT_DENSE)
    kept_hbm, refs = dict(zip(KEPT, refs[:n])), refs[n:]
    dense_hbm, refs = dict(zip(KEPT_DENSE, refs[:m])), refs[m:]
    hidden, chosen, tiles, *refs = refs
    weights, refs = refs[:6], refs[6:]
    kept, refs = dict(zip(KEPT, refs[:n])), refs[n:]
    dense, refs = dict(zip(KEPT_DENSE, refs[:m])), refs[m:]
    normed, load_sem, keep_sem, dense_sem = refs[:4]
    names = ("vectors", "qkv", "out", "up", "down", "qkv_b", "out_b")
    first = pltpu.make_async_copy(hidden_hbm, hidden, load_sem.at[7])
    first.start()
    loads = {k: pltpu.make_async_copy(whole[j], dst, load_sem.at[j])
             for j, (k, dst) in enumerate(zip(names, [tiles] + weights))}
    flow = Gather(GATHER_PARTS, given, whole, *refs[4:]) if remote else None
    if not remote:
        for c in loads.values():
            c.start()

    def need(*wanted):
        for k in wanted:
            if k == "hidden":
                first.wait()
                continue
            loads[k].wait()
            if k == "vectors":
                vec_ref[...] = read_vectors(tiles, map_ref)

    saves = {k: pltpu.make_async_copy(kept[k], kept_hbm[k], keep_sem.at[j]) for j, k in enumerate(KEPT)}
    dense_saves = {k: pltpu.make_async_copy(dense[k], dense_hbm[k], dense_sem.at[j]) for j, k in enumerate(KEPT_DENSE)}

    def keep(*wanted):
        for k in wanted:
            saves[k].start()

    def keep_dense(*wanted):
        for k in wanted:
            dense_saves[k].start()

    qkv, out, up, down, qkv_b, out_b = weights
    b = Block(spot_ref.shape[1], dict(kept, middle=dense["x"], qkv=qkv, out=out, up=up, down=down,
                                      gain_attn=vec_ref.at[0:1], gain_mlp=vec_ref.at[1:2]))
    d = Block(hidden.shape[0], dict(dense, qkv=qkv_b, out=out_b, normed=normed,
                                    gain_attn=vec_ref.at[3:4], gain_mlp=vec_ref.at[4:5]))

    def norm(_):
        keep_dense("x")
        d.norm()

    def join(_):
        keep_dense("projected", "merged", "lse")
        need("out_b")
        d.join()
        keep_dense("branch", "normed_mlp")

    routed = routed_forward_steps(b, need, hidden, spot_ref, chosen, vec_ref, kept["change"], keep)
    steps = routed + [(1, norm), (0, lambda _: need("qkv_b")), (3, d.project), (6, d.attend), (1, join)]
    if remote:
        last = {part[0]: p for p, part in enumerate(GATHER_PARTS)}

        def take(step, p):
            flow.steps[step](p)
            a = GATHER_PARTS[p][0]
            if step == 6 and p == last[a] and a < len(names):
                loads[names[a]].start()

        units = [[] for _ in range(sum(c for c, _ in steps) + 1)]
        for unit, step, p in GATHER_PLAN:
            units[unit].append(functools.partial(take, step, p))
        flow.begin()
        run(steps, units)
        for f in units[-1]:
            f()
        flow.finish()
    else:
        run(steps)
    for c in list(saves.values()) + list(dense_saves.values()):
        c.wait()


def forward(remote, hidden, spot, place_map, weights, outer, inner):
    length, rows = hidden.shape[0], spot.shape[1]
    f32, b16 = jnp.float32, jnp.bfloat16
    kept = kept_shapes(rows)
    every = dict(Block.scratch(length), x=((length, D), f32))
    dense = [every[k] for k in KEPT_DENSE]
    whole = [shape(w.shape[0] * inner, w.shape[1] * outer) for w in weights] if remote else []
    tiles = (16 * inner, 128 * outer)
    scratch = (buffers(((length, D), b16), ((length, rows), b16), (tiles, b16), *WEIGHTS, *WEIGHTS[:2], *kept, *dense, ((length, D), b16))
               + [pltpu.SemaphoreType.DMA((k,)) for k in (8, len(kept), len(dense))])
    if remote:
        scratch += Gather.semaphores(len(GATHER_PARTS))
    results = pl.pallas_call(
        functools.partial(forward_kernel, remote),
        in_specs=any_specs(1) + vmem_specs(2) + any_specs(9),
        out_specs=any_specs(len(whole)) + vmem_specs(1) + any_specs(len(kept) + len(dense)),
        out_shape=whole + [shape(16, D, dtype=f32)] + [shape(*s, dtype=t) for s, t in kept + dense],
        scratch_shapes=scratch,
        compiler_params=pltpu.CompilerParams(vmem_limit_bytes=VMEM_BYTES, **(dict(collective_id=0, has_side_effects=True) if remote else {})),
        name="forward",
    )(hidden, spot, place_map, *weights)
    if remote:
        weights, results = results[:9], results[9:]
    return weights, results[0], results[1 : 1 + len(kept)], results[1 + len(kept) :]


DENSE_IN = ("x", "projected", "merged", "lse", "grad_merged", "plus")


def backward_kernel(remote, *refs):
    spot_ref, map_ref, vec_ref, gmlp_ref, *refs = refs
    weights_hbm, refs = refs[:5], refs[5:]
    n, m = len(KEPT), len(DENSE_IN)
    dense_hbm, refs = dict(zip(DENSE_IN, refs[:m])), refs[m:]
    kept_hbm, refs = dict(zip(KEPT, refs[:n])), refs[n:]
    given, refs = refs[:3], refs[3:]
    input_hbm, *refs = refs
    if remote:
        outs, refs = refs[:9], refs[9:]
    else:
        gvec_ref, *refs = refs
    made, refs = refs[:5], refs[5:]
    if remote:
        k = len(PARTS)
        core_in, second_in, first_in, refs = refs[:k], refs[k : 2 * k], refs[2 * k : 3 * k], refs[3 * k :]
    (x, plus, projected, merged, grad_merged, lse, normed, qkv, turned, grad_rows, gate, out, up, down, x_a, active, slope,
     stage, load_sem, stage_sem, row_sem, *refs) = refs
    half = spot_ref.shape[1]
    top, rest = pl.ds(0, half), pl.ds(half, half)
    a_refs = dict(x=x_a, change=plus.at[rest], branch=plus.at[top], projected=projected.at[top], merged=merged.at[top],
                  lse=lse.at[:, :, top], active=active, slope=slope, normed=normed.at[top], normed_mlp=normed.at[rest])
    copies = dict(zip(("d_qkv", "qkv", "out", "up", "down"), zip(weights_hbm, (qkv, qkv, out, up, down))))
    copies.update({"d_" + k: (dense_hbm[k], r) for k, r in zip(DENSE_IN, (x, projected, merged, lse, grad_merged, plus))})
    copies.update({k: (kept_hbm[k], a_refs[k]) for k in KEPT})
    copies = {k: pltpu.make_async_copy(*v, load_sem.at[j]) for j, (k, v) in enumerate(copies.items())}
    late = ("change", "normed_mlp", "branch", "merged", "projected", "lse", "normed", "qkv")
    for k in ("d_projected", "d_merged", "d_grad_merged", "d_lse", "d_x", "d_qkv", "d_plus", "x", "down", "active", "slope", "up", "out"):
        copies[k].start()

    def need(*names):
        for k in names:
            copies[k].wait()

    d = Block(x.shape[0], dict(x=x, branch=plus, projected=projected, merged=merged, lse=lse, active=grad_merged, normed=normed,
                               qkv=qkv, gain_attn=vec_ref.at[3:4]))
    b = Block(half, dict(a_refs, grad_low=grad_merged.at[rest], qkv=qkv, out=out, up=up, down=down,
                         gain_attn=vec_ref.at[0:1], gain_mlp=vec_ref.at[1:2]))
    if remote:
        gvec_ref, tile, *refs = refs
    gvec_ref[...] = jnp.zeros_like(gvec_ref)
    gvec_ref[4:5] = gmlp_ref[...]

    def vec(j, value):
        gvec_ref[j : j + 1] = value

    ship = Ship((stage,), stage_sem)
    gqkv_b, gqkv_a, gout_a, gup_a, gdown_a = made

    def finish(t, g):
        x[t] = g

    attend, qkv_step, norm_step = attend_steps(d, ship, gqkv_b, lambda v: vec(3, v), finish, turned, False)

    def norm(_):
        norm_step[1](0)
        for k in late:
            copies[k].start()

    steps = [(0, lambda _: need("d_projected", "d_merged", "d_grad_merged", "d_lse")), attend,
             (0, lambda _: need("d_x")), (0, lambda _: d.norm()), qkv_step, (0, lambda _: need("d_qkv", "d_plus")), (1, norm)]
    steps += routed_backward_steps(b, need, x, spot_ref, vec_ref, a_refs["change"], grad_rows, gate, ship,
                                   (gqkv_a, gout_a, gup_a, gdown_a), vec, turned, input_hbm, row_sem.at[0])
    if not remote:
        run(steps)
    else:
        grads = (gqkv_b, *given, gqkv_a, gout_a, gup_a, gdown_a, tile)
        sums = Scatter(PARTS, grads, outs, core_in, second_in, first_in, *Scatter.unpack(PARTS, refs))

        hooks = [[] for _ in range(sum(c for c, _ in steps) + 1)]
        for unit, step, p in BACK_PLAN:
            hooks[unit].append(functools.partial(sums.steps[step], p))
        greet(*place())
        run(steps, hooks)
        tile[...] = write_vectors(gvec_ref[...], *tile.shape, map_ref)
        for g in hooks[-1]:
            g()
        sums.finish()
    pltpu.make_async_copy(x, input_hbm, row_sem.at[0]).wait()


def backward(remote, spot, place_map, vec, gmlp, weights, dense, kept, given, outer, inner):
    length, rows = dense[0].shape[0], spot.shape[1]
    f32, b16 = jnp.float32, jnp.bfloat16
    made = [shape(*WEIGHTS[j][0]) for j in (0, 0, 1, 2, 3)]
    results = [shape(length, D, dtype=f32)]
    specs = any_specs(1)
    if remote:
        shards = [shape(s[0] // inner, s[1] // outer, dtype=f32) for s, _ in WEIGHTS]
        results += shards + shards + [shape(16, 128, dtype=f32)]
        specs += any_specs(9)
        lands = Scatter.shapes(PARTS)
    else:
        results += [shape(16, D, dtype=f32)]
        specs += vmem_specs(1)
        lands = []
    every = dict(Block.scratch(length), x=((length, D), f32))
    short = Block.scratch(rows)
    scratch = buffers(*[every[k] for k in ("x", "x", "projected", "merged", "merged", "lse", "normed")], WEIGHTS[0],
                      ((128, length), f32), ((rows, D), b16), ((rows, 128), f32), *WEIGHTS[1:],
                      ((rows, D), b16), short["active"], short["slope"], ((D, D), b16))
    scratch += [pltpu.SemaphoreType.DMA((k,)) for k in (5 + len(DENSE_IN) + len(kept), 2, 1)]
    if remote:
        scratch += buffers(((16, D), f32), ((16 * inner, 128 * outer), b16)) + Scatter.scratch(PARTS)
    return pl.pallas_call(
        functools.partial(backward_kernel, remote),
        in_specs=vmem_specs(4) + any_specs(5 + len(dense) + len(kept) + len(given)),
        out_specs=specs + any_specs(len(made) + len(lands)),
        out_shape=results + made + lands,
        scratch_shapes=scratch,
        compiler_params=pltpu.CompilerParams(vmem_limit_bytes=VMEM_BYTES, **(dict(collective_id=1, has_side_effects=True) if remote else {})),
        name="backward",
    )(spot, place_map, vec, gmlp, *weights, *dense, *kept, *given)


def pack_vectors(vectors):
    rows = jnp.stack([jnp.pad(v, (0, 128 - v.shape[0])) for v in vectors])
    return jnp.pad(rows, ((0, 16 - rows.shape[0]), (0, 0)))


def spread_vectors(vectors, outer, inner):
    rows = vectors.reshape(vectors.shape[0], outer, inner, -1).transpose(2, 0, 1, 3).astype(jnp.bfloat16)
    tiles = jnp.pad(rows, ((0, 0), (0, 16 - rows.shape[1]), (0, 0), (0, 128 - rows.shape[3])))
    return tiles.reshape(inner * 16, outer * 128)


def deliver_kernel(n, *refs):
    tile, sums, outs, vectors = refs[0], refs[1 : n + 1], refs[n + 1 : 2 * n + 1], refs[2 * n + 1 :]
    for a, b in zip(sums, outs):
        b[...] = a[...]
    for j, v in enumerate(vectors):
        v[...] = tile[j : j + 1, : v.shape[1]]


def deliver(tile, sums, each, count):
    n = len(sums)
    return pl.pallas_call(
        functools.partial(deliver_kernel, n),
        in_specs=vmem_specs(1 + n),
        out_specs=vmem_specs(n + count),
        out_shape=[shape(*s.shape, dtype=s.dtype) for s in sums] + [shape(1, each, dtype=jnp.float32)] * count,
        name="deliver",
    )(tile, *sums)


def fits(shards, outer, inner):
    return outer == 2 and inner == 16 and all(s.shape[0] % 16 == 0 and s.shape[1] % 128 == 0 for s in shards)


def per_device(outer, inner, *args):
    hidden, cotangent, capacity_class, token_index = args[:4]
    (gain_attn_a, qkv_a, out_a, gain_mlp_a, up_a, down_a, router_shard,
     gain_attn_b, qkv_b, out_b, gain_mlp_b, up_b, down_b) = args[4:]
    hidden, cotangent = hidden[0], cotangent[0]
    length = hidden.shape[0]
    tile = pack_vectors((gain_attn_a, gain_mlp_a, router_shard, gain_attn_b, gain_mlp_b))
    shards = [tile, qkv_a, out_a, up_a, down_a, qkv_b, out_b, up_b, down_b]
    remote = fits(shards, outer, inner)
    if not remote:
        shards = [lax.all_gather(lax.all_gather(s, "inner", axis=0, tiled=True), "outer", axis=1, tiled=True) for s in shards]

    capacity = (length // 8) << capacity_class[0]
    slots = lax.broadcasted_iota(jnp.int32, token_index.shape, 1)
    spot = jnp.where(slots < capacity, token_index, -1)
    whole, vec, kept, kept_dense = forward(remote, hidden, spot, lane_map(outer, inner), shards, outer, inner)
    saved = dict(zip(KEPT_DENSE, kept_dense))
    output, plus, grad_merged, gmlp, *given = dense_middle(
        cotangent, vec, whole[6:], [saved[k] for k in MIDDLE_IN])
    dense = [saved[k] for k in DENSE_IN[:4]] + [grad_merged, plus]
    input_grad, *res = backward(remote, spot, lane_map(outer, inner), vec, gmlp, (whole[5], *whole[1:5]), dense, kept, given, outer, inner)
    if remote:
        done, gtile = res[:8], res[8]
    else:
        gvec, gqkv_b, *grads_a = res
        done = [
            lax.psum_scatter(
                lax.psum_scatter(s, "outer", scatter_dimension=1, tiled=True), "inner", scatter_dimension=0, tiled=True
            ).astype(jnp.float32)
            for s in [gqkv_b, *given, *grads_a, spread_vectors(gvec[:5], outer, inner)]
        ]
        done, gtile = done[:8], done[8]
    each = gain_attn_a.shape[0]
    res = deliver(gtile, done, each, 5)
    gb, ga, v = res[:4], res[4:8], [r[0] for r in res[8:]]
    return (output[None], input_grad[None], v[0], ga[0], ga[1], v[1], ga[2], ga[3], v[2], v[3], gb[0], gb[1], v[4], gb[2], gb[3])


def solution(mesh):
    outer, inner = mesh.shape["outer"], mesh.shape["inner"]
    both = ("outer", "inner")
    rows, vector, matrix = P(both, None, None), P(both), P("inner", "outer")
    block = (vector, matrix, matrix, vector, matrix, matrix)
    return jax.shard_map(
        functools.partial(per_device, outer, inner),
        mesh=mesh,
        in_specs=(rows, rows, vector, P(both, None)) + block + (vector,) + block,
        out_specs=(rows, rows) + block + (vector,) + block,
        check_vma=False,
    )
```

time: 453 us -> 368 us (0.81)
  Pallas kernels: 440 us -> 354 us
    pallas_call x3 -> x2, Pallas kernels: 277 us -> 212 us  [the longest x1 160 us: backward(): pl.pallas_call(functools.partial(backward_kernel, remote), in_specs=vmem_...]
    pallas_call x1, Pallas kernels: 160 us -> 139 us  [forward(): pl.pallas_call(functools.partial(forward_kernel, remote), in_specs=any_sp...]
where the time goes in v4:
time: 368 us; the launch traced here: 364 us
  Pallas kernels  354 us (96%)
  local copies, waits for them, and re-layouts  6.4 us (2%)
    pallas_call x1, Pallas kernels, backward(): pl.pallas_call(functools.partial(backward_kernel, remote), in_specs=vmem_...  160 us
    pallas_call x1, Pallas kernels, forward(): pl.pallas_call(functools.partial(forward_kernel, remote), in_specs=any_sp...  139 us
    pallas_call x1, Pallas kernels, dense_middle(): pl.pallas_call(middle_kernel, in_specs=any_specs(1) + vmem_specs(1) + any...  52.2 us

profile of v4, /device:TPU:0, one launch (start us, length us, event | category | flops | bytes accessed | tf_op | source)
XLA Modules:
  0.0 363.6 jit_solution(2244624781850100069)
XLA Ops:
  1.3 0.7 pad_bitcast_fusion.4
  2.0 0.7 pad_bitcast_fusion.2
  2.6 0.7 pad_bitcast_fusion
  3.3 1.3 compare_select_fusion.2.refs_1_.refs_0_
  4.6 0.6 pad.25.refs_3_
  5.2 0.6 pad_add_fusion.refs_2_.refs_1_
  5.8 139.2 %forward.1 = (bf16[256,256]{1,0:T(8,128)(2,1)}, bf16[768,2304]{1,0:T(8,128)(2,1)}, bf16[768,768]{1,0:T(8,128)(2,1)}, bf16[768,3072]{1,0:T(8,128)(2,1)}, bf16[307...) custom-call(bf16[1024,768]{1,0:T(8,128)(2,1)} %bitcast.22, ...), custom_call_target="tpu_custom_call" | custom-call | tf_op jit(solution)/shard_map/forward/pallas_call | solution.py:1020
  145.0 52.2 %dense_middle.1 = (bf16[1024,768]{1,0:T(8,128)(2,1)}, f32[1024,768]{1,0:T(8,128)}, bf16[1024,768]{1,0:T(8,128)(2,1)}, f32[1,768]{1,0:T(1,128)}, bf16[768,768]{1,...) custom-call(bf16[1024,768]{1,0:T(8,128)(2,1)} %bitcast.21, ...), custom_call_target="tpu_custom_call" | custom-call | tf_op jit(solution)/shard_map/dense_middle/pallas_call | solution.py:777
  197.2 159.8 %backward.1 = (f32[1024,768]{1,0:T(8,128)}, f32[48,1152]{1,0:T(8,128)}, f32[48,384]{1,0:T(8,128)}, f32[48,1536]{1,0:T(8,128)}, f32[192,384]{1,0:T(8,128)}, /*ind...) custom-call(s32[1,512]{1,0:T(1,128)} %compare_select_fusion.2.refs_1, ...), custom_call_target="tpu_custom_call" | custom-call | tf_op jit(solution)/shard_map/backward/pallas_call | solution.py:1141
  357.0 2.7 deliver.1
  359.7 3.8 %copy.34 = f32[1,1024,768]{2,1,0:T(8,128)} copy(f32[1,1024,768]{2,1,0:T(8,128)} %bitcast.20) | data formatting | bytes 6291456
  (2 shorter events, 0.1 us)
